TPU v7x, 32 devices: a whole 2x2x4 slice. The times are simulated.
32 devices in a mesh: gx: 4 (over z), gy: 8 (over y, x, core).
Axes of the slice: x: 2, y: 2, z: 4, core: 2. Of those that a mesh axis runs over, the one named last changes fastest.
Arguments:
- adjoint_guess: float32 [16, 128, 256], P('gx', 'gy'), may hold values from -80 to 80, as said below
- velocity: float32 [3, 16, 4096], P(None, 'gx', 'gy'), may hold values from -1 to 1
- leaf_rate: float32 [16, 4096], P('gx', 'gy'), may hold values from 0.2 to 5
- canopy: int32 [16, 4096], P('gx', 'gy'), may hold values from 0 to 1, as said below
- solid: int32 [16, 4096], P('gx', 'gy'), may hold values from 0 to 1, as said below
- receptors: int32 [8], replicated, may hold values from 0 to 2047
Outputs:
- adjoint_field: float32 [16, 128, 256], P('gx', 'gy')
- residual: float32 [16, 128, 256], P('gx', 'gy')
Inputs may be any that keep to these rules, and one draw needn't show every extreme that they name: `adjoint_guess`: finite values. 1 marks building cells; every horizontal column is solid from the ground up to its building's height. `canopy`: 1 marks tree-crown cells; none is solid.
All inputs are finite; a program needn't handle non-finite values.
Results may differ from a plain program's by a relative error of at most 0.0003.
Values sent between devices are 32-bit elements; how exact they have to be, the bound alone decides.
No kernel may reach another device: no remote copies, remote signals or barrier semaphores. Data moves between devices by JAX's collectives and lax.ppermute only.
A program may use at most 64 MiB of HBM per device.

v0:
```python
import jax
import jax.numpy as jnp
from jax import lax
from jax.sharding import PartitionSpec as P

NZ = 32
R = 8
CYCLES = 3


horiz_diff = 4.0
vert_diff = 2.0
decay_rate = 3.5
penalty = 40.0
leaf_gain = 4.0
source_gain = 32.0


def padded_2(shard, sides, width):
    for axis, dim in sides:
        size, length = (lax.axis_size(axis), shard.shape[dim])
        up = [(i, (i + 1) % size) for i in range(size - 1)]
        down = [(j, i) for i, j in up]
        last = lax.slice_in_dim(shard, length - width, length, axis=dim)
        initial = lax.slice_in_dim(shard, 0, width, axis=dim)
        before = lax.ppermute(last, axis, up)
        after = lax.ppermute(initial, axis, down)
        shard = jnp.concatenate([before, shard, after], axis=dim)
    return shard


def coefficient_fields(flows, reaction):
    east_flow = flows[0]
    north_flow = flows[1]
    rise_flow = flows[2]
    couplings = [
        horiz_diff + jax.nn.relu(east_flow),
        horiz_diff + jax.nn.relu(-east_flow),
        horiz_diff + jax.nn.relu(north_flow),
        horiz_diff + jax.nn.relu(-north_flow),
        vert_diff + jax.nn.relu(rise_flow),
        vert_diff + jax.nn.relu(-rise_flow),
    ]
    diagonal = (
        decay_rate
        + reaction
        + couplings[0]
        + couplings[1]
        + couplings[2]
        + couplings[3]
        + couplings[4]
        + couplings[5]
    )
    return [jnp.repeat(piece, R, axis=-1) for piece in [diagonal] + couplings]


def apply_operator(padded, coefficients):
    centre = padded[1:-1, 1:-1]
    zero_lane = jnp.zeros(centre.shape[:-1] + (R,), jnp.float32)
    upper_cells = jnp.concatenate([centre[..., R:], zero_lane], axis=-1)
    lower_cells = jnp.concatenate([zero_lane, centre[..., :-R]], axis=-1)
    diagonal, east_c, west_c, north_c, south_c, upper_c, lower_c = coefficients
    return (
        diagonal * centre
        - east_c * padded[2:, 1:-1]
        - west_c * padded[:-2, 1:-1]
        - north_c * padded[1:-1, 2:]
        - south_c * padded[1:-1, :-2]
        - upper_c * upper_cells
        - lower_c * lower_cells
    )


def per_receptor(first, second):
    return jnp.sum((first * second).reshape(-1, R), axis=0)


def spread_lanes(values):
    return jnp.tile(values, NZ)


def residual_of(image_in, source_in):
    return source_in - image_in


def image_only(image_in, source_in):
    return image_in


def body(adjoint_guess, velocity, leaf_rate, canopy, solid, receptors):
    rows_dev = adjoint_guess.shape[0]
    cols_dev = adjoint_guess.shape[1]
    total_cols = cols_dev * lax.axis_size("gy")
    row_start = lax.axis_index("gx") * rows_dev
    col_start = lax.axis_index("gy") * cols_dev
    flows = velocity.reshape(3, rows_dev, cols_dev, NZ)
    reaction = (
        penalty * solid.astype(jnp.float32) + leaf_gain * leaf_rate * canopy.astype(jnp.float32)
    ).reshape(rows_dev, cols_dev, NZ)
    coefficients = coefficient_fields(flows, reaction)
    rec_rows = receptors // total_cols
    rec_cols = receptors % total_cols

    def operate(values):
        padded = padded_2(values, (("gx", 0), ("gy", 1)), 1)
        return apply_operator(padded, coefficients)

    global_rows = row_start + jnp.arange(rows_dev, dtype=jnp.int32)
    global_cols = col_start + jnp.arange(cols_dev, dtype=jnp.int32)
    hit_rows = (global_rows[:, None] == rec_rows[None, :]).astype(jnp.float32)
    hit_cols = (global_cols[:, None] == rec_cols[None, :]).astype(jnp.float32)
    receptor_plane = source_gain * hit_rows[:, None, :] * hit_cols[None, :, :]
    ground_lane = jnp.zeros((rows_dev, cols_dev, R), jnp.float32)
    upper_lanes = jnp.zeros((rows_dev, cols_dev, (NZ - 2) * R), jnp.float32)
    source = jnp.concatenate([ground_lane, receptor_plane, upper_lanes], axis=-1)

    def operator_pair(values, make_middle):
        first_image = operate(values)
        middle = make_middle(first_image, source)
        second_image = operate(middle)
        return (first_image, middle, second_image)

    iterate = adjoint_guess
    ignored, residual, image_dir = operator_pair(iterate, residual_of)
    squares, against = lax.psum(
        (per_receptor(residual, residual), per_receptor(residual, image_dir)), ("gx", "gy")
    )
    alpha_step = squares / against
    for cycle_index in range(CYCLES):
        halfway = residual - spread_lanes(alpha_step) * image_dir
        if cycle_index + 1 < CYCLES:
            turned, copied, again = operator_pair(halfway, image_only)
            self_half, half_turn, self_turn, half_again, turn_again = lax.psum(
                (
                    per_receptor(halfway, halfway),
                    per_receptor(halfway, turned),
                    per_receptor(turned, turned),
                    per_receptor(halfway, again),
                    per_receptor(turned, again),
                ),
                ("gx", "gy"),
            )
            omega_step = half_turn / self_turn
            iterate = (
                iterate + spread_lanes(alpha_step) * residual + spread_lanes(omega_step) * halfway
            )
            residual = halfway - spread_lanes(omega_step) * turned
            image_dir = turned - spread_lanes(omega_step) * again
            squares = self_half - 2.0 * omega_step * half_turn + omega_step * omega_step * self_turn
            against = (
                half_turn
                - omega_step * half_again
                - omega_step * self_turn
                + omega_step * omega_step * turn_again
            )
            alpha_step = squares / against
        else:
            turned = operate(halfway)
            along_turn, turn_power = lax.psum(
                (per_receptor(turned, halfway), per_receptor(turned, turned)), ("gx", "gy")
            )
            omega_step = along_turn / turn_power
            iterate = (
                iterate + spread_lanes(alpha_step) * residual + spread_lanes(omega_step) * halfway
            )
            residual = halfway - spread_lanes(omega_step) * turned
    return (iterate, residual)


def solution(mesh):
    return jax.shard_map(
        body,
        mesh=mesh,
        in_specs=(
            P("gx", "gy", None),
            P(None, "gx", "gy"),
            P("gx", "gy"),
            P("gx", "gy"),
            P("gx", "gy"),
            P(),
        ),
        out_specs=(P("gx", "gy", None), P("gx", "gy", None)),
        check_vma=False,
    )
```

profile of v0, /device:TPU:0, one launch (start us, length us, event | category | flops | bytes accessed | tf_op | source)
XLA Modules:
  0.0 286.4 jit_solution(6530466100209439689)
XLA Ops:
  2.7 5.6 %collective-permute-start.1 = (f32[1,16,256]{2,1,0:T(8,128)S(1)}, f32[1,16,256]{2,1,0:T(8,128)S(1)}, u32[]{:S(2)}, u32[]{:S(2)}) collective-permute-start(f32[1,16,256]{2,1,0:T(8,128)S(1)} %get-tuple-element.89), channel_id=1, source_target_pairs={{0,8},{8,16},{16,24},{1,9},{9,17},{17,25},{2,10},{10,18},{18,26},{... | collective-permute-start | bytes 49160 | tf_op jit(solution)/shard_map/ppermute | solution.py:26
  14.4 3.0 %collective-permute-start.3 = (f32[6,1,256]{2,1,0:T(1,128)S(1)}, f32[6,1,256]{2,1,0:T(1,128)S(1)}, u32[]{:S(2)}, u32[]{:S(2)}) collective-permute-start(f32[6,1,256]{2,1,0:T(1,128)S(1)} %get-tuple-element.57), channel_id=1, source_target_pairs={{0,1},{1,2},{2,3},{3,4},{4,5},{5,6},{6,7},{8,9},{9,10},{10,11},{11... | collective-permute-start | bytes 18440 | tf_op jit(solution)/shard_map/ppermute | solution.py:26
  19.6 3.9 %collective-permute-start.5 = (f32[1,16,256]{2,1,0:T(8,128)S(1)}, f32[1,16,256]{2,1,0:T(8,128)S(1)}, u32[]{:S(2)}, u32[]{:S(2)}) collective-permute-start(f32[1,16,256]{2,1,0:T(8,128)S(1)} %get-tuple-element.84), channel_id=1, source_target_pairs={{0,8},{8,16},{16,24},{1,9},{9,17},{17,25},{2,10},{10,18},{18,26},{... | collective-permute-start | bytes 49160 | tf_op jit(solution)/shard_map/ppermute | solution.py:26
  25.0 4.2 %collective-permute-done.4 = f32[1,16,256]{2,1,0:T(8,128)S(1)} collective-permute-done((f32[1,16,256]{2,1,0:T(8,128)S(1)}, f32[1,16,256]{2,1,0:T(8,128)S(1)}, u32[]{:S(2)}, u32[]{:S(2)}) %collective-permute-start.4) | collective-permute-done | bytes 16416 | tf_op jit(solution)/shard_map/ppermute | solution.py:27
  30.5 3.0 %collective-permute-start.7 = (f32[6,1,256]{2,1,0:T(1,128)S(1)}, f32[6,1,256]{2,1,0:T(1,128)S(1)}, u32[]{:S(2)}, u32[]{:S(2)}) collective-permute-start(f32[6,1,256]{2,1,0:T(1,128)S(1)} %get-tuple-element.55), channel_id=1, source_target_pairs={{0,1},{1,2},{2,3},{3,4},{4,5},{5,6},{6,7},{8,9},{9,10},{10,11},{11... | collective-permute-start | bytes 18440 | tf_op jit(solution)/shard_map/ppermute | solution.py:26
  35.5 43.0 %all-reduce.17 = (f32[8]{0:T(128)S(1)}, f32[8]{0:T(128)S(1)}) all-reduce(f32[8]{0:T(128)S(1)} %reduce_sum.126, f32[8]{0:T(128)S(1)} %reduce_sum.127), channel_id=1, replica_groups=mesh['gx'=4,'gy'=8] {'gx','gy'}, use_global_device_ids=true, to_apply=%region_1.2 | all-reduce | flops 16 | bytes 128 | tf_op jit(solution)/shard_map/psum | solution.py:125
  78.6 2.3 collective-permute-start.9
  82.4 4.2 %collective-permute-done.8 = f32[1,16,256]{2,1,0:T(8,128)S(1)} collective-permute-done((f32[1,16,256]{2,1,0:T(8,128)S(1)}, f32[1,16,256]{2,1,0:T(8,128)S(1)}, u32[]{:S(2)}, u32[]{:S(2)}) %collective-permute-start.8) | collective-permute-done | bytes 16416 | tf_op jit(solution)/shard_map/ppermute | solution.py:27
  87.9 3.0 %collective-permute-start.11 = (f32[6,1,256]{2,1,0:T(1,128)S(1)}, f32[6,1,256]{2,1,0:T(1,128)S(1)}, u32[]{:S(2)}, u32[]{:S(2)}) collective-permute-start(f32[6,1,256]{2,1,0:T(1,128)S(1)} %get-tuple-element.53), channel_id=1, source_target_pairs={{0,1},{1,2},{2,3},{3,4},{4,5},{5,6},{6,7},{8,9},{9,10},{10,11},{11... | collective-permute-start | bytes 18440 | tf_op jit(solution)/shard_map/ppermute | solution.py:26
  91.8 2.7 collective-permute-start.13
  96.7 3.5 %collective-permute-done.12 = f32[1,16,256]{2,1,0:T(8,128)S(1)} collective-permute-done((f32[1,16,256]{2,1,0:T(8,128)S(1)}, f32[1,16,256]{2,1,0:T(8,128)S(1)}, u32[]{:S(2)}, u32[]{:S(2)}) %collective-permute-start.12) | collective-permute-done | bytes 16416 | tf_op jit(solution)/shard_map/ppermute | solution.py:27
  101.4 3.0 %collective-permute-start.15 = (f32[6,1,256]{2,1,0:T(1,128)S(1)}, f32[6,1,256]{2,1,0:T(1,128)S(1)}, u32[]{:S(2)}, u32[]{:S(2)}) collective-permute-start(f32[6,1,256]{2,1,0:T(1,128)S(1)} %get-tuple-element.51), channel_id=1, source_target_pairs={{0,1},{1,2},{2,3},{3,4},{4,5},{5,6},{6,7},{8,9},{9,10},{10,11},{11... | collective-permute-start | bytes 18440 | tf_op jit(solution)/shard_map/ppermute | solution.py:26
  108.2 44.8 %all-reduce.16 = (f32[8]{0:T(128)S(1)}, f32[8]{0:T(128)S(1)}, f32[8]{0:T(128)S(1)}, f32[8]{0:T(128)S(1)}, f32[8]{0:T(128)S(1)}) all-reduce(f32[8]{0:T(128)S(1)} %reduce_sum.132, f32[8]{0:T(128)S(1)} %reduce_sum.128, f32[8]{0:T(128)S(1)} %reduce_sum.129, f32[8]{0:T(128)S(1)} %reduce_sum.131, ...), channel_id=1, replica_groups=mesh['gx'=4,'gy'=8] {'gx','gy'}, use_global_device_ids=true, to_apply=%region_13.14 | all-reduce | flops 40 | bytes 320 | tf_op jit(solution)/shard_map/psum | solution.py:133
  153.3 2.4 collective-permute-start.17
  157.1 4.2 %collective-permute-done.16 = f32[1,16,256]{2,1,0:T(8,128)S(1)} collective-permute-done((f32[1,16,256]{2,1,0:T(8,128)S(1)}, f32[1,16,256]{2,1,0:T(8,128)S(1)}, u32[]{:S(2)}, u32[]{:S(2)}) %collective-permute-start.16) | collective-permute-done | bytes 16416 | tf_op jit(solution)/shard_map/ppermute | solution.py:27
  162.6 3.0 %collective-permute-start.19 = (f32[6,1,256]{2,1,0:T(1,128)S(1)}, f32[6,1,256]{2,1,0:T(1,128)S(1)}, u32[]{:S(2)}, u32[]{:S(2)}) collective-permute-start(f32[6,1,256]{2,1,0:T(1,128)S(1)} %get-tuple-element.49), channel_id=1, source_target_pairs={{0,1},{1,2},{2,3},{3,4},{4,5},{5,6},{6,7},{8,9},{9,10},{10,11},{11... | collective-permute-start | bytes 18440 | tf_op jit(solution)/shard_map/ppermute | solution.py:26
  166.6 2.6 collective-permute-start.21
  171.3 3.5 %collective-permute-done.20 = f32[1,16,256]{2,1,0:T(8,128)S(1)} collective-permute-done((f32[1,16,256]{2,1,0:T(8,128)S(1)}, f32[1,16,256]{2,1,0:T(8,128)S(1)}, u32[]{:S(2)}, u32[]{:S(2)}) %collective-permute-start.20) | collective-permute-done | bytes 16416 | tf_op jit(solution)/shard_map/ppermute | solution.py:27
  176.1 3.0 %collective-permute-start.23 = (f32[6,1,256]{2,1,0:T(1,128)S(1)}, f32[6,1,256]{2,1,0:T(1,128)S(1)}, u32[]{:S(2)}, u32[]{:S(2)}) collective-permute-start(f32[6,1,256]{2,1,0:T(1,128)S(1)} %get-tuple-element.47), channel_id=1, source_target_pairs={{0,1},{1,2},{2,3},{3,4},{4,5},{5,6},{6,7},{8,9},{9,10},{10,11},{11... | collective-permute-start | bytes 18440 | tf_op jit(solution)/shard_map/ppermute | solution.py:26
  182.9 45.0 %all-reduce.15 = (f32[8]{0:T(128)S(1)}, f32[8]{0:T(128)S(1)}, f32[8]{0:T(128)S(1)}, f32[8]{0:T(128)S(1)}, f32[8]{0:T(128)S(1)}) all-reduce(f32[8]{0:T(128)S(1)} %reduce_sum.137, f32[8]{0:T(128)S(1)} %reduce_sum.133, f32[8]{0:T(128)S(1)} %reduce_sum.134, f32[8]{0:T(128)S(1)} %reduce_sum.136, ...), channel_id=1, replica_groups=mesh['gx'=4,'gy'=8] {'gx','gy'}, use_global_device_ids=true, to_apply=%region_23.24 | all-reduce | flops 40 | bytes 320 | tf_op jit(solution)/shard_map/psum | solution.py:133
  228.2 2.3 collective-permute-start.25
  231.9 4.2 %collective-permute-done.24 = f32[1,16,256]{2,1,0:T(8,128)S(1)} collective-permute-done((f32[1,16,256]{2,1,0:T(8,128)S(1)}, f32[1,16,256]{2,1,0:T(8,128)S(1)}, u32[]{:S(2)}, u32[]{:S(2)}) %collective-permute-start.24) | collective-permute-done | bytes 16416 | tf_op jit(solution)/shard_map/ppermute | solution.py:27
  237.5 3.0 %collective-permute-start.27 = (f32[6,1,256]{2,1,0:T(1,128)S(1)}, f32[6,1,256]{2,1,0:T(1,128)S(1)}, u32[]{:S(2)}, u32[]{:S(2)}) collective-permute-start(f32[6,1,256]{2,1,0:T(1,128)S(1)} %get-tuple-element.45), channel_id=1, source_target_pairs={{0,1},{1,2},{2,3},{3,4},{4,5},{5,6},{6,7},{8,9},{9,10},{10,11},{11... | collective-permute-start | bytes 18440 | tf_op jit(solution)/shard_map/ppermute | solution.py:26
  243.2 42.5 %all-reduce.14 = (f32[8]{0:T(128)S(1)}, f32[8]{0:T(128)S(1)}) all-reduce(f32[8]{0:T(128)S(1)} %reduce_sum.138, f32[8]{0:T(128)S(1)} %reduce_sum.139), channel_id=1, replica_groups=mesh['gx'=4,'gy'=8] {'gx','gy'}, use_global_device_ids=true, to_apply=%region_25.26 | all-reduce | flops 16 | bytes 128 | tf_op jit(solution)/shard_map/psum | solution.py:159
  (175 shorter events, 43.0 us)
Async XLA Ops:
  1.4 11.6 %collective-permute-start = (f32[1,16,256]{2,1,0:T(8,128)S(1)}, f32[1,16,256]{2,1,0:T(8,128)S(1)}, u32[]{:S(2)}, u32[]{:S(2)}) collective-permute-start(f32[1,16,256]{2,1,0:T(8,128)S(1)} %get-tuple-element.88), channel_id=1, source_target_pairs={{8,0},{16,8},{24,16},{9,1},{17,9},{25,17},{10,2},{18,10},{26,18},{... | collective-permute-start | bytes 49160 | tf_op jit(solution)/shard_map/ppermute | solution.py:27
  2.7 10.3 %collective-permute-start.1 = (f32[1,16,256]{2,1,0:T(8,128)S(1)}, f32[1,16,256]{2,1,0:T(8,128)S(1)}, u32[]{:S(2)}, u32[]{:S(2)}) collective-permute-start(f32[1,16,256]{2,1,0:T(8,128)S(1)} %get-tuple-element.89), channel_id=1, source_target_pairs={{0,8},{8,16},{16,24},{1,9},{9,17},{17,25},{2,10},{10,18},{18,26},{... | collective-permute-start | bytes 49160 | tf_op jit(solution)/shard_map/ppermute | solution.py:26
  13.1 6.4 %collective-permute-start.2 = (f32[6,1,256]{2,1,0:T(1,128)S(1)}, f32[6,1,256]{2,1,0:T(1,128)S(1)}, u32[]{:S(2)}, u32[]{:S(2)}) collective-permute-start(f32[6,1,256]{2,1,0:T(1,128)S(1)} %get-tuple-element.56), channel_id=1, source_target_pairs={{1,0},{2,1},{3,2},{4,3},{5,4},{6,5},{7,6},{9,8},{10,9},{11,10},{12... | collective-permute-start | bytes 18440 | tf_op jit(solution)/shard_map/ppermute | solution.py:27
  14.4 5.1 %collective-permute-start.3 = (f32[6,1,256]{2,1,0:T(1,128)S(1)}, f32[6,1,256]{2,1,0:T(1,128)S(1)}, u32[]{:S(2)}, u32[]{:S(2)}) collective-permute-start(f32[6,1,256]{2,1,0:T(1,128)S(1)} %get-tuple-element.57), channel_id=1, source_target_pairs={{0,1},{1,2},{2,3},{3,4},{4,5},{5,6},{6,7},{8,9},{9,10},{10,11},{11... | collective-permute-start | bytes 18440 | tf_op jit(solution)/shard_map/ppermute | solution.py:26
  19.6 5.4 %collective-permute-start.5 = (f32[1,16,256]{2,1,0:T(8,128)S(1)}, f32[1,16,256]{2,1,0:T(8,128)S(1)}, u32[]{:S(2)}, u32[]{:S(2)}) collective-permute-start(f32[1,16,256]{2,1,0:T(8,128)S(1)} %get-tuple-element.84), channel_id=1, source_target_pairs={{0,8},{8,16},{16,24},{1,9},{9,17},{17,25},{2,10},{10,18},{18,26},{... | collective-permute-start | bytes 49160 | tf_op jit(solution)/shard_map/ppermute | solution.py:26
  23.5 5.7 %collective-permute-start.4 = (f32[1,16,256]{2,1,0:T(8,128)S(1)}, f32[1,16,256]{2,1,0:T(8,128)S(1)}, u32[]{:S(2)}, u32[]{:S(2)}) collective-permute-start(f32[1,16,256]{2,1,0:T(8,128)S(1)} %get-tuple-element.85), channel_id=1, source_target_pairs={{8,0},{16,8},{24,16},{9,1},{17,9},{25,17},{10,2},{18,10},{26,18},{... | collective-permute-start | bytes 49160 | tf_op jit(solution)/shard_map/ppermute | solution.py:27
  29.2 5.3 %collective-permute-start.6 = (f32[6,1,256]{2,1,0:T(1,128)S(1)}, f32[6,1,256]{2,1,0:T(1,128)S(1)}, u32[]{:S(2)}, u32[]{:S(2)}) collective-permute-start(f32[6,1,256]{2,1,0:T(1,128)S(1)} %get-tuple-element.54), channel_id=1, source_target_pairs={{1,0},{2,1},{3,2},{4,3},{5,4},{6,5},{7,6},{9,8},{10,9},{11,10},{12... | collective-permute-start | bytes 18440 | tf_op jit(solution)/shard_map/ppermute | solution.py:27
  30.5 4.0 %collective-permute-start.7 = (f32[6,1,256]{2,1,0:T(1,128)S(1)}, f32[6,1,256]{2,1,0:T(1,128)S(1)}, u32[]{:S(2)}, u32[]{:S(2)}) collective-permute-start(f32[6,1,256]{2,1,0:T(1,128)S(1)} %get-tuple-element.55), channel_id=1, source_target_pairs={{0,1},{1,2},{2,3},{3,4},{4,5},{5,6},{6,7},{8,9},{9,10},{10,11},{11... | collective-permute-start | bytes 18440 | tf_op jit(solution)/shard_map/ppermute | solution.py:26
  80.9 5.6 %collective-permute-start.8 = (f32[1,16,256]{2,1,0:T(8,128)S(1)}, f32[1,16,256]{2,1,0:T(8,128)S(1)}, u32[]{:S(2)}, u32[]{:S(2)}) collective-permute-start(f32[1,16,256]{2,1,0:T(8,128)S(1)} %get-tuple-element.81), channel_id=1, source_target_pairs={{8,0},{16,8},{24,16},{9,1},{17,9},{25,17},{10,2},{18,10},{26,18},{... | collective-permute-start | bytes 49160 | tf_op jit(solution)/shard_map/ppermute | solution.py:27
  86.6 4.4 %collective-permute-start.10 = (f32[6,1,256]{2,1,0:T(1,128)S(1)}, f32[6,1,256]{2,1,0:T(1,128)S(1)}, u32[]{:S(2)}, u32[]{:S(2)}) collective-permute-start(f32[6,1,256]{2,1,0:T(1,128)S(1)} %get-tuple-element.52), channel_id=1, source_target_pairs={{1,0},{2,1},{3,2},{4,3},{5,4},{6,5},{7,6},{9,8},{10,9},{11,10},{12... | collective-permute-start | bytes 18440 | tf_op jit(solution)/shard_map/ppermute | solution.py:27
  91.8 4.8 %collective-permute-start.13 = (f32[1,16,256]{2,1,0:T(8,128)S(1)}, f32[1,16,256]{2,1,0:T(8,128)S(1)}, u32[]{:S(2)}, u32[]{:S(2)}) collective-permute-start(f32[1,16,256]{2,1,0:T(8,128)S(1)} %get-tuple-element.76), channel_id=1, source_target_pairs={{0,8},{8,16},{16,24},{1,9},{9,17},{17,25},{2,10},{10,18},{18,26},{... | collective-permute-start | bytes 49160 | tf_op jit(solution)/shard_map/ppermute | solution.py:26
  94.5 5.6 %collective-permute-start.12 = (f32[1,16,256]{2,1,0:T(8,128)S(1)}, f32[1,16,256]{2,1,0:T(8,128)S(1)}, u32[]{:S(2)}, u32[]{:S(2)}) collective-permute-start(f32[1,16,256]{2,1,0:T(8,128)S(1)} %get-tuple-element.77), channel_id=1, source_target_pairs={{8,0},{16,8},{24,16},{9,1},{17,9},{25,17},{10,2},{18,10},{26,18},{... | collective-permute-start | bytes 49160 | tf_op jit(solution)/shard_map/ppermute | solution.py:27
  100.1 5.3 %collective-permute-start.14 = (f32[6,1,256]{2,1,0:T(1,128)S(1)}, f32[6,1,256]{2,1,0:T(1,128)S(1)}, u32[]{:S(2)}, u32[]{:S(2)}) collective-permute-start(f32[6,1,256]{2,1,0:T(1,128)S(1)} %get-tuple-element.50), channel_id=1, source_target_pairs={{1,0},{2,1},{3,2},{4,3},{5,4},{6,5},{7,6},{9,8},{10,9},{11,10},{12... | collective-permute-start | bytes 18440 | tf_op jit(solution)/shard_map/ppermute | solution.py:27
  101.4 4.0 %collective-permute-start.15 = (f32[6,1,256]{2,1,0:T(1,128)S(1)}, f32[6,1,256]{2,1,0:T(1,128)S(1)}, u32[]{:S(2)}, u32[]{:S(2)}) collective-permute-start(f32[6,1,256]{2,1,0:T(1,128)S(1)} %get-tuple-element.51), channel_id=1, source_target_pairs={{0,1},{1,2},{2,3},{3,4},{4,5},{5,6},{6,7},{8,9},{9,10},{10,11},{11... | collective-permute-start | bytes 18440 | tf_op jit(solution)/shard_map/ppermute | solution.py:26
  155.7 5.6 %collective-permute-start.16 = (f32[1,16,256]{2,1,0:T(8,128)S(1)}, f32[1,16,256]{2,1,0:T(8,128)S(1)}, u32[]{:S(2)}, u32[]{:S(2)}) collective-permute-start(f32[1,16,256]{2,1,0:T(8,128)S(1)} %get-tuple-element.71), channel_id=1, source_target_pairs={{8,0},{16,8},{24,16},{9,1},{17,9},{25,17},{10,2},{18,10},{26,18},{... | collective-permute-start | bytes 49160 | tf_op jit(solution)/shard_map/ppermute | solution.py:27
  161.3 4.4 %collective-permute-start.18 = (f32[6,1,256]{2,1,0:T(1,128)S(1)}, f32[6,1,256]{2,1,0:T(1,128)S(1)}, u32[]{:S(2)}, u32[]{:S(2)}) collective-permute-start(f32[6,1,256]{2,1,0:T(1,128)S(1)} %get-tuple-element.48), channel_id=1, source_target_pairs={{1,0},{2,1},{3,2},{4,3},{5,4},{6,5},{7,6},{9,8},{10,9},{11,10},{12... | collective-permute-start | bytes 18440 | tf_op jit(solution)/shard_map/ppermute | solution.py:27
  162.6 3.8 %collective-permute-start.19 = (f32[6,1,256]{2,1,0:T(1,128)S(1)}, f32[6,1,256]{2,1,0:T(1,128)S(1)}, u32[]{:S(2)}, u32[]{:S(2)}) collective-permute-start(f32[6,1,256]{2,1,0:T(1,128)S(1)} %get-tuple-element.49), channel_id=1, source_target_pairs={{0,1},{1,2},{2,3},{3,4},{4,5},{5,6},{6,7},{8,9},{9,10},{10,11},{11... | collective-permute-start | bytes 18440 | tf_op jit(solution)/shard_map/ppermute | solution.py:26
  166.6 4.7 %collective-permute-start.21 = (f32[1,16,256]{2,1,0:T(8,128)S(1)}, f32[1,16,256]{2,1,0:T(8,128)S(1)}, u32[]{:S(2)}, u32[]{:S(2)}) collective-permute-start(f32[1,16,256]{2,1,0:T(8,128)S(1)} %get-tuple-element.66), channel_id=1, source_target_pairs={{0,8},{8,16},{16,24},{1,9},{9,17},{17,25},{2,10},{10,18},{18,26},{... | collective-permute-start | bytes 49160 | tf_op jit(solution)/shard_map/ppermute | solution.py:26
  169.2 5.6 %collective-permute-start.20 = (f32[1,16,256]{2,1,0:T(8,128)S(1)}, f32[1,16,256]{2,1,0:T(8,128)S(1)}, u32[]{:S(2)}, u32[]{:S(2)}) collective-permute-start(f32[1,16,256]{2,1,0:T(8,128)S(1)} %get-tuple-element.67), channel_id=1, source_target_pairs={{8,0},{16,8},{24,16},{9,1},{17,9},{25,17},{10,2},{18,10},{26,18},{... | collective-permute-start | bytes 49160 | tf_op jit(solution)/shard_map/ppermute | solution.py:27
  174.8 5.3 %collective-permute-start.22 = (f32[6,1,256]{2,1,0:T(1,128)S(1)}, f32[6,1,256]{2,1,0:T(1,128)S(1)}, u32[]{:S(2)}, u32[]{:S(2)}) collective-permute-start(f32[6,1,256]{2,1,0:T(1,128)S(1)} %get-tuple-element.46), channel_id=1, source_target_pairs={{1,0},{2,1},{3,2},{4,3},{5,4},{6,5},{7,6},{9,8},{10,9},{11,10},{12... | collective-permute-start | bytes 18440 | tf_op jit(solution)/shard_map/ppermute | solution.py:27
  176.1 4.0 %collective-permute-start.23 = (f32[6,1,256]{2,1,0:T(1,128)S(1)}, f32[6,1,256]{2,1,0:T(1,128)S(1)}, u32[]{:S(2)}, u32[]{:S(2)}) collective-permute-start(f32[6,1,256]{2,1,0:T(1,128)S(1)} %get-tuple-element.47), channel_id=1, source_target_pairs={{0,1},{1,2},{2,3},{3,4},{4,5},{5,6},{6,7},{8,9},{9,10},{10,11},{11... | collective-permute-start | bytes 18440 | tf_op jit(solution)/shard_map/ppermute | solution.py:26
  230.5 5.6 %collective-permute-start.24 = (f32[1,16,256]{2,1,0:T(8,128)S(1)}, f32[1,16,256]{2,1,0:T(8,128)S(1)}, u32[]{:S(2)}, u32[]{:S(2)}) collective-permute-start(f32[1,16,256]{2,1,0:T(8,128)S(1)} %get-tuple-element.61), channel_id=1, source_target_pairs={{8,0},{16,8},{24,16},{9,1},{17,9},{25,17},{10,2},{18,10},{26,18},{... | collective-permute-start | bytes 49160 | tf_op jit(solution)/shard_map/ppermute | solution.py:27
  236.2 4.4 %collective-permute-start.26 = (f32[6,1,256]{2,1,0:T(1,128)S(1)}, f32[6,1,256]{2,1,0:T(1,128)S(1)}, u32[]{:S(2)}, u32[]{:S(2)}) collective-permute-start(f32[6,1,256]{2,1,0:T(1,128)S(1)} %get-tuple-element.44), channel_id=1, source_target_pairs={{1,0},{2,1},{3,2},{4,3},{5,4},{6,5},{7,6},{9,8},{10,9},{11,10},{12... | collective-permute-start | bytes 18440 | tf_op jit(solution)/shard_map/ppermute | solution.py:27
  237.5 3.8 %collective-permute-start.27 = (f32[6,1,256]{2,1,0:T(1,128)S(1)}, f32[6,1,256]{2,1,0:T(1,128)S(1)}, u32[]{:S(2)}, u32[]{:S(2)}) collective-permute-start(f32[6,1,256]{2,1,0:T(1,128)S(1)} %get-tuple-element.45), channel_id=1, source_target_pairs={{0,1},{1,2},{2,3},{3,4},{4,5},{5,6},{6,7},{8,9},{9,10},{10,11},{11... | collective-permute-start | bytes 18440 | tf_op jit(solution)/shard_map/ppermute | solution.py:26
  (12 other events, 28.6 us)
where the time goes:
time: 288 us; the launch traced here: 286 us
  blocking collectives  175 us (61%)
  starting transfers between devices  61 us (21%)
  waiting for transfers between devices  26.5 us (9%)
  local copies, waits for them, and re-layouts  16.4 us (6%)
  other arithmetic  5.81 us (2%)
    psum x2, blocking collectives, body(): lax.psum((per_receptor(halfway, halfway), per_receptor(halfway, turned),...  89.9 us
    psum x1, blocking collectives, body(): lax.psum((per_receptor(residual, residual), per_receptor(residual, image_...  43 us
    ppermute x14, starting transfers between devices, padded_2(): before = lax.ppermute(last, axis, up)  42.9 us
    psum x1, blocking collectives, body(): lax.psum((per_receptor(turned, halfway), per_receptor(turned, turned)), (...  42.5 us
    ppermute x14, waiting for transfers between devices, padded_2(): after = lax.ppermute(initial, axis, down)  23.8 us
    ppermute x14, starting transfers between devices, padded_2(): after = lax.ppermute(initial, axis, down)  18.1 us
    reshape x14, local copies, waits for them, and re-layouts, per_receptor(): return jnp.sum((first * second).reshape(-1, R), axis=0)  8.14 us
  transfers between devices with their start and end apart: 28, of which 13 were waited for; matrix products, arithmetic and copies ran while one was open for 3% of the time, Pallas kernels for 0%

commit v1 on v0

v1 whole, which is shorter than its diff:
```python
import functools
import math

import jax
import jax.numpy as jnp
from jax import lax
from jax.experimental import pallas as pl
from jax.experimental.pallas import tpu as pltpu
from jax.sharding import PartitionSpec as P

NZ = 32
R = 8
CYCLES = 3
DEPTH = 2 * CYCLES + 1
VECS = DEPTH
HALO = 8
SCALE = 16.0
SHIFT = 2.0
LANES = 128

horiz_diff = 4.0
vert_diff = 2.0
decay_rate = 3.5
penalty = 40.0
leaf_gain = 4.0
source_gain = 32.0


def two_sum(a, b):
    s = a + b
    t = s - a
    return s, (a - (s - t)) + (b - t)


def quick_sum(a, b):
    s = a + b
    return s, b - (s - a)


def split(a):
    c = a * 4097.0
    hi = c - (c - a)
    return hi, a - hi


def two_prod(a, b):
    p = a * b
    ah, al = split(a)
    bh, bl = split(b)
    return p, (((ah * bh - p) + ah * bl) + al * bh) + al * bl


def krylov_kernel(
    rows, cols, rec_ref, left_ref, own_ref, right_ref, ex_ref, gram_ref, vec_ref,
    f_ref, coef_ref, raw_ref, wide_ref, hi_ref, lo_ref,
):
    win = rows + 2 * DEPTH
    crows = win - 2
    width = cols + 2 * HALO
    tiles = width // 8
    total_rows = left_ref.shape[0]
    total_cols = cols * lax.axis_size("gy")
    row0 = lax.axis_index("gx") * rows - DEPTH
    col0 = lax.axis_index("gy") * cols - HALO
    lane = lax.broadcasted_iota(jnp.int32, (8, LANES), 1)
    sub = lax.broadcasted_iota(jnp.int32, (8, LANES), 0)

    def inside_row(i):
        at = row0 + i
        ok = jnp.logical_and(at >= 0, at < total_rows)
        return jnp.where(ok, 1.0, 0.0), jnp.clip(at, 0, total_rows - 1)

    def parts(at, lo):
        return (
            left_ref[at, :, lo : lo + LANES],
            own_ref[at, :, lo : lo + LANES],
            right_ref[at, :, lo : lo + LANES],
        )

    spans = ((0, HALO), (HALO, HALO + cols), (HALO + cols, width))

    @pl.loop(0, win)
    def _(i):
        ok, at = inside_row(i)
        for h in range(2):
            for (c0, c1), piece in zip(spans, parts(at, h * LANES)):
                f_ref[0, h, i, 8 + c0 : 8 + c1] = piece * ok

    @pl.loop(0, crows)
    def _(i):
        _, at = inside_row(i + 1)
        base = pl.multiple_of(i * width, 8)
        for (c0, c1), piece in zip(spans, parts(at, 2 * LANES)):
            raw_ref[pl.ds(base + c0, c1 - c0), :] = piece

    raw = raw_ref[...]
    first = raw.astype(jnp.bfloat16)
    rest = raw - first.astype(jnp.float32)
    second = rest.astype(jnp.bfloat16)
    third = (rest - second.astype(jnp.float32)).astype(jnp.bfloat16)
    wide_ref[...] = jnp.dot(
        jnp.concatenate([first, second, third], axis=1),
        ex_ref[...],
        preferred_element_type=jnp.float32,
    )

    @pl.loop(0, crows)
    def _(i):
        ok, _ = inside_row(i + 1)
        base = pl.multiple_of(i * width, 8)
        for t in range(tiles):
            at_col = col0 + 8 * t + sub
            seen = jnp.logical_and(at_col >= 0, at_col < total_cols)
            keep = jnp.where(seen, ok * (1.0 / SCALE), 0.0)
            for h in range(2):
                u, v, w, reaction = [
                    wide_ref[pl.ds(base + 8 * t, 8), pl.ds((2 * c + h) * LANES, LANES)]
                    for c in range(4)
                ]
                side = [
                    horiz_diff + jnp.maximum(u, 0.0),
                    horiz_diff + jnp.maximum(-u, 0.0),
                    horiz_diff + jnp.maximum(v, 0.0),
                    horiz_diff + jnp.maximum(-v, 0.0),
                    vert_diff + jnp.maximum(w, 0.0),
                    vert_diff + jnp.maximum(-w, 0.0),
                ]
                diag = decay_rate + reaction
                for one in side:
                    diag = diag + one
                if h == 1:
                    side[4] = jnp.where(lane < LANES - R, side[4], 0.0)
                else:
                    side[5] = jnp.where(lane >= R, side[5], 0.0)
                for c, one in enumerate([diag] + side):
                    coef_ref[c, h, i, 8 * t : 8 * t + 8] = one * keep

    def apply(step, finish):
        src, dst = step - 1, step
        shown = range(tiles) if step < DEPTH else range(HALO // 8, tiles - HALO // 8)

        @pl.loop(step, win - step)
        def _(i):
            for t in shown:
                c0 = 8 + 8 * t
                mid = [f_ref[src, h, i, c0 : c0 + 8] for h in range(2)]
                up = [pltpu.roll(m, LANES - R, 1) for m in mid]
                down = [pltpu.roll(m, R, 1) for m in mid]
                above = [jnp.where(lane < LANES - R, up[0], up[1]), up[1]]
                below = [down[0], jnp.where(lane >= R, down[1], down[0])]
                for h in range(2):
                    near = [
                        mid[h],
                        f_ref[src, h, i + 1, c0 : c0 + 8],
                        f_ref[src, h, i - 1, c0 : c0 + 8],
                        f_ref[src, h, i, c0 + 1 : c0 + 9],
                        f_ref[src, h, i, c0 - 1 : c0 + 7],
                        above[h],
                        below[h],
                    ]
                    terms = [
                        coef_ref[c, h, i - 1, 8 * t : 8 * t + 8] * near[c] for c in range(7)
                    ]
                    image = (terms[0] - terms[1]) - (terms[2] + terms[3])
                    image = image - ((terms[4] + terms[5]) + terms[6])
                    f_ref[dst, h, i, c0 : c0 + 8] = finish(image, mid[h])

    apply(1, lambda image, mid: -SCALE * image)
    for q in range(R):
        cell = rec_ref[q]
        i = cell // total_cols - row0
        c = cell % total_cols - col0
        seen = (i >= 1) & (i < win - 1) & (c >= 0) & (c < width)
        i = jnp.clip(i, 1, win - 2)
        c = jnp.clip(c, 0, width - 1)
        base = pl.multiple_of(8 + (c // 8) * 8, 8)
        gain = jnp.where(seen, source_gain, 0.0)
        spot = jnp.where((sub == c % 8) & (lane == R + q), gain, 0.0)
        f_ref[1, 0, i, pl.ds(base, 8)] += spot
    for step in range(2, DEPTH + 1):
        apply(step, lambda image, mid: image - SHIFT * mid)

    pieces = [
        (h, i, t) for h in range(2) for i in range(rows) for t in range(cols // 8)
    ]
    count = len(pieces)
    for k in range(VECS):
        for m, (h, i, t) in enumerate(pieces):
            c0 = 8 + HALO + 8 * t
            x = f_ref[k + 1, h, DEPTH + i, c0 : c0 + 8]
            vec_ref[k, h, i, 8 * t : 8 * t + 8] = x
            hi_ref[k, m], lo_ref[k, m] = split(x)

    zero = jnp.zeros((8, LANES), jnp.float32)
    sums = {}
    for group in ([0, 1, 2, 3], [4, 5], [6]):
        pairs = [(i, j) for j in group for i in range(j + 1)]

        def add(m, carry, pairs=pairs):
            need = sorted({i for pair in pairs for i in pair})
            hi = {k: hi_ref[k, m] for k in need}
            lo = {k: lo_ref[k, m] for k in need}
            out = []
            for (i, j), (s, e) in zip(pairs, carry):
                s, miss = two_sum(s, hi[i] * hi[j])
                if i == j:
                    cross = 2.0 * (hi[i] * lo[j])
                else:
                    cross = hi[i] * lo[j] + lo[i] * hi[j]
                out.append((s, e + ((cross + lo[i] * lo[j]) + miss)))
            return tuple(out)

        done = lax.fori_loop(0, count, add, tuple((zero, zero) for _ in pairs))
        for pair, value in zip(pairs, done):
            sums[pair] = value

    def merge(a, b, axis, step):
        where = (sub if axis == 0 else lane) & step
        first = where == 0
        size = 8 if axis == 0 else LANES
        out = []
        for x, y in zip(a, b):
            kept = jnp.where(first, x, y)
            moved = jnp.where(first, y, x)
            if 2 * step == size:
                moved = pltpu.roll(moved, step, axis)
            else:
                moved = jnp.where(
                    first, pltpu.roll(moved, size - step, axis), pltpu.roll(moved, step, axis)
                )
            out.append((kept, moved))
        (s0, s1), (e0, e1) = out
        s, miss = two_sum(s0, s1)
        return s, (e0 + e1) + miss

    def tree(items, axis, steps):
        for step in steps:
            half = len(items) // 2
            items = [merge(items[n], items[n + half], axis, step) for n in range(half)]
        return items[0]

    columns = []
    for j in range(8):
        i_list = [sums.get((min(i, j), max(i, j)), (zero, zero)) for i in range(8)]
        columns.append(tree(i_list, 0, (4, 2, 1)) if j < VECS else (zero, zero))
    s, e = tree(columns, 1, (64, 32, 16))
    low = (lane & R) == 0
    s1 = jnp.where(low, pltpu.roll(s, LANES - R, 1), pltpu.roll(s, R, 1))
    e1 = jnp.where(low, pltpu.roll(e, LANES - R, 1), pltpu.roll(e, R, 1))
    s, miss = two_sum(s, s1)
    e = (e + e1) + miss
    s, e = quick_sum(s, e)
    chunk = jnp.where(low, s, e)
    for n in range(gram_ref.shape[0] // 8):
        gram_ref[8 * n : 8 * n + 8] = chunk


def finish_kernel(gram_ref, guess_ref, vec_ref, x_ref, r_ref):
    lane = lax.broadcasted_iota(jnp.int32, (8, LANES), 1)
    sub = lax.broadcasted_iota(jnp.int32, (8, LANES), 0)
    devices = gram_ref.shape[0] // 8
    ways = math.gcd(devices, 8)
    zero = jnp.zeros((8, LANES), jnp.float32)

    def gather(n, carry):
        out = []
        for w, (s, e) in enumerate(carry):
            at = pl.multiple_of((n * ways + w) * 8, 8)
            s, miss = two_sum(s, gram_ref[pl.ds(at, 8), :])
            out.append((s, e + miss))
        return tuple(out)

    items = list(lax.fori_loop(0, devices // ways, gather, ((zero, zero),) * ways))
    while len(items) > 1:
        half = len(items) // 2
        merged = []
        for n in range(half):
            s, miss = two_sum(items[n][0], items[n + half][0])
            merged.append((s, (items[n][1] + items[n + half][1]) + miss))
        items = merged
    s, e = items[0]
    low = (lane & R) == 0
    g_hi = jnp.where(low, s, pltpu.roll(s, R, 1))
    g_lo = jnp.where(low, pltpu.roll(s, LANES - R, 1) + e, s + pltpu.roll(e, R, 1))
    g_hi, g_lo = quick_sum(g_hi, g_lo)

    def reduced(p, e, axis, steps):
        for step in steps:
            p, miss = two_sum(p, pltpu.roll(p, step, axis))
            e = (e + pltpu.roll(e, step, axis)) + miss
        return quick_sum(p, e)

    def product(a, b):
        p, e = two_prod(a[0], b[0])
        return p, e + (a[0] * b[1] + a[1] * b[0])

    def image_of(p, axis):
        step = 1 if axis == 0 else 2 * R
        s, miss = two_sum(SHIFT * p[0], pltpu.roll(p[0], step, axis))
        return quick_sum(s, (SHIFT * p[1] + pltpu.roll(p[1], step, axis)) + miss)

    def minus(a, factor, b):
        p, e = two_prod(factor, b[0])
        s, miss = two_sum(a[0], -p)
        return quick_sum(s, (a[1] - (e + factor * b[1])) + miss)

    def ratio(p_row, top, bottom):
        y = reduced(*product((g_hi, g_lo), p_row), 1, (16, 32, 64))
        a = reduced(*product(top, y), 0, (4, 2, 1))
        b = reduced(*product(bottom, y), 0, (4, 2, 1))
        return a[0] / b[0]

    row = (jnp.where(lane < 2 * R, 1.0, 0.0), zero)
    col = (jnp.where(sub == 0, 1.0, 0.0), zero)
    gained = zero
    for _ in range(CYCLES):
        row_image, col_image = image_of(row, 1), image_of(col, 0)
        alpha = ratio(row, col, col_image)
        row_half = minus(row, alpha, row_image)
        col_half = minus(col, alpha, col_image)
        row_turned, col_turned = image_of(row_half, 1), image_of(col_half, 0)
        omega = ratio(row_turned, col_half, col_turned)
        gained = gained + ((alpha / SCALE) * col[0] + (omega / SCALE) * col_half[0])
        row = minus(row_half, omega, row_turned)
        col = minus(col_half, omega, col_turned)

    def spread(x, k):
        return jnp.broadcast_to(x[k : k + 1], (8, LANES))

    r_factor = [spread(col[0], k) for k in range(VECS)]
    x_factor = [spread(gained, k) for k in range(VECS - 1)]
    rows, cols = guess_ref.shape[:2]
    for i in range(rows):
        for t in range(cols // 8):
            for h in range(2):
                c, l = slice(8 * t, 8 * t + 8), slice(h * LANES, (h + 1) * LANES)
                v = [vec_ref[k, h, i, c] for k in range(VECS)]
                x, r = x_factor[0] * v[0], r_factor[0] * v[0]
                for k in range(1, VECS):
                    r = r + r_factor[k] * v[k]
                    if k < VECS - 1:
                        x = x + x_factor[k] * v[k]
                x_ref[i, c, l] = guess_ref[i, c, l] + x
                r_ref[i, c, l] = r


def body(adjoint_guess, velocity, leaf_rate, canopy, solid, receptors):
    rows, cols, lanes = adjoint_guess.shape
    ngx, ngy = lax.axis_size("gx"), lax.axis_size("gy")
    devices = ngx * ngy
    width = cols + 2 * HALO
    win = rows + 2 * DEPTH
    reaction = penalty * solid.astype(jnp.float32) + leaf_gain * leaf_rate * canopy.astype(
        jnp.float32
    )
    fields = jnp.concatenate([velocity, reaction[None]], axis=0).reshape(4, rows, cols, NZ)
    fields = jnp.transpose(fields, (1, 2, 0, 3)).reshape(rows, cols, 4 * NZ)
    payload = jnp.concatenate([adjoint_guess, fields], axis=-1)
    own = lax.all_gather(payload, "gx", axis=0, tiled=True)
    up = [(j, j + 1) for j in range(ngy - 1)]
    down = [(j + 1, j) for j in range(ngy - 1)]
    left = lax.ppermute(own[:, cols - HALO :], "gy", up)
    right = lax.ppermute(own[:, :HALO], "gy", down)

    source_lane = jnp.arange(4 * NZ)[:, None]
    wide_lane = jnp.arange(4 * NZ * R)[None, :]
    spread = (source_lane == wide_lane // R).astype(jnp.bfloat16)
    spread = jnp.concatenate([spread] * 3, axis=0)

    vmem = pl.BlockSpec(memory_space=pltpu.VMEM)
    smem = pl.BlockSpec(memory_space=pltpu.SMEM)
    gram, vectors = pl.pallas_call(
        functools.partial(krylov_kernel, rows, cols),
        out_shape=(
            jax.ShapeDtypeStruct((devices * 8, LANES), jnp.float32),
            jax.ShapeDtypeStruct((VECS, 2, rows, cols, LANES), jnp.float32),
        ),
        in_specs=[smem, vmem, vmem, vmem, vmem],
        out_specs=(vmem, vmem),
        scratch_shapes=[
            pltpu.VMEM((DEPTH + 1, 2, win, width + 16, LANES), jnp.float32),
            pltpu.VMEM((7, 2, win - 2, width, LANES), jnp.float32),
            pltpu.VMEM(((win - 2) * width, LANES), jnp.float32),
            pltpu.VMEM(((win - 2) * width, 8 * LANES), jnp.float32),
            pltpu.VMEM((VECS, 2 * rows * cols // 8, 8, LANES), jnp.float32),
            pltpu.VMEM((VECS, 2 * rows * cols // 8, 8, LANES), jnp.float32),
        ],
        compiler_params=pltpu.CompilerParams(vmem_limit_bytes=40 * 1024 * 1024),
        name="krylov",
    )(receptors, left, own, right, spread)
    everyone = lax.all_to_all(gram, ("gx", "gy"), 0, 0, tiled=True)
    out = jax.ShapeDtypeStruct((rows, cols, lanes), jnp.float32)
    return pl.pallas_call(
        finish_kernel,
        out_shape=(out, out),
        in_specs=[vmem, vmem, vmem],
        out_specs=(vmem, vmem),
        compiler_params=pltpu.CompilerParams(vmem_limit_bytes=16 * 1024 * 1024),
        name="finish",
    )(everyone, adjoint_guess, vectors)


def solution(mesh):
    return jax.shard_map(
        body,
        mesh=mesh,
        in_specs=(
            P("gx", "gy", None),
            P(None, "gx", "gy"),
            P("gx", "gy"),
            P("gx", "gy"),
            P("gx", "gy"),
            P(),
        ),
        out_specs=(P("gx", "gy", None), P("gx", "gy", None)),
        check_vma=False,
    )
```

time: 288 us -> 56.4 us (0.20)
  blocking collectives: 175 us -> 34.2 us
  starting transfers between devices: 61 us -> 4.33 us
  waiting for transfers between devices: 26.5 us -> 0.84 us
  local copies, waits for them, and re-layouts: 16.4 us -> 1.76 us
  Pallas kernels: 0 us -> 13.3 us
  other arithmetic: 5.81 us -> 0.99 us
    psum x4 -> x0, blocking collectives: 175 us -> none  [the longest x2 89.9 us: body(): lax.psum((per_receptor(halfway, halfway), per_receptor(halfway, turned),...]
    ppermute x28 -> x2, starting transfers between devices: 61 us -> 4.33 us  [the longest x1 3.04 us: body(): left = lax.ppermute(own[:, cols - HALO:], 'gy', up)]
    ppermute x28 -> x2, waiting for transfers between devices: 26.5 us -> 0.84 us  [the longest x1 0.83 us: body(): left = lax.ppermute(own[:, cols - HALO:], 'gy', up)]
    all_to_all x0 -> x1, blocking collectives: none -> 17.9 us  [body(): everyone = lax.all_to_all(gram, ('gx', 'gy'), 0, 0, tiled=True)]
    all_gather x0 -> x1, blocking collectives: none -> 16.2 us  [body(): own = lax.all_gather(payload, 'gx', axis=0, tiled=True)]
    pallas_call x0 -> x2, Pallas kernels: none -> 13.3 us  [the longest x1 10.7 us: body(): pl.pallas_call(functools.partial(krylov_kernel, rows, cols), out_shape=(j...]
    reshape x28 -> x1, local copies, waits for them, and re-layouts: 11.2 us -> 0.12 us  [body(): fields = jnp.transpose(fields, (1, 2, 0, 3)).reshape(rows, cols, 4 * NZ)]
    reduce_sum x14 -> x0, other arithmetic: 4.02 us -> none  [per_receptor(): return jnp.sum((first * second).reshape(-1, R), axis=0)]
  transfers between devices with their start and end apart: 28 -> 2, of which waited for: 13 -> 1; matrix products, arithmetic and copies ran while one was open for 3% -> 0% of each run, Pallas kernels for 0% -> 0%
where the time goes in v1:
time: 56.4 us; the launch traced here: 56.1 us
  blocking collectives  34.2 us (61%)
  Pallas kernels  13.3 us (24%)
  starting transfers between devices  4.33 us (8%)
  local copies, waits for them, and re-layouts  1.76 us (3%)
  other arithmetic  0.99 us (2%)
  waiting for transfers between devices  0.84 us (1%)
  between operations  0.73 us (1%)
    all_to_all x1, blocking collectives, body(): everyone = lax.all_to_all(gram, ('gx', 'gy'), 0, 0, tiled=True)  17.9 us
    all_gather x1, blocking collectives, body(): own = lax.all_gather(payload, 'gx', axis=0, tiled=True)  16.2 us
    pallas_call x1, Pallas kernels, body(): pl.pallas_call(functools.partial(krylov_kernel, rows, cols), out_shape=(j...  10.7 us
    ppermute x1, starting transfers between devices, body(): left = lax.ppermute(own[:, cols - HALO:], 'gy', up)  3.04 us
    pallas_call x1, Pallas kernels, body(): pl.pallas_call(finish_kernel, out_shape=(out, out), in_specs=[vmem, vmem,...  2.59 us
    unnamed x6, local copies, waits for them, and re-layouts  1.38 us
    ppermute x1, starting transfers between devices, body(): right = lax.ppermute(own[:, :HALO], 'gy', down)  1.29 us
  transfers between devices with their start and end apart: 2, of which 1 were waited for; matrix products, arithmetic and copies ran while one was open for 0% of the time, Pallas kernels for 0%

profile of v1, /device:TPU:0, one launch (start us, length us, event | category | flops | bytes accessed | tf_op | source)
XLA Modules:
  0.0 56.1 jit_solution(18008809195630006002)
XLA Ops:
  0.6 0.7 %multiply_add_fusion = f32[4,512]{1,0:T(4,128)S(1)} fusion(s32[4,512]{1,0:T(4,128)} %param.9, f32[4,512]{1,0:T(4,128)} %param.8, s32[4,512]{1,0:T(4,128)} %param.10), kind=kLoop, calls=%fused_computation.7 | loop fusion | flops 12288 | bytes 32768 | tf_op jit(solution)/shard_map/add | solution.py:353
  1.4 0.0 copy-start.2
  1.4 0.1 concatenate.17
  1.5 0.7 %copy-done.2 = f32[3,4,512]{2,1,0:T(4,128)S(1)} copy-done((f32[3,4,512]{2,1,0:T(4,128)S(1)}, f32[3,4,512]{2,1,0:T(4,128)}, u32[]{:S(2)}) %copy-start.2) | copy-done | bytes 24600
  2.1 0.1 concatenate.16
  2.2 0.1 copy.10
  2.3 0.1 maximum_bitcast_fusion
  2.4 0.0 copy-start
  2.4 0.1 reshape.50
  2.5 0.7 %copy-done = f32[4,16,256]{2,1,0:T(8,128)S(1)} copy-done((f32[4,16,256]{2,1,0:T(8,128)S(1)}, f32[4,16,256]{2,1,0:T(8,128)}, u32[]{:S(2)}) %copy-start) | copy-done | bytes 65560
  3.2 16.2 %all_gather.3.own_ref = f32[16,16,384]{2,1,0:T(8,128)S(1)} all-gather(f32[4,16,384]{2,1,0:T(8,128)S(1)} %pad_maximum_fusion), channel_id=1, replica_groups=mesh['gx'=4,'gy'=8] {'gx'}, dimensions={0}, use_global_device_ids=true | all-gather | bytes 491520 | tf_op jit(solution)/shard_map/all_gather | solution.py:359
  19.5 1.3 %collective-permute-start.1 = (f32[16,8,384]{2,1,0:T(8,128)S(1)}, f32[16,8,384]{2,1,0:T(8,128)S(1)}, u32[]{:S(2)}, u32[]{:S(2)}) collective-permute-start(f32[16,8,384]{2,1,0:T(8,128)S(1)} %get-tuple-element.6), channel_id=1, source_target_pairs={{1,0},{2,1},{3,2},{4,3},{5,4},{6,5},{7,6},{9,8},{10,9},{11,10},{12... | collective-permute-start | bytes 589832 | tf_op jit(solution)/shard_map/ppermute | solution.py:363
  20.8 3.0 %collective-permute-start = (f32[16,8,384]{2,1,0:T(8,128)S(1)}, f32[16,8,384]{2,1,0:T(8,128)S(1)}, u32[]{:S(2)}, u32[]{:S(2)}) collective-permute-start(f32[16,8,384]{2,1,0:T(8,128)S(1)} %get-tuple-element.7), channel_id=1, source_target_pairs={{0,1},{1,2},{2,3},{3,4},{4,5},{5,6},{6,7},{8,9},{9,10},{10,11},{11... | collective-permute-start | bytes 589832 | tf_op jit(solution)/shard_map/ppermute | solution.py:362
  23.8 0.1 iota_compare_fusion
  23.9 0.0 copy-start.1
  23.9 0.1 add_convert_fusion.ex_ref
  24.0 0.0 collective-permute-done.1.right_ref
  24.0 0.8 %collective-permute-done.left_ref = f32[16,8,384]{2,1,0:T(8,128)S(1)} collective-permute-done((f32[16,8,384]{2,1,0:T(8,128)S(1)}, f32[16,8,384]{2,1,0:T(8,128)S(1)}, u32[]{:S(2)}, u32[]{:S(2)}) %collective-permute-start) | collective-permute-done | bytes 196640 | tf_op jit(solution)/shard_map/ppermute | solution.py:362
  24.9 0.0 copy-done.1
  24.9 10.7 %krylov.1 = (f32[256,128]{1,0:T(8,128)S(1)}, f32[7,2,4,16,128]{4,3,2,1,0:T(8,128)S(1)}) custom-call(s32[8]{0:T(128)S(1)} %copy-done.1, f32[16,8,384]{2,1,0:T(8,128)S(1)} %collective-permute-done.left_ref, f32[16,16,384]{2,1,0:T(8,128)S(1)} %all_gather.3.own_ref, f32[16,8,384]{2,1,0:T(8,128)S(1)} %collective-permute-done.1.right_ref, ...), custom_call_target="tpu_custom_call" | custom-call | tf_op jit(solution)/shard_map/krylov/pallas_call | solution.py:372
  35.6 17.9 %all_to_all.11 = f32[32,8,128]{2,1,0:T(8,128)S(1)} all-to-all(f32[32,8,128]{2,1,0:T(8,128)S(1)} %bitcast.6), channel_id=1, replica_groups=mesh['gx'=4,'gy'=8] {'gx','gy'}, dimensions={0} | all-to-all | bytes 262144 | tf_op jit(solution)/shard_map/all_to_all | solution.py:391
  53.5 2.6 %finish.1 = (f32[4,16,256]{2,1,0:T(8,128)}, f32[4,16,256]{2,1,0:T(8,128)}) custom-call(f32[256,128]{1,0:T(8,128)S(1)} %bitcast.5, f32[4,16,256]{2,1,0:T(8,128)S(1)} %copy-done, f32[7,2,4,16,128]{4,3,2,1,0:T(8,128)S(1)} %get-tuple-element.5.vec_ref), custom_call_target="tpu_custom_call" | custom-call | tf_op jit(solution)/shard_map/finish/pallas_call | solution.py:393
  (3 shorter events, 0.0 us)
Async XLA Ops:
  1.4 0.7 %copy-start.2 = (f32[3,4,512]{2,1,0:T(4,128)S(1)}, f32[3,4,512]{2,1,0:T(4,128)}, u32[]{:S(2)}) copy-start(f32[3,4,512]{2,1,0:T(4,128)} %param.7) | copy-start | bytes 73732
  2.4 0.8 %copy-start = (f32[4,16,256]{2,1,0:T(8,128)S(1)}, f32[4,16,256]{2,1,0:T(8,128)}, u32[]{:S(2)}) copy-start(f32[4,16,256]{2,1,0:T(8,128)} %guess_ref.1) | copy-start | bytes 196612
  19.5 4.5 %collective-permute-start.1 = (f32[16,8,384]{2,1,0:T(8,128)S(1)}, f32[16,8,384]{2,1,0:T(8,128)S(1)}, u32[]{:S(2)}, u32[]{:S(2)}) collective-permute-start(f32[16,8,384]{2,1,0:T(8,128)S(1)} %get-tuple-element.6), channel_id=1, source_target_pairs={{1,0},{2,1},{3,2},{4,3},{5,4},{6,5},{7,6},{9,8},{10,9},{11,10},{12... | collective-permute-start | bytes 589832 | tf_op jit(solution)/shard_map/ppermute | solution.py:363
  20.8 4.1 %collective-permute-start = (f32[16,8,384]{2,1,0:T(8,128)S(1)}, f32[16,8,384]{2,1,0:T(8,128)S(1)}, u32[]{:S(2)}, u32[]{:S(2)}) collective-permute-start(f32[16,8,384]{2,1,0:T(8,128)S(1)} %get-tuple-element.7), channel_id=1, source_target_pairs={{0,1},{1,2},{2,3},{3,4},{4,5},{5,6},{6,7},{8,9},{9,10},{10,11},{11... | collective-permute-start | bytes 589832 | tf_op jit(solution)/shard_map/ppermute | solution.py:362
  23.9 1.0 %copy-start.1 = (s32[8]{0:T(128)S(1)}, s32[8]{0:T(128)}, u32[]{:S(2)}) copy-start(s32[8]{0:T(128)} %rec_ref.1) | copy-start | bytes 100

commit v2 on v1

--- a/solution.py
+++ b/solution.py
@@ -79,14 +79,14 @@
 
     spans = ((0, HALO), (HALO, HALO + cols), (HALO + cols, width))
 
-    @pl.loop(0, win)
+    @pl.loop(0, win, unroll=True)
     def _(i):
         ok, at = inside_row(i)
         for h in range(2):
             for (c0, c1), piece in zip(spans, parts(at, h * LANES)):
                 f_ref[0, h, i, 8 + c0 : 8 + c1] = piece * ok
 
-    @pl.loop(0, crows)
+    @pl.loop(0, crows, unroll=True)
     def _(i):
         _, at = inside_row(i + 1)
         base = pl.multiple_of(i * width, 8)
@@ -104,7 +104,7 @@
         preferred_element_type=jnp.float32,
     )
 
-    @pl.loop(0, crows)
+    @pl.loop(0, crows, unroll=True)
     def _(i):
         ok, _ = inside_row(i + 1)
         base = pl.multiple_of(i * width, 8)
@@ -139,31 +139,37 @@
         src, dst = step - 1, step
         shown = range(tiles) if step < DEPTH else range(HALO // 8, tiles - HALO // 8)
 
-        @pl.loop(step, win - step)
-        def _(i):
+        def load(i):
+            return [[f_ref[src, h, i, 8 + 8 * t : 16 + 8 * t] for t in range(tiles)] for h in range(2)]
+
+        def one_row(i, carry):
+            west, mid = carry
+            east = load(i + 1)
+            ahead = [[pltpu.roll(m, 7, 0) for m in mid[h]] for h in range(2)]
+            behind = [[pltpu.roll(m, 1, 0) for m in mid[h]] for h in range(2)]
             for t in shown:
-                c0 = 8 + 8 * t
-                mid = [f_ref[src, h, i, c0 : c0 + 8] for h in range(2)]
-                up = [pltpu.roll(m, LANES - R, 1) for m in mid]
-                down = [pltpu.roll(m, R, 1) for m in mid]
+                up = [pltpu.roll(mid[h][t], LANES - R, 1) for h in range(2)]
+                down = [pltpu.roll(mid[h][t], R, 1) for h in range(2)]
                 above = [jnp.where(lane < LANES - R, up[0], up[1]), up[1]]
                 below = [down[0], jnp.where(lane >= R, down[1], down[0])]
                 for h in range(2):
-                    near = [
-                        mid[h],
-                        f_ref[src, h, i + 1, c0 : c0 + 8],
-                        f_ref[src, h, i - 1, c0 : c0 + 8],
-                        f_ref[src, h, i, c0 + 1 : c0 + 9],
-                        f_ref[src, h, i, c0 - 1 : c0 + 7],
-                        above[h],
-                        below[h],
-                    ]
+                    north, south = ahead[h][t], behind[h][t]
+                    if t + 1 < tiles:
+                        north = jnp.where(sub < 7, north, ahead[h][t + 1])
+                    if t > 0:
+                        south = jnp.where(sub > 0, south, behind[h][t - 1])
+                    near = [mid[h][t], east[h][t], west[h][t], north, south, above[h], below[h]]
                     terms = [
                         coef_ref[c, h, i - 1, 8 * t : 8 * t + 8] * near[c] for c in range(7)
                     ]
                     image = (terms[0] - terms[1]) - (terms[2] + terms[3])
                     image = image - ((terms[4] + terms[5]) + terms[6])
-                    f_ref[dst, h, i, c0 : c0 + 8] = finish(image, mid[h])
+                    f_ref[dst, h, i, 8 + 8 * t : 16 + 8 * t] = finish(image, mid[h][t])
+            return mid, east
+
+        carry = load(step - 1), load(step)
+        for i in range(step, win - step):
+            carry = one_row(i, carry)
 
     apply(1, lambda image, mid: -SCALE * image)
     for q in range(R):
@@ -210,7 +216,7 @@
                 out.append((s, e + ((cross + lo[i] * lo[j]) + miss)))
             return tuple(out)
 
-        done = lax.fori_loop(0, count, add, tuple((zero, zero) for _ in pairs))
+        done = lax.fori_loop(0, count, add, tuple((zero, zero) for _ in pairs), unroll=True)
         for pair, value in zip(pairs, done):
             sums[pair] = value
 

time: 56.4 us -> 50.2 us (0.89)
  Pallas kernels: 13.3 us -> 7.08 us
    pallas_call x1, Pallas kernels: 10.7 us -> 4.49 us  [body(): pl.pallas_call(functools.partial(krylov_kernel, rows, cols), out_shape=(j...]
where the time goes in v2:
time: 50.2 us; the launch traced here: 49.9 us
  blocking collectives  34.1 us (68%)
  Pallas kernels  7.08 us (14%)
  starting transfers between devices  4.33 us (9%)
  local copies, waits for them, and re-layouts  1.76 us (4%)
  other arithmetic  0.99 us (2%)
  waiting for transfers between devices  0.84 us (2%)
  between operations  0.73 us (1%)
    all_to_all x1, blocking collectives, body(): everyone = lax.all_to_all(gram, ('gx', 'gy'), 0, 0, tiled=True)  17.9 us
    all_gather x1, blocking collectives, body(): own = lax.all_gather(payload, 'gx', axis=0, tiled=True)  16.2 us
    pallas_call x1, Pallas kernels, body(): pl.pallas_call(functools.partial(krylov_kernel, rows, cols), out_shape=(j...  4.49 us
    ppermute x1, starting transfers between devices, body(): left = lax.ppermute(own[:, cols - HALO:], 'gy', up)  3.04 us
    pallas_call x1, Pallas kernels, body(): pl.pallas_call(finish_kernel, out_shape=(out, out), in_specs=[vmem, vmem,...  2.59 us
    unnamed x6, local copies, waits for them, and re-layouts  1.38 us
    ppermute x1, starting transfers between devices, body(): right = lax.ppermute(own[:, :HALO], 'gy', down)  1.29 us
  transfers between devices with their start and end apart: 2, of which 1 were waited for; matrix products, arithmetic and copies ran while one was open for 0% of the time, Pallas kernels for 0%

profile of v2, /device:TPU:0, one launch (start us, length us, event | category | flops | bytes accessed | tf_op | source)
XLA Modules:
  0.0 49.9 jit_solution(13598767804278362513)
XLA Ops:
  0.6 0.7 %multiply_add_fusion = f32[4,512]{1,0:T(4,128)S(1)} fusion(s32[4,512]{1,0:T(4,128)} %param.9, f32[4,512]{1,0:T(4,128)} %param.8, s32[4,512]{1,0:T(4,128)} %param.10), kind=kLoop, calls=%fused_computation.7 | loop fusion | flops 12288 | bytes 32768 | tf_op jit(solution)/shard_map/add | solution.py:359
  1.4 0.0 copy-start.2
  1.4 0.1 concatenate.17
  1.5 0.7 %copy-done.2 = f32[3,4,512]{2,1,0:T(4,128)S(1)} copy-done((f32[3,4,512]{2,1,0:T(4,128)S(1)}, f32[3,4,512]{2,1,0:T(4,128)}, u32[]{:S(2)}) %copy-start.2) | copy-done | bytes 24600
  2.1 0.1 concatenate.16
  2.2 0.1 copy.10
  2.3 0.1 maximum_bitcast_fusion
  2.4 0.0 copy-start
  2.4 0.1 reshape.50
  2.5 0.7 %copy-done = f32[4,16,256]{2,1,0:T(8,128)S(1)} copy-done((f32[4,16,256]{2,1,0:T(8,128)S(1)}, f32[4,16,256]{2,1,0:T(8,128)}, u32[]{:S(2)}) %copy-start) | copy-done | bytes 65560
  3.2 16.2 %all_gather.3.own_ref = f32[16,16,384]{2,1,0:T(8,128)S(1)} all-gather(f32[4,16,384]{2,1,0:T(8,128)S(1)} %pad_maximum_fusion), channel_id=1, replica_groups=mesh['gx'=4,'gy'=8] {'gx'}, dimensions={0}, use_global_device_ids=true | all-gather | bytes 491520 | tf_op jit(solution)/shard_map/all_gather | solution.py:365
  19.5 1.3 %collective-permute-start.1 = (f32[16,8,384]{2,1,0:T(8,128)S(1)}, f32[16,8,384]{2,1,0:T(8,128)S(1)}, u32[]{:S(2)}, u32[]{:S(2)}) collective-permute-start(f32[16,8,384]{2,1,0:T(8,128)S(1)} %get-tuple-element.6), channel_id=1, source_target_pairs={{1,0},{2,1},{3,2},{4,3},{5,4},{6,5},{7,6},{9,8},{10,9},{11,10},{12... | collective-permute-start | bytes 589832 | tf_op jit(solution)/shard_map/ppermute | solution.py:369
  20.8 3.0 %collective-permute-start = (f32[16,8,384]{2,1,0:T(8,128)S(1)}, f32[16,8,384]{2,1,0:T(8,128)S(1)}, u32[]{:S(2)}, u32[]{:S(2)}) collective-permute-start(f32[16,8,384]{2,1,0:T(8,128)S(1)} %get-tuple-element.7), channel_id=1, source_target_pairs={{0,1},{1,2},{2,3},{3,4},{4,5},{5,6},{6,7},{8,9},{9,10},{10,11},{11... | collective-permute-start | bytes 589832 | tf_op jit(solution)/shard_map/ppermute | solution.py:368
  23.8 0.1 iota_compare_fusion
  23.9 0.0 copy-start.1
  23.9 0.1 add_convert_fusion.ex_ref
  24.0 0.0 collective-permute-done.1.right_ref
  24.0 0.8 %collective-permute-done.left_ref = f32[16,8,384]{2,1,0:T(8,128)S(1)} collective-permute-done((f32[16,8,384]{2,1,0:T(8,128)S(1)}, f32[16,8,384]{2,1,0:T(8,128)S(1)}, u32[]{:S(2)}, u32[]{:S(2)}) %collective-permute-start) | collective-permute-done | bytes 196640 | tf_op jit(solution)/shard_map/ppermute | solution.py:368
  24.9 0.0 copy-done.1
  24.9 4.5 %krylov.1 = (f32[256,128]{1,0:T(8,128)S(1)}, f32[7,2,4,16,128]{4,3,2,1,0:T(8,128)S(1)}) custom-call(s32[8]{0:T(128)S(1)} %copy-done.1, f32[16,8,384]{2,1,0:T(8,128)S(1)} %collective-permute-done.left_ref, f32[16,16,384]{2,1,0:T(8,128)S(1)} %all_gather.3.own_ref, f32[16,8,384]{2,1,0:T(8,128)S(1)} %collective-permute-done.1.right_ref, ...), custom_call_target="tpu_custom_call" | custom-call | tf_op jit(solution)/shard_map/krylov/pallas_call | solution.py:378
  29.4 17.9 %all_to_all.11 = f32[32,8,128]{2,1,0:T(8,128)S(1)} all-to-all(f32[32,8,128]{2,1,0:T(8,128)S(1)} %bitcast.6), channel_id=1, replica_groups=mesh['gx'=4,'gy'=8] {'gx','gy'}, dimensions={0} | all-to-all | bytes 262144 | tf_op jit(solution)/shard_map/all_to_all | solution.py:397
  47.3 2.6 %finish.1 = (f32[4,16,256]{2,1,0:T(8,128)}, f32[4,16,256]{2,1,0:T(8,128)}) custom-call(f32[256,128]{1,0:T(8,128)S(1)} %bitcast.5, f32[4,16,256]{2,1,0:T(8,128)S(1)} %copy-done, f32[7,2,4,16,128]{4,3,2,1,0:T(8,128)S(1)} %get-tuple-element.5.vec_ref), custom_call_target="tpu_custom_call" | custom-call | tf_op jit(solution)/shard_map/finish/pallas_call | solution.py:399
  (3 shorter events, 0.0 us)
Async XLA Ops:
  1.4 0.7 %copy-start.2 = (f32[3,4,512]{2,1,0:T(4,128)S(1)}, f32[3,4,512]{2,1,0:T(4,128)}, u32[]{:S(2)}) copy-start(f32[3,4,512]{2,1,0:T(4,128)} %param.7) | copy-start | bytes 73732
  2.4 0.8 %copy-start = (f32[4,16,256]{2,1,0:T(8,128)S(1)}, f32[4,16,256]{2,1,0:T(8,128)}, u32[]{:S(2)}) copy-start(f32[4,16,256]{2,1,0:T(8,128)} %guess_ref.1) | copy-start | bytes 196612
  19.5 4.5 %collective-permute-start.1 = (f32[16,8,384]{2,1,0:T(8,128)S(1)}, f32[16,8,384]{2,1,0:T(8,128)S(1)}, u32[]{:S(2)}, u32[]{:S(2)}) collective-permute-start(f32[16,8,384]{2,1,0:T(8,128)S(1)} %get-tuple-element.6), channel_id=1, source_target_pairs={{1,0},{2,1},{3,2},{4,3},{5,4},{6,5},{7,6},{9,8},{10,9},{11,10},{12... | collective-permute-start | bytes 589832 | tf_op jit(solution)/shard_map/ppermute | solution.py:369
  20.8 4.1 %collective-permute-start = (f32[16,8,384]{2,1,0:T(8,128)S(1)}, f32[16,8,384]{2,1,0:T(8,128)S(1)}, u32[]{:S(2)}, u32[]{:S(2)}) collective-permute-start(f32[16,8,384]{2,1,0:T(8,128)S(1)} %get-tuple-element.7), channel_id=1, source_target_pairs={{0,1},{1,2},{2,3},{3,4},{4,5},{5,6},{6,7},{8,9},{9,10},{10,11},{11... | collective-permute-start | bytes 589832 | tf_op jit(solution)/shard_map/ppermute | solution.py:368
  23.9 1.0 %copy-start.1 = (s32[8]{0:T(128)S(1)}, s32[8]{0:T(128)}, u32[]{:S(2)}) copy-start(s32[8]{0:T(128)} %rec_ref.1) | copy-start | bytes 100

commit v3 on v2

--- a/solution.py
+++ b/solution.py
@@ -48,6 +48,61 @@
     ah, al = split(a)
     bh, bl = split(b)
     return p, (((ah * bh - p) + ah * bl) + al * bh) + al * bl
+
+
+def pack_kernel(
+    guess_ref, velocity_ref, leaf_ref, canopy_ref, solid_ref, out_ref,
+    v_ref, l_ref, c_ref, s_ref, sem,
+):
+    copies = [
+        pltpu.make_async_copy(velocity_ref, v_ref, sem.at[0]),
+        pltpu.make_async_copy(leaf_ref, l_ref, sem.at[1]),
+        pltpu.make_async_copy(canopy_ref, c_ref, sem.at[2]),
+        pltpu.make_async_copy(solid_ref, s_ref, sem.at[3]),
+    ]
+    rows, cols = guess_ref.shape[:2]
+    times = out_ref.shape[0] // rows
+    for n in range(times):
+        place = out_ref.at[pl.ds(n * rows, rows), :, pl.ds(0, NZ * R)]
+        copies.append(pltpu.make_async_copy(guess_ref, place, sem.at[4 + n]))
+    for copy in copies:
+        copy.start()
+    for copy in copies[:4]:
+        copy.wait()
+    lane = lax.broadcasted_iota(jnp.int32, (8, LANES), 1)
+    sub = lax.broadcasted_iota(jnp.int32, (8, LANES), 0)
+    reaction = penalty * s_ref[...].astype(jnp.float32) + leaf_gain * l_ref[...] * c_ref[
+        ...
+    ].astype(jnp.float32)
+    fields = [v_ref[0], v_ref[1], v_ref[2], reaction]
+    for x in range(rows):
+        for t in range(cols // 8):
+            base = 8 * t * NZ
+            spread = []
+            for field in fields:
+                near = field[x : x + 1, base : base + LANES]
+                far = field[x : x + 1, base + LANES : base + 2 * LANES]
+                spread.append(
+                    jnp.where(
+                        sub < 4,
+                        jnp.broadcast_to(near, (8, LANES)),
+                        jnp.broadcast_to(far, (8, LANES)),
+                    )
+                )
+            whole = None
+            for d in range(4):
+                mixed = spread[d]
+                for s in range(1, 4):
+                    mixed = jnp.where(sub % 4 == s, spread[(s + d) % 4], mixed)
+                if d == 0:
+                    whole = mixed
+                else:
+                    here = (lane // NZ - sub) % 4 == d
+                    whole = jnp.where(here, pltpu.roll(mixed, NZ * d, 1), whole)
+            for n in range(times):
+                out_ref[n * rows + x, 8 * t : 8 * t + 8, NZ * R :] = whole
+    for copy in copies[4:]:
+        copy.wait()
 
 
 def krylov_kernel(
@@ -356,13 +411,24 @@
     devices = ngx * ngy
     width = cols + 2 * HALO
     win = rows + 2 * DEPTH
-    reaction = penalty * solid.astype(jnp.float32) + leaf_gain * leaf_rate * canopy.astype(
-        jnp.float32
-    )
-    fields = jnp.concatenate([velocity, reaction[None]], axis=0).reshape(4, rows, cols, NZ)
-    fields = jnp.transpose(fields, (1, 2, 0, 3)).reshape(rows, cols, 4 * NZ)
-    payload = jnp.concatenate([adjoint_guess, fields], axis=-1)
-    own = lax.all_gather(payload, "gx", axis=0, tiled=True)
+    vmem = pl.BlockSpec(memory_space=pltpu.VMEM)
+    smem = pl.BlockSpec(memory_space=pltpu.SMEM)
+    hbm = pl.BlockSpec(memory_space=pl.ANY)
+    payload = pl.pallas_call(
+        pack_kernel,
+        out_shape=jax.ShapeDtypeStruct((ngx * rows, cols, lanes + 4 * NZ), jnp.float32),
+        in_specs=[hbm] * 5,
+        out_specs=vmem,
+        scratch_shapes=[
+            pltpu.VMEM(velocity.shape, jnp.float32),
+            pltpu.VMEM(leaf_rate.shape, jnp.float32),
+            pltpu.VMEM(canopy.shape, jnp.int32),
+            pltpu.VMEM(solid.shape, jnp.int32),
+            pltpu.SemaphoreType.DMA((4 + ngx,)),
+        ],
+        name="pack",
+    )(adjoint_guess, velocity, leaf_rate, canopy, solid)
+    own = lax.all_to_all(payload, "gx", 0, 0, tiled=True)
     up = [(j, j + 1) for j in range(ngy - 1)]
     down = [(j + 1, j) for j in range(ngy - 1)]
     left = lax.ppermute(own[:, cols - HALO :], "gy", up)
@@ -373,8 +439,6 @@
     spread = (source_lane == wide_lane // R).astype(jnp.bfloat16)
     spread = jnp.concatenate([spread] * 3, axis=0)
 
-    vmem = pl.BlockSpec(memory_space=pltpu.VMEM)
-    smem = pl.BlockSpec(memory_space=pltpu.SMEM)
     gram, vectors = pl.pallas_call(
         functools.partial(krylov_kernel, rows, cols),
         out_shape=(

time: 50.2 us -> 48.6 us (0.968)
  blocking collectives: 34.1 us -> 15.3 us
  waiting for transfers between devices: 0.84 us -> 12.5 us
  starting transfers between devices: 4.33 us -> 10.7 us
  Pallas kernels: 7.08 us -> 8.88 us
  local copies, waits for them, and re-layouts: 1.76 us -> 0.04 us
  other arithmetic: 0.99 us -> 0.16 us
    all_gather x1 -> x0, blocking collectives: 16.2 us -> none  [body(): own = lax.all_gather(payload, 'gx', axis=0, tiled=True)]
    all_to_all x0 -> x1, waiting for transfers between devices: none -> 11.7 us  [body(): own = lax.all_to_all(payload, 'gx', 0, 0, tiled=True)]
    all_to_all x0 -> x1, starting transfers between devices: none -> 6.33 us  [body(): own = lax.all_to_all(payload, 'gx', 0, 0, tiled=True)]
    all_to_all x1, blocking collectives: 17.9 us -> 15.3 us  [body(): everyone = lax.all_to_all(gram, ('gx', 'gy'), 0, 0, tiled=True)]
    pallas_call x0 -> x1, Pallas kernels: none -> 1.81 us  [body(): pl.pallas_call(pack_kernel, out_shape=jax.ShapeDtypeStruct((ngx * rows, c...]
    unnamed x6 -> x4, local copies, waits for them, and re-layouts: 1.38 us -> 0.01 us
    add x1 -> x0, other arithmetic: 0.74 us -> none  [body(): penalty * solid.astype(jnp.float32)]
  transfers between devices with their start and end apart: 2 -> 3, of which waited for: 1 -> 2; matrix products, arithmetic and copies ran while one was open for 0% -> 0% of each run, Pallas kernels for 0% -> 0%
where the time goes in v3:
time: 48.6 us; the launch traced here: 48.3 us
  blocking collectives  15.3 us (31%)
  waiting for transfers between devices  12.5 us (26%)
  starting transfers between devices  10.7 us (22%)
  Pallas kernels  8.88 us (18%)
  between operations  0.71 us (1%)
    all_to_all x1, blocking collectives, body(): everyone = lax.all_to_all(gram, ('gx', 'gy'), 0, 0, tiled=True)  15.3 us
    all_to_all x1, waiting for transfers between devices, body(): own = lax.all_to_all(payload, 'gx', 0, 0, tiled=True)  11.7 us
    all_to_all x1, starting transfers between devices, body(): own = lax.all_to_all(payload, 'gx', 0, 0, tiled=True)  6.33 us
    pallas_call x1, Pallas kernels, body(): pl.pallas_call(functools.partial(krylov_kernel, rows, cols), out_shape=(j...  4.47 us
    ppermute x1, starting transfers between devices, body(): left = lax.ppermute(own[:, cols - HALO:], 'gy', up)  3.04 us
    pallas_call x1, Pallas kernels, body(): pl.pallas_call(finish_kernel, out_shape=(out, out), in_specs=[vmem, vmem,...  2.59 us
    pallas_call x1, Pallas kernels, body(): pl.pallas_call(pack_kernel, out_shape=jax.ShapeDtypeStruct((ngx * rows, c...  1.81 us
    ppermute x1, starting transfers between devices, body(): right = lax.ppermute(own[:, :HALO], 'gy', down)  1.29 us
  transfers between devices with their start and end apart: 3, of which 2 were waited for; matrix products, arithmetic and copies ran while one was open for 0% of the time, Pallas kernels for 0%

profile of v3, /device:TPU:0, one launch (start us, length us, event | category | flops | bytes accessed | tf_op | source)
XLA Modules:
  0.0 48.3 jit_solution(15221063502249268659)
XLA Ops:
  0.6 1.8 %pack.1 = f32[16,16,384]{2,1,0:T(8,128)} custom-call(f32[4,16,256]{2,1,0:T(8,128)} %guess_ref.3, f32[3,4,512]{2,1,0:T(4,128)} %velocity_ref.1, f32[4,512]{1,0:T(4,128)} %leaf_ref.1, s32[4,512]{1,0:T(4,128)} %canopy_ref.1, s32[4,512]{1,0:T(4,128)} %solid_ref.1), custom_call_target="tpu_custom_call" | custom-call | tf_op jit(solution)/shard_map/pack/pallas_call | solution.py:417
  2.5 6.3 %all-to-all-start = ((f32[16,16,384]{2,1,0:T(8,128)}), f32[16,16,384]{2,1,0:T(8,128)S(1)}, u32[]{:S(2)}, u32[]{:S(2)}) async-start(f32[16,16,384]{2,1,0:T(8,128)} %pack.1), calls=%async_computation | async-start | bytes 786432 | tf_op jit(solution)/shard_map/all_to_all | solution.py:431
  8.8 11.7 %all-to-all-done.own_ref = f32[16,16,384]{2,1,0:T(8,128)S(1)} async-done(((f32[16,16,384]{2,1,0:T(8,128)}), f32[16,16,384]{2,1,0:T(8,128)S(1)}, u32[]{:S(2)}, u32[]{:S(2)}) %all-to-all-start) | async-done | bytes 393248 | tf_op jit(solution)/shard_map/all_to_all | solution.py:431
  20.5 1.3 %collective-permute-start.1 = (f32[16,8,384]{2,1,0:T(8,128)S(1)}, f32[16,8,384]{2,1,0:T(8,128)S(1)}, u32[]{:S(2)}, u32[]{:S(2)}) collective-permute-start(f32[16,8,384]{2,1,0:T(8,128)S(1)} %get-tuple-element.6), channel_id=1, source_target_pairs={{1,0},{2,1},{3,2},{4,3},{5,4},{6,5},{7,6},{9,8},{10,9},{11,10},{12... | collective-permute-start | bytes 589832 | tf_op jit(solution)/shard_map/ppermute | solution.py:435
  21.8 3.0 %collective-permute-start = (f32[16,8,384]{2,1,0:T(8,128)S(1)}, f32[16,8,384]{2,1,0:T(8,128)S(1)}, u32[]{:S(2)}, u32[]{:S(2)}) collective-permute-start(f32[16,8,384]{2,1,0:T(8,128)S(1)} %get-tuple-element.7), channel_id=1, source_target_pairs={{0,1},{1,2},{2,3},{3,4},{4,5},{5,6},{6,7},{8,9},{9,10},{10,11},{11... | collective-permute-start | bytes 589832 | tf_op jit(solution)/shard_map/ppermute | solution.py:434
  24.8 0.1 iota_compare_fusion
  24.9 0.0 copy-start.1
  24.9 0.1 add_convert_fusion.ex_ref
  25.0 0.0 collective-permute-done.1.right_ref
  25.0 0.8 %collective-permute-done.left_ref = f32[16,8,384]{2,1,0:T(8,128)S(1)} collective-permute-done((f32[16,8,384]{2,1,0:T(8,128)S(1)}, f32[16,8,384]{2,1,0:T(8,128)S(1)}, u32[]{:S(2)}, u32[]{:S(2)}) %collective-permute-start) | collective-permute-done | bytes 196640 | tf_op jit(solution)/shard_map/ppermute | solution.py:434
  25.9 0.0 copy-done.1
  25.9 4.5 %krylov.1 = (f32[256,128]{1,0:T(8,128)S(1)}, f32[7,2,4,16,128]{4,3,2,1,0:T(8,128)S(1)}) custom-call(s32[8]{0:T(128)S(1)} %copy-done.1, f32[16,8,384]{2,1,0:T(8,128)S(1)} %collective-permute-done.left_ref, f32[16,16,384]{2,1,0:T(8,128)S(1)} %all-to-all-done.own_ref, f32[16,8,384]{2,1,0:T(8,128)S(1)} %collective-permute-done.1.right_ref, ...), custom_call_target="tpu_custom_call" | custom-call | tf_op jit(solution)/shard_map/krylov/pallas_call | solution.py:442
  30.4 0.0 copy-start
  30.4 15.3 %all_to_all.16 = f32[32,8,128]{2,1,0:T(8,128)S(1)} all-to-all(f32[32,8,128]{2,1,0:T(8,128)S(1)} %bitcast.3), channel_id=1, replica_groups=mesh['gx'=4,'gy'=8] {'gx','gy'}, dimensions={0} | all-to-all | bytes 262144 | tf_op jit(solution)/shard_map/all_to_all | solution.py:461
  45.7 0.0 copy-done
  45.7 2.6 %finish.1 = (f32[4,16,256]{2,1,0:T(8,128)}, f32[4,16,256]{2,1,0:T(8,128)}) custom-call(f32[256,128]{1,0:T(8,128)S(1)} %bitcast.2, f32[4,16,256]{2,1,0:T(8,128)S(1)} %copy-done, f32[7,2,4,16,128]{4,3,2,1,0:T(8,128)S(1)} %get-tuple-element.5.vec_ref), custom_call_target="tpu_custom_call" | custom-call | tf_op jit(solution)/shard_map/finish/pallas_call | solution.py:463
  (2 shorter events, 0.0 us)
Async XLA Ops:
  2.5 18.0 %all-to-all-start = ((f32[16,16,384]{2,1,0:T(8,128)}), f32[16,16,384]{2,1,0:T(8,128)S(1)}, u32[]{:S(2)}, u32[]{:S(2)}) async-start(f32[16,16,384]{2,1,0:T(8,128)} %pack.1), calls=%async_computation | async-start | bytes 786432 | tf_op jit(solution)/shard_map/all_to_all | solution.py:431
  20.5 4.5 %collective-permute-start.1 = (f32[16,8,384]{2,1,0:T(8,128)S(1)}, f32[16,8,384]{2,1,0:T(8,128)S(1)}, u32[]{:S(2)}, u32[]{:S(2)}) collective-permute-start(f32[16,8,384]{2,1,0:T(8,128)S(1)} %get-tuple-element.6), channel_id=1, source_target_pairs={{1,0},{2,1},{3,2},{4,3},{5,4},{6,5},{7,6},{9,8},{10,9},{11,10},{12... | collective-permute-start | bytes 589832 | tf_op jit(solution)/shard_map/ppermute | solution.py:435
  21.8 4.1 %collective-permute-start = (f32[16,8,384]{2,1,0:T(8,128)S(1)}, f32[16,8,384]{2,1,0:T(8,128)S(1)}, u32[]{:S(2)}, u32[]{:S(2)}) collective-permute-start(f32[16,8,384]{2,1,0:T(8,128)S(1)} %get-tuple-element.7), channel_id=1, source_target_pairs={{0,1},{1,2},{2,3},{3,4},{4,5},{5,6},{6,7},{8,9},{9,10},{10,11},{11... | collective-permute-start | bytes 589832 | tf_op jit(solution)/shard_map/ppermute | solution.py:434
  24.9 1.0 %copy-start.1 = (s32[8]{0:T(128)S(1)}, s32[8]{0:T(128)}, u32[]{:S(2)}) copy-start(s32[8]{0:T(128)} %rec_ref.1) | copy-start | bytes 100
  30.4 15.3 %copy-start = (f32[4,16,256]{2,1,0:T(8,128)S(1)}, f32[4,16,256]{2,1,0:T(8,128)}, u32[]{:S(2)}) copy-start(f32[4,16,256]{2,1,0:T(8,128)} %guess_ref.3) | copy-start | bytes 196612

commit v4 on v3

--- a/solution.py
+++ b/solution.py
@@ -105,10 +105,50 @@
         copy.wait()
 
 
+def reach_of(i, rows):
+    return max(DEPTH - i, i - (DEPTH + rows - 1), 0)
+
+
+def tiles_within(reach, cols):
+    shown = []
+    for t in range((cols + 2 * HALO) // 8):
+        away = max(HALO - (8 * t + 7), 8 * t - (HALO + cols) + 1, 0)
+        if away <= reach:
+            shown.append(t)
+    return shown
+
+
+def stencil_row(west, mid, east, coef_ref, at, shown):
+    lane = lax.broadcasted_iota(jnp.int32, (8, LANES), 1)
+    sub = lax.broadcasted_iota(jnp.int32, (8, LANES), 0)
+    tiles = len(mid[0])
+    ahead = [[pltpu.roll(m, 7, 0) for m in mid[h]] for h in range(2)]
+    behind = [[pltpu.roll(m, 1, 0) for m in mid[h]] for h in range(2)]
+    images = {}
+    for t in shown:
+        up = [pltpu.roll(mid[h][t], LANES - R, 1) for h in range(2)]
+        down = [pltpu.roll(mid[h][t], R, 1) for h in range(2)]
+        above = [jnp.where(lane < LANES - R, up[0], up[1]), up[1]]
+        below = [down[0], jnp.where(lane >= R, down[1], down[0])]
+        for h in range(2):
+            north, south = ahead[h][t], behind[h][t]
+            if t + 1 < tiles:
+                north = jnp.where(sub < 7, north, ahead[h][t + 1])
+            if t > 0:
+                south = jnp.where(sub > 0, south, behind[h][t - 1])
+            near = [mid[h][t], east[h][t], west[h][t], north, south, above[h], below[h]]
+            terms = [coef_ref[c, h, at, 8 * t : 8 * t + 8] * near[c] for c in range(7)]
+            image = (terms[0] - terms[1]) - (terms[2] + terms[3])
+            images[h, t] = image - ((terms[4] + terms[5]) + terms[6])
+    return images
+
+
 def krylov_kernel(
-    rows, cols, rec_ref, left_ref, own_ref, right_ref, ex_ref, gram_ref, vec_ref,
-    f_ref, coef_ref, raw_ref, wide_ref, hi_ref, lo_ref,
+    rows, cols, rec_ref, left_ref, own_ref, right_ref, ex_ref, gram_ref, f_ref, coef_ref,
+    raw_ref, wide_ref, hi_ref, lo_ref, cell_ref, cell_sem,
 ):
+    fetch = pltpu.make_async_copy(rec_ref, cell_ref, cell_sem)
+    fetch.start()
     win = rows + 2 * DEPTH
     crows = win - 2
     width = cols + 2 * HALO
@@ -134,19 +174,16 @@
 
     spans = ((0, HALO), (HALO, HALO + cols), (HALO + cols, width))
 
-    @pl.loop(0, win, unroll=True)
-    def _(i):
+    for i in range(win):
         ok, at = inside_row(i)
         for h in range(2):
             for (c0, c1), piece in zip(spans, parts(at, h * LANES)):
-                f_ref[0, h, i, 8 + c0 : 8 + c1] = piece * ok
-
-    @pl.loop(0, crows, unroll=True)
-    def _(i):
+                f_ref[0, h, i, c0:c1] = piece * ok
+
+    for i in range(crows):
         _, at = inside_row(i + 1)
-        base = pl.multiple_of(i * width, 8)
         for (c0, c1), piece in zip(spans, parts(at, 2 * LANES)):
-            raw_ref[pl.ds(base + c0, c1 - c0), :] = piece
+            raw_ref[i * width + c0 : i * width + c1, :] = piece
 
     raw = raw_ref[...]
     first = raw.astype(jnp.bfloat16)
@@ -159,17 +196,16 @@
         preferred_element_type=jnp.float32,
     )
 
-    @pl.loop(0, crows, unroll=True)
-    def _(i):
+    for i in range(crows):
         ok, _ = inside_row(i + 1)
-        base = pl.multiple_of(i * width, 8)
-        for t in range(tiles):
+        for t in tiles_within(DEPTH - 1 - reach_of(i + 1, rows), cols):
+            at = i * width + 8 * t
             at_col = col0 + 8 * t + sub
             seen = jnp.logical_and(at_col >= 0, at_col < total_cols)
             keep = jnp.where(seen, ok * (1.0 / SCALE), 0.0)
             for h in range(2):
                 u, v, w, reaction = [
-                    wide_ref[pl.ds(base + 8 * t, 8), pl.ds((2 * c + h) * LANES, LANES)]
+                    wide_ref[at : at + 8, (2 * c + h) * LANES : (2 * c + h + 1) * LANES]
                     for c in range(4)
                 ]
                 side = [
@@ -190,51 +226,28 @@
                 for c, one in enumerate([diag] + side):
                     coef_ref[c, h, i, 8 * t : 8 * t + 8] = one * keep
 
+    def load(k, i):
+        return [[f_ref[k, h, i, 8 * t : 8 * t + 8] for t in range(tiles)] for h in range(2)]
+
     def apply(step, finish):
-        src, dst = step - 1, step
-        shown = range(tiles) if step < DEPTH else range(HALO // 8, tiles - HALO // 8)
-
-        def load(i):
-            return [[f_ref[src, h, i, 8 + 8 * t : 16 + 8 * t] for t in range(tiles)] for h in range(2)]
-
-        def one_row(i, carry):
-            west, mid = carry
-            east = load(i + 1)
-            ahead = [[pltpu.roll(m, 7, 0) for m in mid[h]] for h in range(2)]
-            behind = [[pltpu.roll(m, 1, 0) for m in mid[h]] for h in range(2)]
-            for t in shown:
-                up = [pltpu.roll(mid[h][t], LANES - R, 1) for h in range(2)]
-                down = [pltpu.roll(mid[h][t], R, 1) for h in range(2)]
-                above = [jnp.where(lane < LANES - R, up[0], up[1]), up[1]]
-                below = [down[0], jnp.where(lane >= R, down[1], down[0])]
-                for h in range(2):
-                    north, south = ahead[h][t], behind[h][t]
-                    if t + 1 < tiles:
-                        north = jnp.where(sub < 7, north, ahead[h][t + 1])
-                    if t > 0:
-                        south = jnp.where(sub > 0, south, behind[h][t - 1])
-                    near = [mid[h][t], east[h][t], west[h][t], north, south, above[h], below[h]]
-                    terms = [
-                        coef_ref[c, h, i - 1, 8 * t : 8 * t + 8] * near[c] for c in range(7)
-                    ]
-                    image = (terms[0] - terms[1]) - (terms[2] + terms[3])
-                    image = image - ((terms[4] + terms[5]) + terms[6])
-                    f_ref[dst, h, i, 8 + 8 * t : 16 + 8 * t] = finish(image, mid[h][t])
-            return mid, east
-
-        carry = load(step - 1), load(step)
+        west, mid = load(step - 1, step - 1), load(step - 1, step)
         for i in range(step, win - step):
-            carry = one_row(i, carry)
+            east = load(step - 1, i + 1)
+            shown = tiles_within(DEPTH - step - reach_of(i, rows), cols)
+            images = stencil_row(west, mid, east, coef_ref, i - 1, shown)
+            for (h, t), image in images.items():
+                f_ref[step, h, i, 8 * t : 8 * t + 8] = finish(image, mid[h][t])
+            west, mid = mid, east
 
     apply(1, lambda image, mid: -SCALE * image)
+    fetch.wait()
     for q in range(R):
-        cell = rec_ref[q]
-        i = cell // total_cols - row0
-        c = cell % total_cols - col0
+        i = cell_ref[0, q] - row0
+        c = cell_ref[1, q] - col0
         seen = (i >= 1) & (i < win - 1) & (c >= 0) & (c < width)
         i = jnp.clip(i, 1, win - 2)
         c = jnp.clip(c, 0, width - 1)
-        base = pl.multiple_of(8 + (c // 8) * 8, 8)
+        base = pl.multiple_of((c // 8) * 8, 8)
         gain = jnp.where(seen, source_gain, 0.0)
         spot = jnp.where((sub == c % 8) & (lane == R + q), gain, 0.0)
         f_ref[1, 0, i, pl.ds(base, 8)] += spot
@@ -247,10 +260,8 @@
     count = len(pieces)
     for k in range(VECS):
         for m, (h, i, t) in enumerate(pieces):
-            c0 = 8 + HALO + 8 * t
-            x = f_ref[k + 1, h, DEPTH + i, c0 : c0 + 8]
-            vec_ref[k, h, i, 8 * t : 8 * t + 8] = x
-            hi_ref[k, m], lo_ref[k, m] = split(x)
+            c0 = HALO + 8 * t
+            hi_ref[k, m], lo_ref[k, m] = split(f_ref[k + 1, h, DEPTH + i, c0 : c0 + 8])
 
     zero = jnp.zeros((8, LANES), jnp.float32)
     sums = {}
@@ -316,12 +327,25 @@
         gram_ref[8 * n : 8 * n + 8] = chunk
 
 
-def finish_kernel(gram_ref, guess_ref, vec_ref, x_ref, r_ref):
+def finish_kernel(gram_ref, f_ref, coef_ref, x_ref, r_ref):
+    rows, cols = x_ref.shape[:2]
+    tiles = (cols + 2 * HALO) // 8
     lane = lax.broadcasted_iota(jnp.int32, (8, LANES), 1)
     sub = lax.broadcasted_iota(jnp.int32, (8, LANES), 0)
     devices = gram_ref.shape[0] // 8
     ways = math.gcd(devices, 8)
     zero = jnp.zeros((8, LANES), jnp.float32)
+
+    def plus(a, b):
+        s, miss = two_sum(a[0], b[0])
+        return s, (a[1] + b[1]) + miss
+
+    def total(items):
+        while len(items) > 1:
+            half = len(items) // 2
+            pairs = [plus(items[2 * n], items[2 * n + 1]) for n in range(half)]
+            items = pairs + items[2 * half :]
+        return items[0]
 
     def gather(n, carry):
         out = []
@@ -331,78 +355,125 @@
             out.append((s, e + miss))
         return tuple(out)
 
-    items = list(lax.fori_loop(0, devices // ways, gather, ((zero, zero),) * ways))
-    while len(items) > 1:
-        half = len(items) // 2
-        merged = []
-        for n in range(half):
-            s, miss = two_sum(items[n][0], items[n + half][0])
-            merged.append((s, (items[n][1] + items[n + half][1]) + miss))
-        items = merged
-    s, e = items[0]
+    steps = devices // ways
+    s, e = total(
+        list(lax.fori_loop(0, steps, gather, ((zero, zero),) * ways, unroll=steps <= 8))
+    )
     low = (lane & R) == 0
     g_hi = jnp.where(low, s, pltpu.roll(s, R, 1))
     g_lo = jnp.where(low, pltpu.roll(s, LANES - R, 1) + e, s + pltpu.roll(e, R, 1))
     g_hi, g_lo = quick_sum(g_hi, g_lo)
 
-    def reduced(p, e, axis, steps):
-        for step in steps:
-            p, miss = two_sum(p, pltpu.roll(p, step, axis))
-            e = (e + pltpu.roll(e, step, axis)) + miss
-        return quick_sum(p, e)
-
-    def product(a, b):
-        p, e = two_prod(a[0], b[0])
+    def column(x, j):
+        x = jnp.where(lane // (2 * R) == j, x, 0.0)
+        for step in (64, 32, 16):
+            x = x + pltpu.roll(x, step, 1)
+        return x
+
+    grams = [(column(g_hi, j), column(g_lo, j)) for j in range(VECS)]
+    gram_splits = [split(g[0]) for g in grams]
+
+    def product(a, b, a_split, b_split):
+        p = a[0] * b[0]
+        (ah, al), (bh, bl) = a_split, b_split
+        e = (((ah * bh - p) + ah * bl) + al * bh) + al * bl
         return p, e + (a[0] * b[1] + a[1] * b[0])
-
-    def image_of(p, axis):
-        step = 1 if axis == 0 else 2 * R
-        s, miss = two_sum(SHIFT * p[0], pltpu.roll(p[0], step, axis))
-        return quick_sum(s, (SHIFT * p[1] + pltpu.roll(p[1], step, axis)) + miss)
 
     def minus(a, factor, b):
         p, e = two_prod(factor, b[0])
         s, miss = two_sum(a[0], -p)
         return quick_sum(s, (a[1] - (e + factor * b[1])) + miss)
 
-    def ratio(p_row, top, bottom):
-        y = reduced(*product((g_hi, g_lo), p_row), 1, (16, 32, 64))
-        a = reduced(*product(top, y), 0, (4, 2, 1))
-        b = reduced(*product(bottom, y), 0, (4, 2, 1))
-        return a[0] / b[0]
-
-    row = (jnp.where(lane < 2 * R, 1.0, 0.0), zero)
-    col = (jnp.where(sub == 0, 1.0, 0.0), zero)
-    gained = zero
-    for _ in range(CYCLES):
-        row_image, col_image = image_of(row, 1), image_of(col, 0)
-        alpha = ratio(row, col, col_image)
-        row_half = minus(row, alpha, row_image)
-        col_half = minus(col, alpha, col_image)
-        row_turned, col_turned = image_of(row_half, 1), image_of(col_half, 0)
-        omega = ratio(row_turned, col_half, col_turned)
-        gained = gained + ((alpha / SCALE) * col[0] + (omega / SCALE) * col_half[0])
-        row = minus(row_half, omega, row_turned)
-        col = minus(col_half, omega, col_turned)
-
-    def spread(x, k):
-        return jnp.broadcast_to(x[k : k + 1], (8, LANES))
-
-    r_factor = [spread(col[0], k) for k in range(VECS)]
-    x_factor = [spread(gained, k) for k in range(VECS - 1)]
-    rows, cols = guess_ref.shape[:2]
-    for i in range(rows):
-        for t in range(cols // 8):
-            for h in range(2):
-                c, l = slice(8 * t, 8 * t + 8), slice(h * LANES, (h + 1) * LANES)
-                v = [vec_ref[k, h, i, c] for k in range(VECS)]
-                x, r = x_factor[0] * v[0], r_factor[0] * v[0]
-                for k in range(1, VECS):
-                    r = r + r_factor[k] * v[k]
-                    if k < VECS - 1:
-                        x = x + x_factor[k] * v[k]
-                x_ref[i, c, l] = guess_ref[i, c, l] + x
-                r_ref[i, c, l] = r
+
+    def list_image(p):
+        out = [(SHIFT * p[0][0], SHIFT * p[0][1])]
+        for k in range(1, len(p)):
+            out.append(quick_sum(*plus((SHIFT * p[k][0], SHIFT * p[k][1]), p[k - 1])))
+        return out + [p[-1]]
+
+    def sub_image(p):
+        moved = pltpu.roll(p[0], 1, 0), pltpu.roll(p[1], 1, 0)
+        return quick_sum(*plus((SHIFT * p[0], SHIFT * p[1]), moved))
+
+    def list_minus(a, factor, b):
+        a = a + [(zero, zero)] * (len(b) - len(a))
+        return [minus(x, factor, y) for x, y in zip(a, b)]
+
+    def apply_gram(p):
+        return quick_sum(
+            *total([product(g, x, gs, split(x[0])) for g, gs, x in zip(grams, gram_splits, p)])
+        )
+
+    def dot(a, b):
+        p, e = product(a, b, split(a[0]), split(b[0]))
+        for step in (4, 2, 1):
+            p, e = plus((p, e), (pltpu.roll(p, step, 0), pltpu.roll(e, step, 0)))
+        return quick_sum(p, e)
+
+    as_list = [(zero + 1.0, zero)]
+    as_sub = (jnp.where(sub == 0, 1.0, 0.0), zero)
+    gained = []
+    for cycle in range(CYCLES):
+        list1 = list_image(as_list)
+        list2 = list_image(list1)
+        sub1 = sub_image(as_sub)
+        sub2 = sub_image(sub1)
+        y0, y1, y2 = apply_gram(as_list), apply_gram(list1), apply_gram(list2)
+        m00, m01, m02 = dot(as_sub, y0), dot(sub1, y0), dot(sub2, y0)
+        m11, m12, m22 = dot(sub1, y1), dot(sub2, y1), dot(sub2, y2)
+        alpha = m00[0] / m01[0]
+        along = minus(m01, alpha, minus(plus(m02, m11), alpha, m12))
+        power = minus(m11, alpha, minus((2.0 * m12[0], 2.0 * m12[1]), alpha, m22))
+        omega = along[0] / power[0]
+        if cycle + 1 < CYCLES:
+            half_list = list_minus(as_list, alpha, list1)
+            turn_list = list_minus(list1, alpha, list2)
+            gained = gained + [zero] * (len(half_list) - len(gained))
+            for k, one in enumerate(half_list):
+                gained[k] = gained[k] + (omega / SCALE) * one[0]
+            for k, one in enumerate(as_list):
+                gained[k] = gained[k] + (alpha / SCALE) * one[0]
+            as_list = list_minus(half_list, omega, turn_list)
+            as_sub = minus(minus(as_sub, alpha, sub1), omega, minus(sub1, alpha, sub2))
+
+    def combine(i, t, h):
+        at = slice(8 * t, 8 * t + 8)
+        out = as_list[0][0] * f_ref[1, h, i, at]
+        for k in range(1, len(as_list)):
+            out = out + as_list[k][0] * f_ref[k + 1, h, i, at]
+        return out
+
+    def grid(reach, make):
+        out = {}
+        for i in range(DEPTH - reach, DEPTH + rows + reach):
+            shown = tiles_within(reach - reach_of(i, rows), cols)
+            row = make(i, shown)
+            out[i] = [[row.get((h, t), zero) for t in range(tiles)] for h in range(2)]
+        return out
+
+    residual = grid(
+        2, lambda i, shown: {(h, t): combine(i, t, h) for h in range(2) for t in shown}
+    )
+
+    def image_row(values, i, shown):
+        return stencil_row(values[i - 1], values[i], values[i + 1], coef_ref, i - 1, shown)
+
+    def half_row(i, shown):
+        images = image_row(residual, i, shown)
+        return {(h, t): residual[i][h][t] - alpha * image for (h, t), image in images.items()}
+
+    half = grid(1, half_row)
+    for i in range(DEPTH, DEPTH + rows):
+        own = range(HALO // 8, (HALO + cols) // 8)
+        for (h, t), turned in image_row(half, i, own).items():
+            at = slice(8 * t, 8 * t + 8)
+            out = (i - DEPTH, slice(8 * t - HALO, 8 * t - HALO + 8), slice(h * LANES, (h + 1) * LANES))
+            x = gained[0] * f_ref[1, h, i, at]
+            for k in range(1, len(gained)):
+                x = x + gained[k] * f_ref[k + 1, h, i, at]
+            x = (f_ref[0, h, i, at] + x) + (alpha / SCALE) * residual[i][h][t]
+            x_ref[out] = x + (omega / SCALE) * half[i][h][t]
+            r_ref[out] = half[i][h][t] - omega * turned
 
 
 def body(adjoint_guess, velocity, leaf_rate, canopy, solid, receptors):
@@ -412,8 +483,7 @@
     width = cols + 2 * HALO
     win = rows + 2 * DEPTH
     vmem = pl.BlockSpec(memory_space=pltpu.VMEM)
-    smem = pl.BlockSpec(memory_space=pltpu.SMEM)
-    hbm = pl.BlockSpec(memory_space=pl.ANY)
+    hbm = pl.BlockSpec(memory_space=pltpu.HBM)
     payload = pl.pallas_call(
         pack_kernel,
         out_shape=jax.ShapeDtypeStruct((ngx * rows, cols, lanes + 4 * NZ), jnp.float32),
@@ -434,30 +504,32 @@
     left = lax.ppermute(own[:, cols - HALO :], "gy", up)
     right = lax.ppermute(own[:, :HALO], "gy", down)
 
+    total_cols = cols * ngy
+    cells = jnp.stack([receptors // total_cols, receptors % total_cols])
     source_lane = jnp.arange(4 * NZ)[:, None]
     wide_lane = jnp.arange(4 * NZ * R)[None, :]
     spread = (source_lane == wide_lane // R).astype(jnp.bfloat16)
     spread = jnp.concatenate([spread] * 3, axis=0)
-
-    gram, vectors = pl.pallas_call(
+    gram, vectors, coefficients = pl.pallas_call(
         functools.partial(krylov_kernel, rows, cols),
         out_shape=(
             jax.ShapeDtypeStruct((devices * 8, LANES), jnp.float32),
-            jax.ShapeDtypeStruct((VECS, 2, rows, cols, LANES), jnp.float32),
+            jax.ShapeDtypeStruct((DEPTH + 1, 2, win, width, LANES), jnp.float32),
+            jax.ShapeDtypeStruct((7, 2, win - 2, width, LANES), jnp.float32),
         ),
-        in_specs=[smem, vmem, vmem, vmem, vmem],
-        out_specs=(vmem, vmem),
+        in_specs=[pl.BlockSpec(memory_space=pl.ANY), vmem, vmem, vmem, vmem],
+        out_specs=(vmem, vmem, vmem),
         scratch_shapes=[
-            pltpu.VMEM((DEPTH + 1, 2, win, width + 16, LANES), jnp.float32),
-            pltpu.VMEM((7, 2, win - 2, width, LANES), jnp.float32),
             pltpu.VMEM(((win - 2) * width, LANES), jnp.float32),
             pltpu.VMEM(((win - 2) * width, 8 * LANES), jnp.float32),
             pltpu.VMEM((VECS, 2 * rows * cols // 8, 8, LANES), jnp.float32),
             pltpu.VMEM((VECS, 2 * rows * cols // 8, 8, LANES), jnp.float32),
+            pltpu.SMEM((2, R), jnp.int32),
+            pltpu.SemaphoreType.DMA(()),
         ],
         compiler_params=pltpu.CompilerParams(vmem_limit_bytes=40 * 1024 * 1024),
         name="krylov",
-    )(receptors, left, own, right, spread)
+    )(cells, left, own, right, spread)
     everyone = lax.all_to_all(gram, ("gx", "gy"), 0, 0, tiled=True)
     out = jax.ShapeDtypeStruct((rows, cols, lanes), jnp.float32)
     return pl.pallas_call(
@@ -467,7 +539,7 @@
         out_specs=(vmem, vmem),
         compiler_params=pltpu.CompilerParams(vmem_limit_bytes=16 * 1024 * 1024),
         name="finish",
-    )(everyone, adjoint_guess, vectors)
+    )(everyone, vectors, coefficients)
 
 
 def solution(mesh):

time: 48.6 us -> 47.2 us (0.971)
  Pallas kernels: 8.88 us -> 7.55 us
  other arithmetic: 0.16 us -> 0.83 us
  waiting for transfers between devices: 12.5 us -> 11.9 us
    pallas_call x1, Pallas kernels: 2.59 us -> 1.68 us  [body(): pl.pallas_call(finish_kernel, out_shape=(out, out), in_specs=[vmem, vmem,...]
    all_to_all x1, waiting for transfers between devices: 11.7 us -> 10.9 us  [body(): own = lax.all_to_all(payload, 'gx', 0, 0, tiled=True)]
    another operation x0 -> x2, other arithmetic: none -> 0.67 us  [body(): cells = jnp.stack([receptors // total_cols, receptors % total_cols])]
  transfers between devices with their start and end apart: 3 -> 3, of which waited for: 2 -> 2; matrix products, arithmetic and copies ran while one was open for 0% -> 2% of each run, Pallas kernels for 0% -> 0%
where the time goes in v4:
time: 47.2 us; the launch traced here: 46.9 us
  blocking collectives  15.3 us (32%)
  waiting for transfers between devices  11.9 us (25%)
  starting transfers between devices  10.7 us (23%)
  Pallas kernels  7.55 us (16%)
  other arithmetic  0.83 us (2%)
  between operations  0.69 us (1%)
    all_to_all x1, blocking collectives, body(): everyone = lax.all_to_all(gram, ('gx', 'gy'), 0, 0, tiled=True)  15.3 us
    all_to_all x1, waiting for transfers between devices, body(): own = lax.all_to_all(payload, 'gx', 0, 0, tiled=True)  10.9 us
    all_to_all x1, starting transfers between devices, body(): own = lax.all_to_all(payload, 'gx', 0, 0, tiled=True)  6.33 us
    pallas_call x1, Pallas kernels, body(): pl.pallas_call(functools.partial(krylov_kernel, rows, cols), out_shape=(j...  4.04 us
    ppermute x1, starting transfers between devices, body(): left = lax.ppermute(own[:, cols - HALO:], 'gy', up)  3.04 us
    pallas_call x1, Pallas kernels, body(): pl.pallas_call(pack_kernel, out_shape=jax.ShapeDtypeStruct((ngx * rows, c...  1.83 us
    pallas_call x1, Pallas kernels, body(): pl.pallas_call(finish_kernel, out_shape=(out, out), in_specs=[vmem, vmem,...  1.68 us
    ppermute x1, starting transfers between devices, body(): right = lax.ppermute(own[:, :HALO], 'gy', down)  1.29 us
  transfers between devices with their start and end apart: 3, of which 2 were waited for; matrix products, arithmetic and copies ran while one was open for 2% of the time, Pallas kernels for 0%

profile of v4, /device:TPU:0, one launch (start us, length us, event | category | flops | bytes accessed | tf_op | source)
XLA Modules:
  0.0 46.9 jit_solution(17510663705103944015)
XLA Ops:
  0.6 1.8 %pack.1 = f32[16,16,384]{2,1,0:T(8,128)} custom-call(f32[4,16,256]{2,1,0:T(8,128)} %guess_ref.1, f32[3,4,512]{2,1,0:T(4,128)} %velocity_ref.1, f32[4,512]{1,0:T(4,128)} %leaf_ref.1, s32[4,512]{1,0:T(4,128)} %canopy_ref.1, s32[4,512]{1,0:T(4,128)} %solid_ref.1), custom_call_target="tpu_custom_call" | custom-call | tf_op jit(solution)/shard_map/pack/pallas_call | solution.py:487
  2.5 6.3 %all-to-all-start = ((f32[16,16,384]{2,1,0:T(8,128)}), f32[16,16,384]{2,1,0:T(8,128)S(1)}, u32[]{:S(2)}, u32[]{:S(2)}) async-start(f32[16,16,384]{2,1,0:T(8,128)} %pack.1), calls=%async_computation | async-start | bytes 786432 | tf_op jit(solution)/shard_map/all_to_all | solution.py:501
  8.8 0.7 %fusion.4 = (s32[1,8]{1,0:T(1,128)S(1)}, s32[1,8]{1,0:T(1,128)S(1)}) fusion(s32[8]{0:T(128)} %param.11), kind=kLoop, calls=%fused_computation.16 | loop fusion | flops 152 | bytes 96 | tf_op jit(solution)/shard_map/stack | solution.py:508
  9.5 0.1 iota_compare_fusion
  9.5 10.9 %all-to-all-done.own_ref = f32[16,16,384]{2,1,0:T(8,128)S(1)} async-done(((f32[16,16,384]{2,1,0:T(8,128)}), f32[16,16,384]{2,1,0:T(8,128)S(1)}, u32[]{:S(2)}, u32[]{:S(2)}) %all-to-all-start) | async-done | bytes 393248 | tf_op jit(solution)/shard_map/all_to_all | solution.py:501
  20.5 1.3 %collective-permute-start.1 = (f32[16,8,384]{2,1,0:T(8,128)S(1)}, f32[16,8,384]{2,1,0:T(8,128)S(1)}, u32[]{:S(2)}, u32[]{:S(2)}) collective-permute-start(f32[16,8,384]{2,1,0:T(8,128)S(1)} %get-tuple-element.8), channel_id=1, source_target_pairs={{1,0},{2,1},{3,2},{4,3},{5,4},{6,5},{7,6},{9,8},{10,9},{11,10},{12... | collective-permute-start | bytes 589832 | tf_op jit(solution)/shard_map/ppermute | solution.py:505
  21.8 3.0 %collective-permute-start = (f32[16,8,384]{2,1,0:T(8,128)S(1)}, f32[16,8,384]{2,1,0:T(8,128)S(1)}, u32[]{:S(2)}, u32[]{:S(2)}) collective-permute-start(f32[16,8,384]{2,1,0:T(8,128)S(1)} %get-tuple-element.9), channel_id=1, source_target_pairs={{0,1},{1,2},{2,3},{3,4},{4,5},{5,6},{6,7},{8,9},{9,10},{10,11},{11... | collective-permute-start | bytes 589832 | tf_op jit(solution)/shard_map/ppermute | solution.py:504
  24.9 0.1 add_convert_fusion.ex_ref
  25.0 0.0 collective-permute-done.1.right_ref
  25.0 0.9 %collective-permute-done.left_ref = f32[16,8,384]{2,1,0:T(8,128)S(1)} collective-permute-done((f32[16,8,384]{2,1,0:T(8,128)S(1)}, f32[16,8,384]{2,1,0:T(8,128)S(1)}, u32[]{:S(2)}, u32[]{:S(2)}) %collective-permute-start) | collective-permute-done | bytes 196640 | tf_op jit(solution)/shard_map/ppermute | solution.py:504
  25.9 4.0 %krylov.1 = (f32[256,128]{1,0:T(8,128)S(1)}, f32[8,2,18,32,128]{4,3,2,1,0:T(8,128)S(1)}, f32[7,2,16,32,128]{4,3,2,1,0:T(8,128)S(1)}) custom-call(s32[2,8]{1,0:T(2,128)S(1)} %pad_add_fusion.rec_ref, f32[16,8,384]{2,1,0:T(8,128)S(1)} %collective-permute-done.left_ref, f32[16,16,384]{2,1,0:T(8,128)S(1)} %all-to-all-done.own_ref, ...), custom_call_target="tpu_custom_call" | custom-call | tf_op jit(solution)/shard_map/krylov/pallas_call | solution.py:513
  29.9 15.3 %all_to_all.16 = f32[32,8,128]{2,1,0:T(8,128)S(1)} all-to-all(f32[32,8,128]{2,1,0:T(8,128)S(1)} %bitcast.7), channel_id=1, replica_groups=mesh['gx'=4,'gy'=8] {'gx','gy'}, dimensions={0} | all-to-all | bytes 262144 | tf_op jit(solution)/shard_map/all_to_all | solution.py:533
  45.2 1.7 %finish.1 = (f32[4,16,256]{2,1,0:T(8,128)}, f32[4,16,256]{2,1,0:T(8,128)}) custom-call(f32[256,128]{1,0:T(8,128)S(1)} %bitcast.6, f32[8,2,18,32,128]{4,3,2,1,0:T(8,128)S(1)} %get-tuple-element.6.f_ref, f32[7,2,16,32,128]{4,3,2,1,0:T(8,128)S(1)} %get-tuple-element.7.coef_ref), custom_call_target="tpu_custom_call" | custom-call | tf_op jit(solution)/shard_map/finish/pallas_call | solution.py:535
  (3 shorter events, 0.0 us)
Async XLA Ops:
  2.5 18.0 %all-to-all-start = ((f32[16,16,384]{2,1,0:T(8,128)}), f32[16,16,384]{2,1,0:T(8,128)S(1)}, u32[]{:S(2)}, u32[]{:S(2)}) async-start(f32[16,16,384]{2,1,0:T(8,128)} %pack.1), calls=%async_computation | async-start | bytes 786432 | tf_op jit(solution)/shard_map/all_to_all | solution.py:501
  20.5 4.5 %collective-permute-start.1 = (f32[16,8,384]{2,1,0:T(8,128)S(1)}, f32[16,8,384]{2,1,0:T(8,128)S(1)}, u32[]{:S(2)}, u32[]{:S(2)}) collective-permute-start(f32[16,8,384]{2,1,0:T(8,128)S(1)} %get-tuple-element.8), channel_id=1, source_target_pairs={{1,0},{2,1},{3,2},{4,3},{5,4},{6,5},{7,6},{9,8},{10,9},{11,10},{12... | collective-permute-start | bytes 589832 | tf_op jit(solution)/shard_map/ppermute | solution.py:505
  21.8 4.1 %collective-permute-start = (f32[16,8,384]{2,1,0:T(8,128)S(1)}, f32[16,8,384]{2,1,0:T(8,128)S(1)}, u32[]{:S(2)}, u32[]{:S(2)}) collective-permute-start(f32[16,8,384]{2,1,0:T(8,128)S(1)} %get-tuple-element.9), channel_id=1, source_target_pairs={{0,1},{1,2},{2,3},{3,4},{4,5},{5,6},{6,7},{8,9},{9,10},{10,11},{11... | collective-permute-start | bytes 589832 | tf_op jit(solution)/shard_map/ppermute | solution.py:504

commit v5 on v4

--- a/solution.py
+++ b/solution.py
@@ -51,7 +51,7 @@
 
 
 def pack_kernel(
-    guess_ref, velocity_ref, leaf_ref, canopy_ref, solid_ref, out_ref,
+    guess_ref, velocity_ref, leaf_ref, canopy_ref, solid_ref, out_ref, far_ref,
     v_ref, l_ref, c_ref, s_ref, sem,
 ):
     copies = [
@@ -59,16 +59,13 @@
         pltpu.make_async_copy(leaf_ref, l_ref, sem.at[1]),
         pltpu.make_async_copy(canopy_ref, c_ref, sem.at[2]),
         pltpu.make_async_copy(solid_ref, s_ref, sem.at[3]),
+        pltpu.make_async_copy(guess_ref, out_ref.at[:, :, pl.ds(0, NZ * R)], sem.at[4]),
     ]
-    rows, cols = guess_ref.shape[:2]
-    times = out_ref.shape[0] // rows
-    for n in range(times):
-        place = out_ref.at[pl.ds(n * rows, rows), :, pl.ds(0, NZ * R)]
-        copies.append(pltpu.make_async_copy(guess_ref, place, sem.at[4 + n]))
     for copy in copies:
         copy.start()
     for copy in copies[:4]:
         copy.wait()
+    rows, cols = guess_ref.shape[:2]
     lane = lax.broadcasted_iota(jnp.int32, (8, LANES), 1)
     sub = lax.broadcasted_iota(jnp.int32, (8, LANES), 0)
     reaction = penalty * s_ref[...].astype(jnp.float32) + leaf_gain * l_ref[...] * c_ref[
@@ -99,10 +96,30 @@
                 else:
                     here = (lane // NZ - sub) % 4 == d
                     whole = jnp.where(here, pltpu.roll(mixed, NZ * d, 1), whole)
-            for n in range(times):
-                out_ref[n * rows + x, 8 * t : 8 * t + 8, NZ * R :] = whole
-    for copy in copies[4:]:
-        copy.wait()
+            out_ref[x, 8 * t : 8 * t + 8, NZ * R :] = whole
+    copies[4].wait()
+    count = far_ref.shape[0]
+    first = jnp.where(lax.axis_index("gx") % 4 < 2, rows - count, 0)
+    for x in range(count):
+        far_ref[x] = out_ref[first + x]
+
+
+def window_row(i, rows, a, own, even, odd, far, farther):
+    at = i - DEPTH
+    if 0 <= at < rows:
+        return own(at)
+    if -rows <= at < 0:
+        return jnp.where(a % 2 == 1, even(at + rows), odd(at + rows))
+    if rows <= at < 2 * rows:
+        return jnp.where(a % 2 == 1, odd(at - rows), even(at - rows))
+    if at < 0:
+        return jnp.where(a % 4 >= 2, far(at + DEPTH), farther(at + DEPTH))
+    return jnp.where(a % 4 >= 2, farther(at - 2 * rows), far(at - 2 * rows))
+
+
+def edge_start(a, rows, total_rows, count):
+    first = jnp.maximum(DEPTH - a * rows, 1)
+    return jnp.minimum(first, rows + 2 * DEPTH - 1 - count)
 
 
 def reach_of(i, rows):
@@ -144,7 +161,8 @@
 
 
 def krylov_kernel(
-    rows, cols, rec_ref, left_ref, own_ref, right_ref, ex_ref, gram_ref, f_ref, coef_ref,
+    rows, cols, rec_ref, outer_ref, inner_ref, own_ref, pair_ref, across_ref, far_ref, farther_ref,
+    ex_ref, gram_ref, f_ref, coef_ref,
     raw_ref, wide_ref, hi_ref, lo_ref, cell_ref, cell_sem,
 ):
     fetch = pltpu.make_async_copy(rec_ref, cell_ref, cell_sem)
@@ -153,7 +171,11 @@
     crows = win - 2
     width = cols + 2 * HALO
     tiles = width // 8
-    total_rows = left_ref.shape[0]
+    total_rows = rows * lax.axis_size("gx")
+    edge_rows = outer_ref.shape[0]
+    edge_row0 = edge_start(lax.axis_index("gx"), rows, total_rows, edge_rows)
+    place = lax.axis_index("gx")
+    odd = lax.axis_index("gy") % 2 == 1
     total_cols = cols * lax.axis_size("gy")
     row0 = lax.axis_index("gx") * rows - DEPTH
     col0 = lax.axis_index("gy") * cols - HALO
@@ -163,26 +185,32 @@
     def inside_row(i):
         at = row0 + i
         ok = jnp.logical_and(at >= 0, at < total_rows)
-        return jnp.where(ok, 1.0, 0.0), jnp.clip(at, 0, total_rows - 1)
-
-    def parts(at, lo):
+        return jnp.where(ok, 1.0, 0.0)
+
+    def parts(i, lo):
+        at_edge = jnp.clip(i - edge_row0, 0, edge_rows - 1)
+        outer = outer_ref[at_edge, :, lo : lo + LANES]
+        inner = inner_ref[at_edge, :, lo : lo + LANES]
+        blocks = [
+            lambda x, ref=ref: ref[x, :, lo : lo + LANES]
+            for ref in (own_ref, pair_ref, across_ref, far_ref, farther_ref)
+        ]
         return (
-            left_ref[at, :, lo : lo + LANES],
-            own_ref[at, :, lo : lo + LANES],
-            right_ref[at, :, lo : lo + LANES],
+            jnp.where(odd, inner, outer),
+            window_row(i, rows, place, *blocks),
+            jnp.where(odd, outer, inner),
         )
 
     spans = ((0, HALO), (HALO, HALO + cols), (HALO + cols, width))
 
     for i in range(win):
-        ok, at = inside_row(i)
+        ok = inside_row(i)
         for h in range(2):
-            for (c0, c1), piece in zip(spans, parts(at, h * LANES)):
+            for (c0, c1), piece in zip(spans, parts(i, h * LANES)):
                 f_ref[0, h, i, c0:c1] = piece * ok
 
     for i in range(crows):
-        _, at = inside_row(i + 1)
-        for (c0, c1), piece in zip(spans, parts(at, 2 * LANES)):
+        for (c0, c1), piece in zip(spans, parts(i + 1, 2 * LANES)):
             raw_ref[i * width + c0 : i * width + c1, :] = piece
 
     raw = raw_ref[...]
@@ -197,7 +225,7 @@
     )
 
     for i in range(crows):
-        ok, _ = inside_row(i + 1)
+        ok = inside_row(i + 1)
         for t in tiles_within(DEPTH - 1 - reach_of(i + 1, rows), cols):
             at = i * width + 8 * t
             at_col = col0 + 8 * t + sub
@@ -484,25 +512,56 @@
     win = rows + 2 * DEPTH
     vmem = pl.BlockSpec(memory_space=pltpu.VMEM)
     hbm = pl.BlockSpec(memory_space=pltpu.HBM)
-    payload = pl.pallas_call(
+    wide = lanes + 4 * NZ
+    own, far_rows = pl.pallas_call(
         pack_kernel,
-        out_shape=jax.ShapeDtypeStruct((ngx * rows, cols, lanes + 4 * NZ), jnp.float32),
+        out_shape=(
+            pltpu.VMEM((rows, cols, wide), jnp.float32),
+            pltpu.VMEM((DEPTH - rows, cols, wide), jnp.float32),
+        ),
         in_specs=[hbm] * 5,
-        out_specs=vmem,
+        out_specs=(vmem, vmem),
         scratch_shapes=[
             pltpu.VMEM(velocity.shape, jnp.float32),
             pltpu.VMEM(leaf_rate.shape, jnp.float32),
             pltpu.VMEM(canopy.shape, jnp.int32),
             pltpu.VMEM(solid.shape, jnp.int32),
-            pltpu.SemaphoreType.DMA((4 + ngx,)),
+            pltpu.SemaphoreType.DMA((5,)),
         ],
+        compiler_params=pltpu.CompilerParams(vmem_limit_bytes=56 * 1024 * 1024),
         name="pack",
     )(adjoint_guess, velocity, leaf_rate, canopy, solid)
-    own = lax.all_to_all(payload, "gx", 0, 0, tiled=True)
-    up = [(j, j + 1) for j in range(ngy - 1)]
-    down = [(j + 1, j) for j in range(ngy - 1)]
-    left = lax.ppermute(own[:, cols - HALO :], "gy", up)
-    right = lax.ppermute(own[:, :HALO], "gy", down)
+    def swap(x, axis, pairs):
+        return lax.ppermute(x, axis, pairs + [(j, i) for i, j in pairs])
+
+    place = lax.axis_index("gx")
+    far = swap(far_rows, "gx", [(j, j + 2) for j in range(ngx - 2) if j % 4 < 2])
+    pair = swap(own, "gx", [(j, j + 1) for j in range(0, ngx - 1, 2)])
+    across = swap(own, "gx", [(j, j + 1) for j in range(1, ngx - 1, 2)])
+    if ngx > 4:
+        other = jnp.where(place % 4 < 2, own[: DEPTH - rows], own[2 * rows - DEPTH :])
+        farther = swap(other, "gx", [(j, j + 2) for j in range(ngx - 2) if j % 4 >= 2])
+    else:
+        farther = jnp.zeros_like(far_rows)
+
+    spans = [
+        (max(0, a * rows - DEPTH + 1), min(ngx * rows, (a + 1) * rows + DEPTH - 1))
+        for a in range(ngx)
+    ]
+    count = max(hi - lo for lo, hi in spans)
+    odd = lax.axis_index("gy") % 2 == 1
+
+    def edges(left):
+        blocks = [
+            lambda x, block=jnp.where(left, b[:, :HALO], b[:, cols - HALO :]): block[x]
+            for b in (own, pair, across, far, farther)
+        ]
+        whole = [window_row(i, rows, place, *blocks) for i in range(1, rows + 2 * DEPTH - 1)]
+        first = edge_start(place, rows, ngx * rows, count) - 1
+        return lax.dynamic_slice_in_dim(jnp.stack(whole), first, count, 0)
+
+    outer = swap(edges(~odd), "gy", [(j, j + 1) for j in range(1, ngy - 1, 2)])
+    inner = swap(edges(odd), "gy", [(j, j + 1) for j in range(0, ngy - 1, 2)])
 
     total_cols = cols * ngy
     cells = jnp.stack([receptors // total_cols, receptors % total_cols])
@@ -517,7 +576,7 @@
             jax.ShapeDtypeStruct((DEPTH + 1, 2, win, width, LANES), jnp.float32),
             jax.ShapeDtypeStruct((7, 2, win - 2, width, LANES), jnp.float32),
         ),
-        in_specs=[pl.BlockSpec(memory_space=pl.ANY), vmem, vmem, vmem, vmem],
+        in_specs=[pl.BlockSpec(memory_space=pl.ANY)] + [vmem] * 8,
         out_specs=(vmem, vmem, vmem),
         scratch_shapes=[
             pltpu.VMEM(((win - 2) * width, LANES), jnp.float32),
@@ -529,7 +588,7 @@
         ],
         compiler_params=pltpu.CompilerParams(vmem_limit_bytes=40 * 1024 * 1024),
         name="krylov",
-    )(cells, left, own, right, spread)
+    )(cells, outer, inner, own, pair, across, far, farther, spread)
     everyone = lax.all_to_all(gram, ("gx", "gy"), 0, 0, tiled=True)
     out = jax.ShapeDtypeStruct((rows, cols, lanes), jnp.float32)
     return pl.pallas_call(

time: 47.2 us -> 40.7 us (0.86)
  waiting for transfers between devices: 11.9 us -> 6.17 us
  Pallas kernels: 7.55 us -> 6.83 us
  starting transfers between devices: 10.7 us -> 10.2 us
    all_to_all x1 -> x0, waiting for transfers between devices: 10.9 us -> none  [body(): own = lax.all_to_all(payload, 'gx', 0, 0, tiled=True)]
    all_to_all x1 -> x0, starting transfers between devices: 6.33 us -> none  [body(): own = lax.all_to_all(payload, 'gx', 0, 0, tiled=True)]
    ppermute x2 -> x5, starting transfers between devices: 4.33 us -> 10.2 us  [swap(): return lax.ppermute(x, axis, pairs + [(j, i) for i, j in pairs])]
    ppermute x2 -> x5, waiting for transfers between devices: 0.93 us -> 6.17 us  [swap(): return lax.ppermute(x, axis, pairs + [(j, i) for i, j in pairs])]
    pallas_call x1, Pallas kernels: 1.83 us -> 0.96 us  [body(): pl.pallas_call(pack_kernel, out_shape=(pltpu.VMEM((rows, cols, wide), jnp...]
  transfers between devices with their start and end apart: 3 -> 5, of which waited for: 2 -> 2; matrix products, arithmetic and copies ran while one was open for 2% -> 2% of each run, Pallas kernels for 0% -> 0%
where the time goes in v5:
time: 40.7 us; the launch traced here: 40.5 us
  blocking collectives  15.4 us (38%)
  starting transfers between devices  10.2 us (25%)
  Pallas kernels  6.83 us (17%)
  waiting for transfers between devices  6.17 us (15%)
  other arithmetic  1.03 us (3%)
  between operations  0.92 us (2%)
    all_to_all x1, blocking collectives, body(): everyone = lax.all_to_all(gram, ('gx', 'gy'), 0, 0, tiled=True)  15.4 us
    ppermute x5, starting transfers between devices, swap(): return lax.ppermute(x, axis, pairs + [(j, i) for i, j in pairs])  10.2 us
    ppermute x5, waiting for transfers between devices, swap(): return lax.ppermute(x, axis, pairs + [(j, i) for i, j in pairs])  6.17 us
    pallas_call x1, Pallas kernels, body(): pl.pallas_call(functools.partial(krylov_kernel, rows, cols), out_shape=(j...  4.17 us
    pallas_call x1, Pallas kernels, body(): pl.pallas_call(finish_kernel, out_shape=(out, out), in_specs=[vmem, vmem,...  1.71 us
    pallas_call x1, Pallas kernels, body(): pl.pallas_call(pack_kernel, out_shape=(pltpu.VMEM((rows, cols, wide), jnp...  0.96 us
  transfers between devices with their start and end apart: 5, of which 2 were waited for; matrix products, arithmetic and copies ran while one was open for 2% of the time, Pallas kernels for 0%

profile of v5, /device:TPU:0, one launch (start us, length us, event | category | flops | bytes accessed | tf_op | source)
XLA Modules:
  0.0 40.5 jit_solution(18088137799717558827)
XLA Ops:
  0.6 1.0 %pack.1 = (f32[4,16,384]{2,1,0:T(8,128)S(1)}, f32[3,16,384]{2,1,0:T(8,128)S(1)}) custom-call(f32[4,16,256]{2,1,0:T(8,128)} %guess_ref.1, f32[3,4,512]{2,1,0:T(4,128)} %velocity_ref.1, f32[4,512]{1,0:T(4,128)} %leaf_ref.1, s32[4,512]{1,0:T(4,128)} %canopy_ref.1, s32[4,512]{1,0:T(4,128)} %solid_ref.1), custom_call_target="tpu_custom_call" | custom-call | tf_op jit(solution)/shard_map/pack/pallas_call | solution.py:516
  1.6 0.7 %collective-permute-start.2 = (f32[4,16,384]{2,1,0:T(8,128)S(1)}, f32[4,16,384]{2,1,0:T(8,128)S(1)}, u32[]{:S(2)}, u32[]{:S(2)}) collective-permute-start(f32[4,16,384]{2,1,0:T(8,128)S(1)} %get-tuple-element.8.own_ref), channel_id=1, source_target_pairs={{8,16},{16,8},{9,17},{17,9},{10,18},{18,10},{11,19},{19,11},{12,20... | collective-permute-start | bytes 294920 | tf_op jit(solution)/shard_map/ppermute | solution.py:535
  2.3 5.9 %collective-permute-start.1 = (f32[4,16,384]{2,1,0:T(8,128)S(1)}, f32[4,16,384]{2,1,0:T(8,128)S(1)}, u32[]{:S(2)}, u32[]{:S(2)}) collective-permute-start(f32[4,16,384]{2,1,0:T(8,128)S(1)} %get-tuple-element.8.own_ref), channel_id=1, source_target_pairs={{0,8},{16,24},{8,0},{24,16},{1,9},{17,25},{9,1},{25,17},{2,10},{18... | collective-permute-start | bytes 294920 | tf_op jit(solution)/shard_map/ppermute | solution.py:535
  8.2 0.0 collective-permute-start
  8.2 0.1 iota_compare_fusion
  8.3 0.7 %fusion.4 = (s32[1,8]{1,0:T(1,128)S(1)}, s32[1,8]{1,0:T(1,128)S(1)}) fusion(s32[8]{0:T(128)} %param.11), kind=kLoop, calls=%fused_computation.54 | loop fusion | flops 152 | bytes 96 | tf_op jit(solution)/shard_map/stack | solution.py:567
  8.9 5.2 %collective-permute-done.far_ref = f32[3,16,384]{2,1,0:T(8,128)S(1)} collective-permute-done((f32[3,16,384]{2,1,0:T(8,128)S(1)}, f32[3,16,384]{2,1,0:T(8,128)S(1)}, u32[]{:S(2)}, u32[]{:S(2)}) %collective-permute-start) | collective-permute-done | bytes 73760 | tf_op jit(solution)/shard_map/ppermute | solution.py:535
  14.2 0.0 collective-permute-done.2.across_ref
  14.3 0.0 collective-permute-done.1.pair_ref
  14.6 0.7 %collective-permute-start.3 = (f32[14,8,384]{2,1,0:T(8,128)S(1)}, f32[14,8,384]{2,1,0:T(8,128)S(1)}, u32[]{:S(2)}, u32[]{:S(2)}) collective-permute-start(f32[14,8,384]{2,1,0:T(8,128)S(1)} %constant_dynamic-slice_fusion.1), channel_id=1, source_target_pairs={{1,2},{3,4},{5,6},{2,1},{4,3},{6,5},{9,10},{11,12},{13,14},{10,9},... | collective-permute-start | bytes 516104 | tf_op jit(solution)/shard_map/ppermute | solution.py:535
  15.3 2.9 %collective-permute-start.4 = (f32[14,8,384]{2,1,0:T(8,128)S(1)}, f32[14,8,384]{2,1,0:T(8,128)S(1)}, u32[]{:S(2)}, u32[]{:S(2)}) collective-permute-start(f32[14,8,384]{2,1,0:T(8,128)S(1)} %constant_dynamic-slice_fusion), channel_id=1, source_target_pairs={{0,1},{2,3},{4,5},{6,7},{1,0},{3,2},{5,4},{7,6},{8,9},{10,11},{12,... | collective-permute-start | bytes 516104 | tf_op jit(solution)/shard_map/ppermute | solution.py:535
  18.2 0.1 add_convert_fusion.ex_ref
  18.3 0.0 collective-permute-done.3.outer_ref
  18.3 0.9 %collective-permute-done.4.inner_ref = f32[14,8,384]{2,1,0:T(8,128)S(1)} collective-permute-done((f32[14,8,384]{2,1,0:T(8,128)S(1)}, f32[14,8,384]{2,1,0:T(8,128)S(1)}, u32[]{:S(2)}, u32[]{:S(2)}) %collective-permute-start.4) | collective-permute-done | bytes 172064 | tf_op jit(solution)/shard_map/ppermute | solution.py:535
  19.3 4.2 %krylov.1 = (f32[256,128]{1,0:T(8,128)S(1)}, f32[8,2,18,32,128]{4,3,2,1,0:T(8,128)S(1)}, f32[7,2,16,32,128]{4,3,2,1,0:T(8,128)S(1)}) custom-call(s32[2,8]{1,0:T(2,128)S(1)} %pad_add_fusion.rec_ref, f32[14,8,384]{2,1,0:T(8,128)S(1)} %collective-permute-done.3.outer_ref, f32[14,8,384]{2,1,0:T(8,128)S(1)} %collective-permute-done.4.inner_ref, ...), custom_call_target="tpu_custom_call" | custom-call | tf_op jit(solution)/shard_map/krylov/pallas_call | solution.py:572
  23.4 15.4 %all_to_all.11 = f32[32,8,128]{2,1,0:T(8,128)S(1)} all-to-all(f32[32,8,128]{2,1,0:T(8,128)S(1)} %bitcast.7), channel_id=1, replica_groups=mesh['gx'=4,'gy'=8] {'gx','gy'}, dimensions={0} | all-to-all | bytes 262144 | tf_op jit(solution)/shard_map/all_to_all | solution.py:592
  38.8 1.7 %finish.1 = (f32[4,16,256]{2,1,0:T(8,128)}, f32[4,16,256]{2,1,0:T(8,128)}) custom-call(f32[256,128]{1,0:T(8,128)S(1)} %bitcast.6, f32[8,2,18,32,128]{4,3,2,1,0:T(8,128)S(1)} %get-tuple-element.10.f_ref, f32[7,2,16,32,128]{4,3,2,1,0:T(8,128)S(1)} %get-tuple-element.11.coef_ref), custom_call_target="tpu_custom_call" | custom-call | tf_op jit(solution)/shard_map/finish/pallas_call | solution.py:594
  (32 shorter events, 0.2 us)
Async XLA Ops:
  1.6 12.6 %collective-permute-start.2 = (f32[4,16,384]{2,1,0:T(8,128)S(1)}, f32[4,16,384]{2,1,0:T(8,128)S(1)}, u32[]{:S(2)}, u32[]{:S(2)}) collective-permute-start(f32[4,16,384]{2,1,0:T(8,128)S(1)} %get-tuple-element.8.own_ref), channel_id=1, source_target_pairs={{8,16},{16,8},{9,17},{17,9},{10,18},{18,10},{11,19},{19,11},{12,20... | collective-permute-start | bytes 294920 | tf_op jit(solution)/shard_map/ppermute | solution.py:535
  2.3 12.0 %collective-permute-start.1 = (f32[4,16,384]{2,1,0:T(8,128)S(1)}, f32[4,16,384]{2,1,0:T(8,128)S(1)}, u32[]{:S(2)}, u32[]{:S(2)}) collective-permute-start(f32[4,16,384]{2,1,0:T(8,128)S(1)} %get-tuple-element.8.own_ref), channel_id=1, source_target_pairs={{0,8},{16,24},{8,0},{24,16},{1,9},{17,25},{9,1},{25,17},{2,10},{18... | collective-permute-start | bytes 294920 | tf_op jit(solution)/shard_map/ppermute | solution.py:535
  8.2 6.0 %collective-permute-start = (f32[3,16,384]{2,1,0:T(8,128)S(1)}, f32[3,16,384]{2,1,0:T(8,128)S(1)}, u32[]{:S(2)}, u32[]{:S(2)}) collective-permute-start(f32[3,16,384]{2,1,0:T(8,128)S(1)} %get-tuple-element.7), channel_id=1, source_target_pairs={{0,16},{8,24},{16,0},{24,8},{1,17},{9,25},{17,1},{25,9},{2,18},{10... | collective-permute-start | bytes 221192 | tf_op jit(solution)/shard_map/ppermute | solution.py:535
  14.6 3.7 %collective-permute-start.3 = (f32[14,8,384]{2,1,0:T(8,128)S(1)}, f32[14,8,384]{2,1,0:T(8,128)S(1)}, u32[]{:S(2)}, u32[]{:S(2)}) collective-permute-start(f32[14,8,384]{2,1,0:T(8,128)S(1)} %constant_dynamic-slice_fusion.1), channel_id=1, source_target_pairs={{1,2},{3,4},{5,6},{2,1},{4,3},{6,5},{9,10},{11,12},{13,14},{10,9},... | collective-permute-start | bytes 516104 | tf_op jit(solution)/shard_map/ppermute | solution.py:535
  15.3 3.9 %collective-permute-start.4 = (f32[14,8,384]{2,1,0:T(8,128)S(1)}, f32[14,8,384]{2,1,0:T(8,128)S(1)}, u32[]{:S(2)}, u32[]{:S(2)}) collective-permute-start(f32[14,8,384]{2,1,0:T(8,128)S(1)} %constant_dynamic-slice_fusion), channel_id=1, source_target_pairs={{0,1},{2,3},{4,5},{6,7},{1,0},{3,2},{5,4},{7,6},{8,9},{10,11},{12,... | collective-permute-start | bytes 516104 | tf_op jit(solution)/shard_map/ppermute | solution.py:535

commit v6 on v5

--- a/solution.py
+++ b/solution.py
@@ -117,9 +117,34 @@
     return jnp.where(a % 4 >= 2, farther(at - 2 * rows), far(at - 2 * rows))
 
 
-def edge_start(a, rows, total_rows, count):
-    first = jnp.maximum(DEPTH - a * rows, 1)
-    return jnp.minimum(first, rows + 2 * DEPTH - 1 - count)
+def edges_kernel(
+    own_ref, pair_ref, across_ref, far_ref, farther_ref, outer_ref, inner_ref
+):
+    rows, cols, wide = own_ref.shape
+    place = lax.axis_index("gx")
+    odd = lax.axis_index("gy") % 2 == 1
+    sub = lax.broadcasted_iota(jnp.int32, (8, wide), 0)
+    refs = (own_ref, pair_ref, across_ref, far_ref, farther_ref)
+
+    def edge(right):
+        c0 = cols - HALO if right else 0
+        blocks = [lambda x, ref=ref: ref[x, c0 : c0 + HALO, :] for ref in refs]
+        tiles = [window_row(DEPTH + x, rows, place, *blocks) for x in range(rows)]
+        for start, way in ((DEPTH, -1), (DEPTH + rows - 1, 1)):
+            for d in range(1, DEPTH // 2 + 1):
+                close = window_row(start + way * d, rows, place, *blocks)
+                distant = window_row(start + way * (DEPTH - d), rows, place, *blocks)
+                distant = pltpu.roll(distant, d if right else HALO - d, 0)
+                if right:
+                    kept = sub >= HALO - DEPTH + d
+                else:
+                    kept = sub < DEPTH - d
+                tiles.append(jnp.where(kept, close, distant))
+        return tiles
+
+    for n, (left, right) in enumerate(zip(edge(False), edge(True))):
+        outer_ref[n] = jnp.where(odd, right, left)
+        inner_ref[n] = jnp.where(odd, left, right)
 
 
 def reach_of(i, rows):
@@ -135,7 +160,7 @@
     return shown
 
 
-def stencil_row(west, mid, east, coef_ref, at, shown):
+def stencil_row(west, mid, east, coef, at, shown):
     lane = lax.broadcasted_iota(jnp.int32, (8, LANES), 1)
     sub = lax.broadcasted_iota(jnp.int32, (8, LANES), 0)
     tiles = len(mid[0])
@@ -154,115 +179,160 @@
             if t > 0:
                 south = jnp.where(sub > 0, south, behind[h][t - 1])
             near = [mid[h][t], east[h][t], west[h][t], north, south, above[h], below[h]]
-            terms = [coef_ref[c, h, at, 8 * t : 8 * t + 8] * near[c] for c in range(7)]
+            terms = [coef(c, h, at, t) * near[c] for c in range(7)]
             image = (terms[0] - terms[1]) - (terms[2] + terms[3])
             images[h, t] = image - ((terms[4] + terms[5]) + terms[6])
     return images
 
 
+def own_tile(t, cols):
+    return t - HALO // 8 if HALO <= 8 * t < HALO + cols else None
+
+
+def coefficients(own_ref, halo_ref, cols):
+    def read(c, h, at, t):
+        n = own_tile(t, cols)
+        if n is not None:
+            return own_ref[c, h, at, 8 * n : 8 * n + 8]
+        side = 0 if 8 * t < HALO else 8
+        return halo_ref[c, h, at, side : side + 8]
+
+    return read
+
+
+def inside_row(i, rows):
+    at = lax.axis_index("gx") * rows - DEPTH + i
+    ok = jnp.logical_and(at >= 0, at < rows * lax.axis_size("gx"))
+    return jnp.where(ok, 1.0, 0.0)
+
+
+def widen(raw, spread):
+    first = raw.astype(jnp.bfloat16)
+    rest = raw - first.astype(jnp.float32)
+    second = rest.astype(jnp.bfloat16)
+    third = (rest - second.astype(jnp.float32)).astype(jnp.bfloat16)
+    pieces = jnp.concatenate([first, second, third], axis=1)
+    return jnp.dot(pieces, spread, preferred_element_type=jnp.float32)
+
+
+def tile_coefficients(wide_ref, at, h, keep):
+    lane = lax.broadcasted_iota(jnp.int32, (8, LANES), 1)
+    u, v, w, reaction = [
+        wide_ref[at : at + 8, (2 * c + h) * LANES : (2 * c + h + 1) * LANES] for c in range(4)
+    ]
+    side = [
+        horiz_diff + jnp.maximum(u, 0.0),
+        horiz_diff + jnp.maximum(-u, 0.0),
+        horiz_diff + jnp.maximum(v, 0.0),
+        horiz_diff + jnp.maximum(-v, 0.0),
+        vert_diff + jnp.maximum(w, 0.0),
+        vert_diff + jnp.maximum(-w, 0.0),
+    ]
+    diag = decay_rate + reaction
+    for one in side:
+        diag = diag + one
+    if h == 1:
+        side[4] = jnp.where(lane < LANES - R, side[4], 0.0)
+    else:
+        side[5] = jnp.where(lane >= R, side[5], 0.0)
+    return [one * keep for one in [diag] + side]
+
+
+def central_kernel(
+    own_ref, pair_ref, across_ref, far_ref, farther_ref, ex_ref, guess_ref, coef_ref,
+    raw_ref, wide_ref,
+):
+    rows, cols, _ = own_ref.shape
+    win = rows + 2 * DEPTH
+    place = lax.axis_index("gx")
+    refs = (own_ref, pair_ref, across_ref, far_ref, farther_ref)
+
+    def middle(i, lo):
+        blocks = [lambda x, ref=ref: ref[x, :, lo : lo + LANES] for ref in refs]
+        return window_row(i, rows, place, *blocks)
+
+    for i in range(win):
+        for h in range(2):
+            guess_ref[h, i] = middle(i, h * LANES) * inside_row(i, rows)
+    for i in range(win - 2):
+        raw_ref[i * cols : (i + 1) * cols, :] = middle(i + 1, 2 * LANES)
+    wide_ref[...] = widen(raw_ref[...], ex_ref[...])
+    for i in range(win - 2):
+        keep = inside_row(i + 1, rows) * (1.0 / SCALE)
+        for t in range(cols // 8):
+            for h in range(2):
+                values = tile_coefficients(wide_ref, i * cols + 8 * t, h, keep)
+                for c, one in enumerate(values):
+                    coef_ref[c, h, i, 8 * t : 8 * t + 8] = one
+
+
 def krylov_kernel(
-    rows, cols, rec_ref, outer_ref, inner_ref, own_ref, pair_ref, across_ref, far_ref, farther_ref,
-    ex_ref, gram_ref, f_ref, coef_ref,
-    raw_ref, wide_ref, hi_ref, lo_ref, cell_ref, cell_sem,
+    rows, cols, rec_ref, outer_ref, inner_ref, guess_ref, mine_ref, ex_ref, gram_ref, f_ref,
+    halo_ref, raw_ref, wide_ref, hi_ref, lo_ref, cell_ref, cell_sem,
 ):
     fetch = pltpu.make_async_copy(rec_ref, cell_ref, cell_sem)
     fetch.start()
     win = rows + 2 * DEPTH
-    crows = win - 2
     width = cols + 2 * HALO
     tiles = width // 8
-    total_rows = rows * lax.axis_size("gx")
-    edge_rows = outer_ref.shape[0]
-    edge_row0 = edge_start(lax.axis_index("gx"), rows, total_rows, edge_rows)
-    place = lax.axis_index("gx")
     odd = lax.axis_index("gy") % 2 == 1
     total_cols = cols * lax.axis_size("gy")
     row0 = lax.axis_index("gx") * rows - DEPTH
     col0 = lax.axis_index("gy") * cols - HALO
     lane = lax.broadcasted_iota(jnp.int32, (8, LANES), 1)
     sub = lax.broadcasted_iota(jnp.int32, (8, LANES), 0)
-
-    def inside_row(i):
-        at = row0 + i
-        ok = jnp.logical_and(at >= 0, at < total_rows)
-        return jnp.where(ok, 1.0, 0.0)
-
-    def parts(i, lo):
-        at_edge = jnp.clip(i - edge_row0, 0, edge_rows - 1)
-        outer = outer_ref[at_edge, :, lo : lo + LANES]
-        inner = inner_ref[at_edge, :, lo : lo + LANES]
-        blocks = [
-            lambda x, ref=ref: ref[x, :, lo : lo + LANES]
-            for ref in (own_ref, pair_ref, across_ref, far_ref, farther_ref)
-        ]
-        return (
-            jnp.where(odd, inner, outer),
-            window_row(i, rows, place, *blocks),
-            jnp.where(odd, outer, inner),
-        )
-
-    spans = ((0, HALO), (HALO, HALO + cols), (HALO + cols, width))
-
-    for i in range(win):
-        ok = inside_row(i)
+    sides = ((0, True), (HALO + cols, False))
+
+    def edge(i, lo, right):
+        away = reach_of(i, rows)
+        if away == 0:
+            n, turn = i - DEPTH, 0
+        else:
+            d = min(away, DEPTH - away)
+            n = rows + (0 if i < DEPTH else DEPTH // 2) + d - 1
+            turn = 0 if d == away else (HALO - d if right else d)
+        outer, inner = [ref[n, :, lo : lo + LANES] for ref in (outer_ref, inner_ref)]
+        tile = jnp.where(odd, inner, outer) if right else jnp.where(odd, outer, inner)
+        return pltpu.roll(tile, turn, 0) if turn else tile
+
+    for i in range(1, win - 1):
         for h in range(2):
-            for (c0, c1), piece in zip(spans, parts(i, h * LANES)):
-                f_ref[0, h, i, c0:c1] = piece * ok
-
-    for i in range(crows):
-        for (c0, c1), piece in zip(spans, parts(i + 1, 2 * LANES)):
-            raw_ref[i * width + c0 : i * width + c1, :] = piece
-
-    raw = raw_ref[...]
-    first = raw.astype(jnp.bfloat16)
-    rest = raw - first.astype(jnp.float32)
-    second = rest.astype(jnp.bfloat16)
-    third = (rest - second.astype(jnp.float32)).astype(jnp.bfloat16)
-    wide_ref[...] = jnp.dot(
-        jnp.concatenate([first, second, third], axis=1),
-        ex_ref[...],
-        preferred_element_type=jnp.float32,
-    )
-
-    for i in range(crows):
-        ok = inside_row(i + 1)
-        for t in tiles_within(DEPTH - 1 - reach_of(i + 1, rows), cols):
-            at = i * width + 8 * t
-            at_col = col0 + 8 * t + sub
+            for c0, right in sides:
+                f_ref[0, h, i, c0 : c0 + HALO] = edge(i, h * LANES, right) * inside_row(i, rows)
+
+    needed = [i for i in range(1, win - 1) if reach_of(i, rows) < DEPTH - 1]
+    for n, i in enumerate(needed):
+        for side, (c0, right) in enumerate(sides):
+            at = (2 * n + side) * HALO
+            raw_ref[at : at + HALO, :] = edge(i, 2 * LANES, right)
+    wide_ref[...] = widen(raw_ref[...], ex_ref[...])
+    for n, i in enumerate(needed):
+        for side, (c0, right) in enumerate(sides):
+            at_col = col0 + c0 + sub
             seen = jnp.logical_and(at_col >= 0, at_col < total_cols)
-            keep = jnp.where(seen, ok * (1.0 / SCALE), 0.0)
+            keep = jnp.where(seen, inside_row(i, rows) * (1.0 / SCALE), 0.0)
             for h in range(2):
-                u, v, w, reaction = [
-                    wide_ref[at : at + 8, (2 * c + h) * LANES : (2 * c + h + 1) * LANES]
-                    for c in range(4)
-                ]
-                side = [
-                    horiz_diff + jnp.maximum(u, 0.0),
-                    horiz_diff + jnp.maximum(-u, 0.0),
-                    horiz_diff + jnp.maximum(v, 0.0),
-                    horiz_diff + jnp.maximum(-v, 0.0),
-                    vert_diff + jnp.maximum(w, 0.0),
-                    vert_diff + jnp.maximum(-w, 0.0),
-                ]
-                diag = decay_rate + reaction
-                for one in side:
-                    diag = diag + one
-                if h == 1:
-                    side[4] = jnp.where(lane < LANES - R, side[4], 0.0)
-                else:
-                    side[5] = jnp.where(lane >= R, side[5], 0.0)
-                for c, one in enumerate([diag] + side):
-                    coef_ref[c, h, i, 8 * t : 8 * t + 8] = one * keep
+                values = tile_coefficients(wide_ref, (2 * n + side) * HALO, h, keep)
+                for c, one in enumerate(values):
+                    halo_ref[c, h, i - 1, side * HALO : (side + 1) * HALO] = one
+
+    coef = coefficients(mine_ref, halo_ref, cols)
+
+    def read(k, h, i, t):
+        n = own_tile(t, cols)
+        if k == 0 and n is not None:
+            return guess_ref[h, i, 8 * n : 8 * n + 8]
+        return f_ref[k, h, i, 8 * t : 8 * t + 8]
 
     def load(k, i):
-        return [[f_ref[k, h, i, 8 * t : 8 * t + 8] for t in range(tiles)] for h in range(2)]
+        return [[read(k, h, i, t) for t in range(tiles)] for h in range(2)]
 
     def apply(step, finish):
         west, mid = load(step - 1, step - 1), load(step - 1, step)
         for i in range(step, win - step):
             east = load(step - 1, i + 1)
             shown = tiles_within(DEPTH - step - reach_of(i, rows), cols)
-            images = stencil_row(west, mid, east, coef_ref, i - 1, shown)
+            images = stencil_row(west, mid, east, coef, i - 1, shown)
             for (h, t), image in images.items():
                 f_ref[step, h, i, 8 * t : 8 * t + 8] = finish(image, mid[h][t])
             west, mid = mid, east
@@ -355,8 +425,9 @@
         gram_ref[8 * n : 8 * n + 8] = chunk
 
 
-def finish_kernel(gram_ref, f_ref, coef_ref, x_ref, r_ref):
+def finish_kernel(gram_ref, f_ref, guess_ref, mine_ref, halo_ref, x_ref, r_ref):
     rows, cols = x_ref.shape[:2]
+    coef = coefficients(mine_ref, halo_ref, cols)
     tiles = (cols + 2 * HALO) // 8
     lane = lax.broadcasted_iota(jnp.int32, (8, LANES), 1)
     sub = lax.broadcasted_iota(jnp.int32, (8, LANES), 0)
@@ -484,7 +555,7 @@
     )
 
     def image_row(values, i, shown):
-        return stencil_row(values[i - 1], values[i], values[i + 1], coef_ref, i - 1, shown)
+        return stencil_row(values[i - 1], values[i], values[i + 1], coef, i - 1, shown)
 
     def half_row(i, shown):
         images = image_row(residual, i, shown)
@@ -499,7 +570,8 @@
             x = gained[0] * f_ref[1, h, i, at]
             for k in range(1, len(gained)):
                 x = x + gained[k] * f_ref[k + 1, h, i, at]
-            x = (f_ref[0, h, i, at] + x) + (alpha / SCALE) * residual[i][h][t]
+            mine = guess_ref[h, i, 8 * t - HALO : 8 * t - HALO + 8]
+            x = (mine + x) + (alpha / SCALE) * residual[i][h][t]
             x_ref[out] = x + (omega / SCALE) * half[i][h][t]
             r_ref[out] = half[i][h][t] - omega * turned
 
@@ -544,61 +616,72 @@
     else:
         farther = jnp.zeros_like(far_rows)
 
-    spans = [
-        (max(0, a * rows - DEPTH + 1), min(ngx * rows, (a + 1) * rows + DEPTH - 1))
-        for a in range(ngx)
-    ]
-    count = max(hi - lo for lo, hi in spans)
-    odd = lax.axis_index("gy") % 2 == 1
-
-    def edges(left):
-        blocks = [
-            lambda x, block=jnp.where(left, b[:, :HALO], b[:, cols - HALO :]): block[x]
-            for b in (own, pair, across, far, farther)
-        ]
-        whole = [window_row(i, rows, place, *blocks) for i in range(1, rows + 2 * DEPTH - 1)]
-        first = edge_start(place, rows, ngx * rows, count) - 1
-        return lax.dynamic_slice_in_dim(jnp.stack(whole), first, count, 0)
-
-    outer = swap(edges(~odd), "gy", [(j, j + 1) for j in range(1, ngy - 1, 2)])
-    inner = swap(edges(odd), "gy", [(j, j + 1) for j in range(0, ngy - 1, 2)])
-
-    total_cols = cols * ngy
-    cells = jnp.stack([receptors // total_cols, receptors % total_cols])
+    edge = pltpu.VMEM((rows + 2 * (DEPTH // 2), HALO, wide), jnp.float32)
+    outer, inner = pl.pallas_call(
+        edges_kernel,
+        out_shape=(edge, edge),
+        in_specs=[vmem] * 5,
+        out_specs=(vmem, vmem),
+        compiler_params=pltpu.CompilerParams(vmem_limit_bytes=8 * 1024 * 1024),
+        name="edges",
+    )(own, pair, across, far, farther)
+    outer = swap(outer, "gy", [(j, j + 1) for j in range(1, ngy - 1, 2)])
+    inner = swap(inner, "gy", [(j, j + 1) for j in range(0, ngy - 1, 2)])
+
     source_lane = jnp.arange(4 * NZ)[:, None]
     wide_lane = jnp.arange(4 * NZ * R)[None, :]
     spread = (source_lane == wide_lane // R).astype(jnp.bfloat16)
     spread = jnp.concatenate([spread] * 3, axis=0)
-    gram, vectors, coefficients = pl.pallas_call(
+    guess, mine = pl.pallas_call(
+        central_kernel,
+        out_shape=(
+            pltpu.VMEM((2, win, cols, LANES), jnp.float32),
+            pltpu.VMEM((7, 2, win - 2, cols, LANES), jnp.float32),
+        ),
+        in_specs=[vmem] * 6,
+        out_specs=(vmem, vmem),
+        scratch_shapes=[
+            pltpu.VMEM(((win - 2) * cols, LANES), jnp.float32),
+            pltpu.VMEM(((win - 2) * cols, 8 * LANES), jnp.float32),
+        ],
+        compiler_params=pltpu.CompilerParams(vmem_limit_bytes=16 * 1024 * 1024),
+        name="central",
+    )(own, pair, across, far, farther, spread)
+
+    total_cols = cols * ngy
+    cells = jnp.stack([receptors // total_cols, receptors % total_cols])
+    halo_rows = win - 4
+    vectors = 2 * rows * cols // 8
+    gram, basis, halo = pl.pallas_call(
         functools.partial(krylov_kernel, rows, cols),
         out_shape=(
             jax.ShapeDtypeStruct((devices * 8, LANES), jnp.float32),
-            jax.ShapeDtypeStruct((DEPTH + 1, 2, win, width, LANES), jnp.float32),
-            jax.ShapeDtypeStruct((7, 2, win - 2, width, LANES), jnp.float32),
+            pltpu.VMEM((DEPTH + 1, 2, win, width, LANES), jnp.float32),
+            pltpu.VMEM((7, 2, win - 2, 2 * HALO, LANES), jnp.float32),
         ),
-        in_specs=[pl.BlockSpec(memory_space=pl.ANY)] + [vmem] * 8,
+        in_specs=[pl.BlockSpec(memory_space=pl.ANY)] + [vmem] * 5,
         out_specs=(vmem, vmem, vmem),
         scratch_shapes=[
-            pltpu.VMEM(((win - 2) * width, LANES), jnp.float32),
-            pltpu.VMEM(((win - 2) * width, 8 * LANES), jnp.float32),
-            pltpu.VMEM((VECS, 2 * rows * cols // 8, 8, LANES), jnp.float32),
-            pltpu.VMEM((VECS, 2 * rows * cols // 8, 8, LANES), jnp.float32),
+            pltpu.VMEM((halo_rows * 2 * HALO, LANES), jnp.float32),
+            pltpu.VMEM((halo_rows * 2 * HALO, 8 * LANES), jnp.float32),
+            pltpu.VMEM((VECS, vectors, 8, LANES), jnp.float32),
+            pltpu.VMEM((VECS, vectors, 8, LANES), jnp.float32),
             pltpu.SMEM((2, R), jnp.int32),
             pltpu.SemaphoreType.DMA(()),
         ],
-        compiler_params=pltpu.CompilerParams(vmem_limit_bytes=40 * 1024 * 1024),
+        compiler_params=pltpu.CompilerParams(vmem_limit_bytes=24 * 1024 * 1024),
         name="krylov",
-    )(cells, outer, inner, own, pair, across, far, farther, spread)
+    )(cells, outer, inner, guess, mine, spread)
     everyone = lax.all_to_all(gram, ("gx", "gy"), 0, 0, tiled=True)
     out = jax.ShapeDtypeStruct((rows, cols, lanes), jnp.float32)
     return pl.pallas_call(
         finish_kernel,
         out_shape=(out, out),
-        in_specs=[vmem, vmem, vmem],
+        in_specs=[vmem] * 5,
         out_specs=(vmem, vmem),
         compiler_params=pltpu.CompilerParams(vmem_limit_bytes=16 * 1024 * 1024),
         name="finish",
-    )(everyone, vectors, coefficients)
+    )(everyone, basis, guess, mine, halo)
 
 
 def solution(mesh):

time: 40.7 us -> 38.8 us (0.953)
  blocking collectives: 15.4 us -> 14.4 us
  waiting for transfers between devices: 6.17 us -> 5.52 us
    all_to_all x1, blocking collectives: 15.4 us -> 14.4 us  [body(): everyone = lax.all_to_all(gram, ('gx', 'gy'), 0, 0, tiled=True)]
    ppermute x5, waiting for transfers between devices: 6.17 us -> 5.52 us  [swap(): return lax.ppermute(x, axis, pairs + [(j, i) for i, j in pairs])]
    pallas_call x1 -> x3, Pallas kernels: 1.71 us -> 2.33 us  [the longest x1 1.7 us: body(): pl.pallas_call(finish_kernel, out_shape=(out, out), in_specs=[vmem] * 5,...]
    pallas_call x1, Pallas kernels: 4.17 us -> 3.75 us  [body(): pl.pallas_call(functools.partial(krylov_kernel, rows, cols), out_shape=(j...]
  transfers between devices with their start and end apart: 5 -> 5, of which waited for: 2 -> 2; matrix products, arithmetic and copies ran while one was open for 2% -> 2% of each run, Pallas kernels for 0% -> 1%
where the time goes in v6:
time: 38.8 us; the launch traced here: 38.6 us
  blocking collectives  14.4 us (37%)
  starting transfers between devices  10.2 us (26%)
  Pallas kernels  7.03 us (18%)
  waiting for transfers between devices  5.52 us (14%)
  other arithmetic  0.83 us (2%)
  between operations  0.71 us (2%)
    all_to_all x1, blocking collectives, body(): everyone = lax.all_to_all(gram, ('gx', 'gy'), 0, 0, tiled=True)  14.4 us
    ppermute x5, starting transfers between devices, swap(): return lax.ppermute(x, axis, pairs + [(j, i) for i, j in pairs])  10.2 us
    ppermute x5, waiting for transfers between devices, swap(): return lax.ppermute(x, axis, pairs + [(j, i) for i, j in pairs])  5.52 us
    pallas_call x1, Pallas kernels, body(): pl.pallas_call(functools.partial(krylov_kernel, rows, cols), out_shape=(j...  3.75 us
    pallas_call x1, Pallas kernels, body(): pl.pallas_call(finish_kernel, out_shape=(out, out), in_specs=[vmem] * 5,...  1.7 us
    pallas_call x1, Pallas kernels, body(): pl.pallas_call(pack_kernel, out_shape=(pltpu.VMEM((rows, cols, wide), jnp...  0.96 us
  transfers between devices with their start and end apart: 5, of which 2 were waited for; matrix products, arithmetic and copies ran while one was open for 2% of the time, Pallas kernels for 1%

profile of v6, /device:TPU:0, one launch (start us, length us, event | category | flops | bytes accessed | tf_op | source)
XLA Modules:
  0.0 38.6 jit_solution(4707184545559296773)
XLA Ops:
  0.6 1.0 %pack.1 = (f32[4,16,384]{2,1,0:T(8,128)S(1)}, f32[3,16,384]{2,1,0:T(8,128)S(1)}) custom-call(f32[4,16,256]{2,1,0:T(8,128)} %guess_ref.1, f32[3,4,512]{2,1,0:T(4,128)} %velocity_ref.1, f32[4,512]{1,0:T(4,128)} %leaf_ref.1, s32[4,512]{1,0:T(4,128)} %canopy_ref.1, s32[4,512]{1,0:T(4,128)} %solid_ref.1), custom_call_target="tpu_custom_call" | custom-call | tf_op jit(solution)/shard_map/pack/pallas_call | solution.py:588
  1.6 0.7 %collective-permute-start.1 = (f32[4,16,384]{2,1,0:T(8,128)S(1)}, f32[4,16,384]{2,1,0:T(8,128)S(1)}, u32[]{:S(2)}, u32[]{:S(2)}) collective-permute-start(f32[4,16,384]{2,1,0:T(8,128)S(1)} %get-tuple-element.11.own_ref), channel_id=1, source_target_pairs={{8,16},{16,8},{9,17},{17,9},{10,18},{18,10},{11,19},{19,11},{12,20... | collective-permute-start | bytes 294920 | tf_op jit(solution)/shard_map/ppermute | solution.py:607
  2.3 5.9 %collective-permute-start = (f32[4,16,384]{2,1,0:T(8,128)S(1)}, f32[4,16,384]{2,1,0:T(8,128)S(1)}, u32[]{:S(2)}, u32[]{:S(2)}) collective-permute-start(f32[4,16,384]{2,1,0:T(8,128)S(1)} %get-tuple-element.11.own_ref), channel_id=1, source_target_pairs={{0,8},{16,24},{8,0},{24,16},{1,9},{17,25},{9,1},{25,17},{2,10},{18... | collective-permute-start | bytes 294920 | tf_op jit(solution)/shard_map/ppermute | solution.py:607
  8.2 0.0 collective-permute-start.2
  8.2 0.7 %fusion.4 = (s32[1,8]{1,0:T(1,128)S(1)}, s32[1,8]{1,0:T(1,128)S(1)}) fusion(s32[8]{0:T(128)} %param.11), kind=kLoop, calls=%fused_computation.16 | loop fusion | flops 152 | bytes 96 | tf_op jit(solution)/shard_map/stack | solution.py:652
  8.8 0.1 iota_compare_fusion
  8.9 5.2 %collective-permute-done.2.far_ref = f32[3,16,384]{2,1,0:T(8,128)S(1)} collective-permute-done((f32[3,16,384]{2,1,0:T(8,128)S(1)}, f32[3,16,384]{2,1,0:T(8,128)S(1)}, u32[]{:S(2)}, u32[]{:S(2)}) %collective-permute-start.2) | collective-permute-done | bytes 73760 | tf_op jit(solution)/shard_map/ppermute | solution.py:607
  14.2 0.0 collective-permute-done.1.across_ref
  14.2 0.0 collective-permute-done.pair_ref
  14.2 0.7 %collective-permute-start.3 = (f32[10,8,384]{2,1,0:T(8,128)S(1)}, f32[10,8,384]{2,1,0:T(8,128)S(1)}, u32[]{:S(2)}, u32[]{:S(2)}) collective-permute-start(f32[10,8,384]{2,1,0:T(8,128)S(1)} %get-tuple-element.13), channel_id=1, source_target_pairs={{1,2},{3,4},{5,6},{2,1},{4,3},{6,5},{9,10},{11,12},{13,14},{10,9},... | collective-permute-start | bytes 368648 | tf_op jit(solution)/shard_map/ppermute | solution.py:607
  14.9 2.9 %collective-permute-start.4 = (f32[10,8,384]{2,1,0:T(8,128)S(1)}, f32[10,8,384]{2,1,0:T(8,128)S(1)}, u32[]{:S(2)}, u32[]{:S(2)}) collective-permute-start(f32[10,8,384]{2,1,0:T(8,128)S(1)} %get-tuple-element.14), channel_id=1, source_target_pairs={{0,1},{2,3},{4,5},{6,7},{1,0},{3,2},{5,4},{7,6},{8,9},{10,11},{12,... | collective-permute-start | bytes 368648 | tf_op jit(solution)/shard_map/ppermute | solution.py:607
  17.8 0.1 add_convert_fusion.ex_ref
  17.9 0.6 %central.1 = (f32[2,18,16,128]{3,2,1,0:T(8,128)S(1)}, f32[7,2,16,16,128]{4,3,2,1,0:T(8,128)S(1)}) custom-call(f32[4,16,384]{2,1,0:T(8,128)S(1)} %get-tuple-element.11.own_ref, f32[4,16,384]{2,1,0:T(8,128)S(1)} %collective-permute-done.pair_ref, f32[4,16,384]{2,1,0:T(8,128)S(1)} %collective-permute-done.1.across_ref, ...), custom_call_target="tpu_custom_call" | custom-call | tf_op jit(solution)/shard_map/central/pallas_call | solution.py:635
  18.5 0.0 collective-permute-done.3.outer_ref
  18.5 0.3 collective-permute-done.4.inner_ref
  18.8 3.7 %krylov.1 = (f32[256,128]{1,0:T(8,128)S(1)}, f32[8,2,18,32,128]{4,3,2,1,0:T(8,128)S(1)}, f32[7,2,16,16,128]{4,3,2,1,0:T(8,128)S(1)}) custom-call(s32[2,8]{1,0:T(2,128)S(1)} %pad_add_fusion.rec_ref, f32[10,8,384]{2,1,0:T(8,128)S(1)} %collective-permute-done.3.outer_ref, f32[10,8,384]{2,1,0:T(8,128)S(1)} %collective-permute-done.4.inner_ref, ...), custom_call_target="tpu_custom_call" | custom-call | tf_op jit(solution)/shard_map/krylov/pallas_call | solution.py:655
  22.6 14.4 %all_to_all.11 = f32[32,8,128]{2,1,0:T(8,128)S(1)} all-to-all(f32[32,8,128]{2,1,0:T(8,128)S(1)} %bitcast.7), channel_id=1, replica_groups=mesh['gx'=4,'gy'=8] {'gx','gy'}, dimensions={0} | all-to-all | bytes 262144 | tf_op jit(solution)/shard_map/all_to_all | solution.py:675
  36.9 1.7 %finish.1 = (f32[4,16,256]{2,1,0:T(8,128)}, f32[4,16,256]{2,1,0:T(8,128)}) custom-call(f32[256,128]{1,0:T(8,128)S(1)} %bitcast.6, f32[8,2,18,32,128]{4,3,2,1,0:T(8,128)S(1)} %get-tuple-element.18.f_ref, f32[2,18,16,128]{3,2,1,0:T(8,128)S(1)} %get-tuple-element.15.guess_ref, f32[7,2,16,16,128]{4,3,2,1,0:T(8,128)S(1)} %get-tuple-element.16.mine_ref, ...), custom_call_target="tpu_custom_call" | custom-call | tf_op jit(solution)/shard_map/finish/pallas_call | solution.py:677
  (4 shorter events, 0.1 us)
Async XLA Ops:
  1.6 12.6 %collective-permute-start.1 = (f32[4,16,384]{2,1,0:T(8,128)S(1)}, f32[4,16,384]{2,1,0:T(8,128)S(1)}, u32[]{:S(2)}, u32[]{:S(2)}) collective-permute-start(f32[4,16,384]{2,1,0:T(8,128)S(1)} %get-tuple-element.11.own_ref), channel_id=1, source_target_pairs={{8,16},{16,8},{9,17},{17,9},{10,18},{18,10},{11,19},{19,11},{12,20... | collective-permute-start | bytes 294920 | tf_op jit(solution)/shard_map/ppermute | solution.py:607
  2.3 11.9 %collective-permute-start = (f32[4,16,384]{2,1,0:T(8,128)S(1)}, f32[4,16,384]{2,1,0:T(8,128)S(1)}, u32[]{:S(2)}, u32[]{:S(2)}) collective-permute-start(f32[4,16,384]{2,1,0:T(8,128)S(1)} %get-tuple-element.11.own_ref), channel_id=1, source_target_pairs={{0,8},{16,24},{8,0},{24,16},{1,9},{17,25},{9,1},{25,17},{2,10},{18... | collective-permute-start | bytes 294920 | tf_op jit(solution)/shard_map/ppermute | solution.py:607
  8.2 6.0 %collective-permute-start.2 = (f32[3,16,384]{2,1,0:T(8,128)S(1)}, f32[3,16,384]{2,1,0:T(8,128)S(1)}, u32[]{:S(2)}, u32[]{:S(2)}) collective-permute-start(f32[3,16,384]{2,1,0:T(8,128)S(1)} %get-tuple-element.12), channel_id=1, source_target_pairs={{0,16},{8,24},{16,0},{24,8},{1,17},{9,25},{17,1},{25,9},{2,18},{10... | collective-permute-start | bytes 221192 | tf_op jit(solution)/shard_map/ppermute | solution.py:607
  14.2 4.3 %collective-permute-start.3 = (f32[10,8,384]{2,1,0:T(8,128)S(1)}, f32[10,8,384]{2,1,0:T(8,128)S(1)}, u32[]{:S(2)}, u32[]{:S(2)}) collective-permute-start(f32[10,8,384]{2,1,0:T(8,128)S(1)} %get-tuple-element.13), channel_id=1, source_target_pairs={{1,2},{3,4},{5,6},{2,1},{4,3},{6,5},{9,10},{11,12},{13,14},{10,9},... | collective-permute-start | bytes 368648 | tf_op jit(solution)/shard_map/ppermute | solution.py:607
  14.9 3.9 %collective-permute-start.4 = (f32[10,8,384]{2,1,0:T(8,128)S(1)}, f32[10,8,384]{2,1,0:T(8,128)S(1)}, u32[]{:S(2)}, u32[]{:S(2)}) collective-permute-start(f32[10,8,384]{2,1,0:T(8,128)S(1)} %get-tuple-element.14), channel_id=1, source_target_pairs={{0,1},{2,3},{4,5},{6,7},{1,0},{3,2},{5,4},{7,6},{8,9},{10,11},{12,... | collective-permute-start | bytes 368648 | tf_op jit(solution)/shard_map/ppermute | solution.py:607

commit v7 on v6

--- a/solution.py
+++ b/solution.py
@@ -268,7 +268,7 @@
 
 def krylov_kernel(
     rows, cols, rec_ref, outer_ref, inner_ref, guess_ref, mine_ref, ex_ref, gram_ref, f_ref,
-    halo_ref, raw_ref, wide_ref, hi_ref, lo_ref, cell_ref, cell_sem,
+    halo_ref, raw_ref, wide_ref, cell_ref, cell_sem,
 ):
     fetch = pltpu.make_async_copy(rec_ref, cell_ref, cell_sem)
     fetch.start()
@@ -355,32 +355,28 @@
     pieces = [
         (h, i, t) for h in range(2) for i in range(rows) for t in range(cols // 8)
     ]
-    count = len(pieces)
-    for k in range(VECS):
-        for m, (h, i, t) in enumerate(pieces):
-            c0 = HALO + 8 * t
-            hi_ref[k, m], lo_ref[k, m] = split(f_ref[k + 1, h, DEPTH + i, c0 : c0 + 8])
-
     zero = jnp.zeros((8, LANES), jnp.float32)
     sums = {}
     for group in ([0, 1, 2, 3], [4, 5], [6]):
         pairs = [(i, j) for j in group for i in range(j + 1)]
 
-        def add(m, carry, pairs=pairs):
+        done = [(zero, zero)] * len(pairs)
+        for h, row, t in pieces:
             need = sorted({i for pair in pairs for i in pair})
-            hi = {k: hi_ref[k, m] for k in need}
-            lo = {k: lo_ref[k, m] for k in need}
+            at = slice(HALO + 8 * t, HALO + 8 * t + 8)
+            full = {k: f_ref[k + 1, h, DEPTH + row, at] for k in need}
+            halves = {k: split(full[k]) for k in need}
+            hi = {k: halves[k][0] for k in need}
+            lo = {k: halves[k][1] for k in need}
             out = []
-            for (i, j), (s, e) in zip(pairs, carry):
+            for (i, j), (s, e) in zip(pairs, done):
                 s, miss = two_sum(s, hi[i] * hi[j])
                 if i == j:
-                    cross = 2.0 * (hi[i] * lo[j])
+                    cross = lo[j] * (hi[i] + full[i])
                 else:
-                    cross = hi[i] * lo[j] + lo[i] * hi[j]
-                out.append((s, e + ((cross + lo[i] * lo[j]) + miss)))
-            return tuple(out)
-
-        done = lax.fori_loop(0, count, add, tuple((zero, zero) for _ in pairs), unroll=True)
+                    cross = hi[i] * lo[j] + lo[i] * full[j]
+                out.append((s, e + (cross + miss)))
+            done = out
         for pair, value in zip(pairs, done):
             sums[pair] = value
 
@@ -421,8 +417,12 @@
     e = (e + e1) + miss
     s, e = quick_sum(s, e)
     chunk = jnp.where(low, s, e)
-    for n in range(gram_ref.shape[0] // 8):
-        gram_ref[8 * n : 8 * n + 8] = chunk
+    folded = chunk
+    for r, turn in ((1, 3), (2, 5), (3, 7)):
+        other = pltpu.roll(pltpu.roll(chunk, turn, 0), 2 * R * (r + 1), 1)
+        folded = jnp.where((sub == r) & (lane // (2 * R) < r), other, folded)
+    for n in range(gram_ref.shape[0] // 4):
+        gram_ref[4 * n : 4 * n + 4] = folded[:4]
 
 
 def finish_kernel(gram_ref, f_ref, guess_ref, mine_ref, halo_ref, x_ref, r_ref):
@@ -431,8 +431,8 @@
     tiles = (cols + 2 * HALO) // 8
     lane = lax.broadcasted_iota(jnp.int32, (8, LANES), 1)
     sub = lax.broadcasted_iota(jnp.int32, (8, LANES), 0)
-    devices = gram_ref.shape[0] // 8
-    ways = math.gcd(devices, 8)
+    pairs = gram_ref.shape[0] // 8
+    ways = math.gcd(pairs, 8)
     zero = jnp.zeros((8, LANES), jnp.float32)
 
     def plus(a, b):
@@ -454,21 +454,31 @@
             out.append((s, e + miss))
         return tuple(out)
 
-    steps = devices // ways
+    steps = pairs // ways
     s, e = total(
         list(lax.fori_loop(0, steps, gather, ((zero, zero),) * ways, unroll=steps <= 8))
     )
+    s, e = plus((s, e), (pltpu.roll(s, 4, 0), pltpu.roll(e, 4, 0)))
     low = (lane & R) == 0
     g_hi = jnp.where(low, s, pltpu.roll(s, R, 1))
     g_lo = jnp.where(low, pltpu.roll(s, LANES - R, 1) + e, s + pltpu.roll(e, R, 1))
     g_hi, g_lo = quick_sum(g_hi, g_lo)
 
+    block = lane // (2 * R)
+
+    def unfold(x):
+        for i, turn in ((4, 1), (5, 3), (6, 5)):
+            x = jnp.where(sub == i, pltpu.roll(pltpu.roll(x, turn, 0), 2 * R * i, 1), x)
+        return x
+
     def column(x, j):
-        x = jnp.where(lane // (2 * R) == j, x, 0.0)
+        turned = jnp.where(block == sub, jnp.broadcast_to(x[j : j + 1], x.shape), 0.0)
+        x = jnp.where(sub <= j, jnp.where(block == j, x, 0.0), turned)
         for step in (64, 32, 16):
             x = x + pltpu.roll(x, step, 1)
-        return x
-
+        return jnp.where(sub < VECS, x, 0.0)
+
+    g_hi, g_lo = unfold(g_hi), unfold(g_lo)
     grams = [(column(g_hi, j), column(g_lo, j)) for j in range(VECS)]
     gram_splits = [split(g[0]) for g in grams]
 
@@ -651,11 +661,10 @@
     total_cols = cols * ngy
     cells = jnp.stack([receptors // total_cols, receptors % total_cols])
     halo_rows = win - 4
-    vectors = 2 * rows * cols // 8
     gram, basis, halo = pl.pallas_call(
         functools.partial(krylov_kernel, rows, cols),
         out_shape=(
-            jax.ShapeDtypeStruct((devices * 8, LANES), jnp.float32),
+            jax.ShapeDtypeStruct((devices * 4, LANES), jnp.float32),
             pltpu.VMEM((DEPTH + 1, 2, win, width, LANES), jnp.float32),
             pltpu.VMEM((7, 2, win - 2, 2 * HALO, LANES), jnp.float32),
         ),
@@ -664,8 +673,6 @@
         scratch_shapes=[
             pltpu.VMEM((halo_rows * 2 * HALO, LANES), jnp.float32),
             pltpu.VMEM((halo_rows * 2 * HALO, 8 * LANES), jnp.float32),
-            pltpu.VMEM((VECS, vectors, 8, LANES), jnp.float32),
-            pltpu.VMEM((VECS, vectors, 8, LANES), jnp.float32),
             pltpu.SMEM((2, R), jnp.int32),
             pltpu.SemaphoreType.DMA(()),
         ],

time: 38.8 us -> 38.2 us (0.985)
  blocking collectives: 14.4 us -> 13.6 us
    all_to_all x1, blocking collectives: 14.4 us -> 13.6 us  [body(): everyone = lax.all_to_all(gram, ('gx', 'gy'), 0, 0, tiled=True)]
  transfers between devices with their start and end apart: 5 -> 5, of which waited for: 2 -> 2; matrix products, arithmetic and copies ran while one was open for 2% -> 2% of each run, Pallas kernels for 1% -> 2%
where the time goes in v7:
time: 38.2 us; the launch traced here: 38 us
  blocking collectives  13.6 us (36%)
  starting transfers between devices  10.2 us (27%)
  Pallas kernels  7.21 us (19%)
  waiting for transfers between devices  5.52 us (14%)
  other arithmetic  0.83 us (2%)
  between operations  0.71 us (2%)
    all_to_all x1, blocking collectives, body(): everyone = lax.all_to_all(gram, ('gx', 'gy'), 0, 0, tiled=True)  13.6 us
    ppermute x5, starting transfers between devices, swap(): return lax.ppermute(x, axis, pairs + [(j, i) for i, j in pairs])  10.2 us
    ppermute x5, waiting for transfers between devices, swap(): return lax.ppermute(x, axis, pairs + [(j, i) for i, j in pairs])  5.52 us
    pallas_call x1, Pallas kernels, body(): pl.pallas_call(functools.partial(krylov_kernel, rows, cols), out_shape=(j...  3.74 us
    pallas_call x1, Pallas kernels, body(): pl.pallas_call(finish_kernel, out_shape=(out, out), in_specs=[vmem] * 5,...  1.89 us
    pallas_call x1, Pallas kernels, body(): pl.pallas_call(pack_kernel, out_shape=(pltpu.VMEM((rows, cols, wide), jnp...  0.96 us
  transfers between devices with their start and end apart: 5, of which 2 were waited for; matrix products, arithmetic and copies ran while one was open for 2% of the time, Pallas kernels for 2%

profile of v7, /device:TPU:0, one launch (start us, length us, event | category | flops | bytes accessed | tf_op | source)
XLA Modules:
  0.0 38.0 jit_solution(1657165390796384505)
XLA Ops:
  0.6 1.0 %pack.1 = (f32[4,16,384]{2,1,0:T(8,128)S(1)}, f32[3,16,384]{2,1,0:T(8,128)S(1)}) custom-call(f32[4,16,256]{2,1,0:T(8,128)} %guess_ref.1, f32[3,4,512]{2,1,0:T(4,128)} %velocity_ref.1, f32[4,512]{1,0:T(4,128)} %leaf_ref.1, s32[4,512]{1,0:T(4,128)} %canopy_ref.1, s32[4,512]{1,0:T(4,128)} %solid_ref.1), custom_call_target="tpu_custom_call" | custom-call | tf_op jit(solution)/shard_map/pack/pallas_call | solution.py:598
  1.6 0.7 %collective-permute-start.1 = (f32[4,16,384]{2,1,0:T(8,128)S(1)}, f32[4,16,384]{2,1,0:T(8,128)S(1)}, u32[]{:S(2)}, u32[]{:S(2)}) collective-permute-start(f32[4,16,384]{2,1,0:T(8,128)S(1)} %get-tuple-element.11.own_ref), channel_id=1, source_target_pairs={{8,16},{16,8},{9,17},{17,9},{10,18},{18,10},{11,19},{19,11},{12,20... | collective-permute-start | bytes 294920 | tf_op jit(solution)/shard_map/ppermute | solution.py:617
  2.3 5.9 %collective-permute-start = (f32[4,16,384]{2,1,0:T(8,128)S(1)}, f32[4,16,384]{2,1,0:T(8,128)S(1)}, u32[]{:S(2)}, u32[]{:S(2)}) collective-permute-start(f32[4,16,384]{2,1,0:T(8,128)S(1)} %get-tuple-element.11.own_ref), channel_id=1, source_target_pairs={{0,8},{16,24},{8,0},{24,16},{1,9},{17,25},{9,1},{25,17},{2,10},{18... | collective-permute-start | bytes 294920 | tf_op jit(solution)/shard_map/ppermute | solution.py:617
  8.2 0.0 collective-permute-start.2
  8.2 0.7 %fusion.4 = (s32[1,8]{1,0:T(1,128)S(1)}, s32[1,8]{1,0:T(1,128)S(1)}) fusion(s32[8]{0:T(128)} %param.11), kind=kLoop, calls=%fused_computation.16 | loop fusion | flops 152 | bytes 96 | tf_op jit(solution)/shard_map/stack | solution.py:662
  8.8 0.1 iota_compare_fusion
  8.9 5.2 %collective-permute-done.2.far_ref = f32[3,16,384]{2,1,0:T(8,128)S(1)} collective-permute-done((f32[3,16,384]{2,1,0:T(8,128)S(1)}, f32[3,16,384]{2,1,0:T(8,128)S(1)}, u32[]{:S(2)}, u32[]{:S(2)}) %collective-permute-start.2) | collective-permute-done | bytes 73760 | tf_op jit(solution)/shard_map/ppermute | solution.py:617
  14.2 0.0 collective-permute-done.1.across_ref
  14.2 0.0 collective-permute-done.pair_ref
  14.2 0.7 %collective-permute-start.3 = (f32[10,8,384]{2,1,0:T(8,128)S(1)}, f32[10,8,384]{2,1,0:T(8,128)S(1)}, u32[]{:S(2)}, u32[]{:S(2)}) collective-permute-start(f32[10,8,384]{2,1,0:T(8,128)S(1)} %get-tuple-element.13), channel_id=1, source_target_pairs={{1,2},{3,4},{5,6},{2,1},{4,3},{6,5},{9,10},{11,12},{13,14},{10,9},... | collective-permute-start | bytes 368648 | tf_op jit(solution)/shard_map/ppermute | solution.py:617
  14.9 2.9 %collective-permute-start.4 = (f32[10,8,384]{2,1,0:T(8,128)S(1)}, f32[10,8,384]{2,1,0:T(8,128)S(1)}, u32[]{:S(2)}, u32[]{:S(2)}) collective-permute-start(f32[10,8,384]{2,1,0:T(8,128)S(1)} %get-tuple-element.14), channel_id=1, source_target_pairs={{0,1},{2,3},{4,5},{6,7},{1,0},{3,2},{5,4},{7,6},{8,9},{10,11},{12,... | collective-permute-start | bytes 368648 | tf_op jit(solution)/shard_map/ppermute | solution.py:617
  17.8 0.1 add_convert_fusion.ex_ref
  17.9 0.6 %central.1 = (f32[2,18,16,128]{3,2,1,0:T(8,128)S(1)}, f32[7,2,16,16,128]{4,3,2,1,0:T(8,128)S(1)}) custom-call(f32[4,16,384]{2,1,0:T(8,128)S(1)} %get-tuple-element.11.own_ref, f32[4,16,384]{2,1,0:T(8,128)S(1)} %collective-permute-done.pair_ref, f32[4,16,384]{2,1,0:T(8,128)S(1)} %collective-permute-done.1.across_ref, ...), custom_call_target="tpu_custom_call" | custom-call | tf_op jit(solution)/shard_map/central/pallas_call | solution.py:645
  18.5 0.0 collective-permute-done.3.outer_ref
  18.5 0.3 collective-permute-done.4.inner_ref
  18.8 3.7 %krylov.1 = (f32[128,128]{1,0:T(8,128)S(1)}, f32[8,2,18,32,128]{4,3,2,1,0:T(8,128)S(1)}, f32[7,2,16,16,128]{4,3,2,1,0:T(8,128)S(1)}) custom-call(s32[2,8]{1,0:T(2,128)S(1)} %pad_add_fusion.rec_ref, f32[10,8,384]{2,1,0:T(8,128)S(1)} %collective-permute-done.3.outer_ref, f32[10,8,384]{2,1,0:T(8,128)S(1)} %collective-permute-done.4.inner_ref, ...), custom_call_target="tpu_custom_call" | custom-call | tf_op jit(solution)/shard_map/krylov/pallas_call | solution.py:664
  22.5 13.6 %all_to_all.11 = f32[32,4,128]{2,1,0:T(4,128)S(1)} all-to-all(f32[32,4,128]{2,1,0:T(4,128)S(1)} %bitcast.7), channel_id=1, replica_groups=mesh['gx'=4,'gy'=8] {'gx','gy'}, dimensions={0} | all-to-all | bytes 131072 | tf_op jit(solution)/shard_map/all_to_all | solution.py:682
  36.1 1.9 %finish.1 = (f32[4,16,256]{2,1,0:T(8,128)}, f32[4,16,256]{2,1,0:T(8,128)}) custom-call(f32[128,128]{1,0:T(8,128)S(1)} %bitcast.6, f32[8,2,18,32,128]{4,3,2,1,0:T(8,128)S(1)} %get-tuple-element.18.f_ref, f32[2,18,16,128]{3,2,1,0:T(8,128)S(1)} %get-tuple-element.15.guess_ref, f32[7,2,16,16,128]{4,3,2,1,0:T(8,128)S(1)} %get-tuple-element.16.mine_ref, ...), custom_call_target="tpu_custom_call" | custom-call | tf_op jit(solution)/shard_map/finish/pallas_call | solution.py:684
  (4 shorter events, 0.1 us)
Async XLA Ops:
  1.6 12.6 %collective-permute-start.1 = (f32[4,16,384]{2,1,0:T(8,128)S(1)}, f32[4,16,384]{2,1,0:T(8,128)S(1)}, u32[]{:S(2)}, u32[]{:S(2)}) collective-permute-start(f32[4,16,384]{2,1,0:T(8,128)S(1)} %get-tuple-element.11.own_ref), channel_id=1, source_target_pairs={{8,16},{16,8},{9,17},{17,9},{10,18},{18,10},{11,19},{19,11},{12,20... | collective-permute-start | bytes 294920 | tf_op jit(solution)/shard_map/ppermute | solution.py:617
  2.3 11.9 %collective-permute-start = (f32[4,16,384]{2,1,0:T(8,128)S(1)}, f32[4,16,384]{2,1,0:T(8,128)S(1)}, u32[]{:S(2)}, u32[]{:S(2)}) collective-permute-start(f32[4,16,384]{2,1,0:T(8,128)S(1)} %get-tuple-element.11.own_ref), channel_id=1, source_target_pairs={{0,8},{16,24},{8,0},{24,16},{1,9},{17,25},{9,1},{25,17},{2,10},{18... | collective-permute-start | bytes 294920 | tf_op jit(solution)/shard_map/ppermute | solution.py:617
  8.2 6.0 %collective-permute-start.2 = (f32[3,16,384]{2,1,0:T(8,128)S(1)}, f32[3,16,384]{2,1,0:T(8,128)S(1)}, u32[]{:S(2)}, u32[]{:S(2)}) collective-permute-start(f32[3,16,384]{2,1,0:T(8,128)S(1)} %get-tuple-element.12), channel_id=1, source_target_pairs={{0,16},{8,24},{16,0},{24,8},{1,17},{9,25},{17,1},{25,9},{2,18},{10... | collective-permute-start | bytes 221192 | tf_op jit(solution)/shard_map/ppermute | solution.py:617
  14.2 4.3 %collective-permute-start.3 = (f32[10,8,384]{2,1,0:T(8,128)S(1)}, f32[10,8,384]{2,1,0:T(8,128)S(1)}, u32[]{:S(2)}, u32[]{:S(2)}) collective-permute-start(f32[10,8,384]{2,1,0:T(8,128)S(1)} %get-tuple-element.13), channel_id=1, source_target_pairs={{1,2},{3,4},{5,6},{2,1},{4,3},{6,5},{9,10},{11,12},{13,14},{10,9},... | collective-permute-start | bytes 368648 | tf_op jit(solution)/shard_map/ppermute | solution.py:617
  14.9 3.9 %collective-permute-start.4 = (f32[10,8,384]{2,1,0:T(8,128)S(1)}, f32[10,8,384]{2,1,0:T(8,128)S(1)}, u32[]{:S(2)}, u32[]{:S(2)}) collective-permute-start(f32[10,8,384]{2,1,0:T(8,128)S(1)} %get-tuple-element.14), channel_id=1, source_target_pairs={{0,1},{2,3},{4,5},{6,7},{1,0},{3,2},{5,4},{7,6},{8,9},{10,11},{12,... | collective-permute-start | bytes 368648 | tf_op jit(solution)/shard_map/ppermute | solution.py:617

commit v8 on v7

--- a/solution.py
+++ b/solution.py
@@ -117,6 +117,15 @@
     return jnp.where(a % 4 >= 2, farther(at - 2 * rows), far(at - 2 * rows))
 
 
+def sides_kernel(own_ref, outer_ref, inner_ref):
+    cols = own_ref.shape[1]
+    odd = lax.axis_index("gy") % 2 == 1
+    for n in range(own_ref.shape[0]):
+        left, right = own_ref[n, :HALO, :], own_ref[n, cols - HALO :, :]
+        outer_ref[n] = jnp.where(odd, right, left)
+        inner_ref[n] = jnp.where(odd, left, right)
+
+
 def edges_kernel(
     own_ref, pair_ref, across_ref, far_ref, farther_ref, outer_ref, inner_ref
 ):
@@ -129,7 +138,7 @@
     def edge(right):
         c0 = cols - HALO if right else 0
         blocks = [lambda x, ref=ref: ref[x, c0 : c0 + HALO, :] for ref in refs]
-        tiles = [window_row(DEPTH + x, rows, place, *blocks) for x in range(rows)]
+        tiles = []
         for start, way in ((DEPTH, -1), (DEPTH + rows - 1, 1)):
             for d in range(1, DEPTH // 2 + 1):
                 close = window_row(start + way * d, rows, place, *blocks)
@@ -267,7 +276,7 @@
 
 
 def krylov_kernel(
-    rows, cols, rec_ref, outer_ref, inner_ref, guess_ref, mine_ref, ex_ref, gram_ref, f_ref,
+    rows, cols, rec_ref, outer_own_ref, inner_own_ref, outer_ref, inner_ref, guess_ref, mine_ref, ex_ref, gram_ref, f_ref,
     halo_ref, raw_ref, wide_ref, cell_ref, cell_sem,
 ):
     fetch = pltpu.make_async_copy(rec_ref, cell_ref, cell_sem)
@@ -285,13 +294,15 @@
 
     def edge(i, lo, right):
         away = reach_of(i, rows)
+        refs = outer_ref, inner_ref
         if away == 0:
+            refs = outer_own_ref, inner_own_ref
             n, turn = i - DEPTH, 0
         else:
             d = min(away, DEPTH - away)
-            n = rows + (0 if i < DEPTH else DEPTH // 2) + d - 1
+            n = (0 if i < DEPTH else DEPTH // 2) + d - 1
             turn = 0 if d == away else (HALO - d if right else d)
-        outer, inner = [ref[n, :, lo : lo + LANES] for ref in (outer_ref, inner_ref)]
+        outer, inner = [ref[n, :, lo : lo + LANES] for ref in refs]
         tile = jnp.where(odd, inner, outer) if right else jnp.where(odd, outer, inner)
         return pltpu.roll(tile, turn, 0) if turn else tile
 
@@ -626,17 +637,25 @@
     else:
         farther = jnp.zeros_like(far_rows)
 
-    edge = pltpu.VMEM((rows + 2 * (DEPTH // 2), HALO, wide), jnp.float32)
-    outer, inner = pl.pallas_call(
-        edges_kernel,
-        out_shape=(edge, edge),
-        in_specs=[vmem] * 5,
-        out_specs=(vmem, vmem),
-        compiler_params=pltpu.CompilerParams(vmem_limit_bytes=8 * 1024 * 1024),
-        name="edges",
-    )(own, pair, across, far, farther)
-    outer = swap(outer, "gy", [(j, j + 1) for j in range(1, ngy - 1, 2)])
-    inner = swap(inner, "gy", [(j, j + 1) for j in range(0, ngy - 1, 2)])
+    def exchange_edges(kernel, tiles, name, *blocks):
+        edge = pltpu.VMEM((tiles, HALO, wide), jnp.float32)
+        outer, inner = pl.pallas_call(
+            kernel,
+            out_shape=(edge, edge),
+            in_specs=[vmem] * len(blocks),
+            out_specs=(vmem, vmem),
+            compiler_params=pltpu.CompilerParams(vmem_limit_bytes=8 * 1024 * 1024),
+            name=name,
+        )(*blocks)
+        return (
+            swap(outer, "gy", [(j, j + 1) for j in range(1, ngy - 1, 2)]),
+            swap(inner, "gy", [(j, j + 1) for j in range(0, ngy - 1, 2)]),
+        )
+
+    outer_own, inner_own = exchange_edges(sides_kernel, rows, "sides", own)
+    outer, inner = exchange_edges(
+        edges_kernel, 2 * (DEPTH // 2), "edges", own, pair, across, far, farther
+    )
 
     source_lane = jnp.arange(4 * NZ)[:, None]
     wide_lane = jnp.arange(4 * NZ * R)[None, :]
@@ -668,7 +687,7 @@
             pltpu.VMEM((DEPTH + 1, 2, win, width, LANES), jnp.float32),
             pltpu.VMEM((7, 2, win - 2, 2 * HALO, LANES), jnp.float32),
         ),
-        in_specs=[pl.BlockSpec(memory_space=pl.ANY)] + [vmem] * 5,
+        in_specs=[pl.BlockSpec(memory_space=pl.ANY)] + [vmem] * 7,
         out_specs=(vmem, vmem, vmem),
         scratch_shapes=[
             pltpu.VMEM((halo_rows * 2 * HALO, LANES), jnp.float32),
@@ -678,7 +697,7 @@
         ],
         compiler_params=pltpu.CompilerParams(vmem_limit_bytes=24 * 1024 * 1024),
         name="krylov",
-    )(cells, outer, inner, guess, mine, spread)
+    )(cells, outer_own, inner_own, outer, inner, guess, mine, spread)
     everyone = lax.all_to_all(gram, ("gx", "gy"), 0, 0, tiled=True)
     out = jax.ShapeDtypeStruct((rows, cols, lanes), jnp.float32)
     return pl.pallas_call(

time: 38.2 us -> 37.3 us (0.976)
  waiting for transfers between devices: 5.52 us -> 1.85 us
  starting transfers between devices: 10.2 us -> 13.7 us
  blocking collectives: 13.6 us -> 12.7 us
    ppermute x5 -> x7, waiting for transfers between devices: 5.52 us -> 1.85 us  [swap(): return lax.ppermute(x, axis, pairs + [(j, i) for i, j in pairs])]
    ppermute x5 -> x7, starting transfers between devices: 10.2 us -> 13.7 us  [swap(): return lax.ppermute(x, axis, pairs + [(j, i) for i, j in pairs])]
    all_to_all x1, blocking collectives: 13.6 us -> 12.7 us  [body(): everyone = lax.all_to_all(gram, ('gx', 'gy'), 0, 0, tiled=True)]
  transfers between devices with their start and end apart: 5 -> 7, of which waited for: 2 -> 2; matrix products, arithmetic and copies ran while one was open for 2% -> 2% of each run, Pallas kernels for 2% -> 2%
where the time goes in v8:
time: 37.3 us; the launch traced here: 37 us
  starting transfers between devices  13.7 us (37%)
  blocking collectives  12.7 us (34%)
  Pallas kernels  7.21 us (19%)
  waiting for transfers between devices  1.85 us (5%)
  other arithmetic  0.83 us (2%)
  between operations  0.73 us (2%)
    ppermute x7, starting transfers between devices, swap(): return lax.ppermute(x, axis, pairs + [(j, i) for i, j in pairs])  13.7 us
    all_to_all x1, blocking collectives, body(): everyone = lax.all_to_all(gram, ('gx', 'gy'), 0, 0, tiled=True)  12.7 us
    pallas_call x1, Pallas kernels, body(): pl.pallas_call(functools.partial(krylov_kernel, rows, cols), out_shape=(j...  3.74 us
    pallas_call x1, Pallas kernels, body(): pl.pallas_call(finish_kernel, out_shape=(out, out), in_specs=[vmem] * 5,...  1.89 us
    ppermute x7, waiting for transfers between devices, swap(): return lax.ppermute(x, axis, pairs + [(j, i) for i, j in pairs])  1.85 us
    pallas_call x1, Pallas kernels, body(): pl.pallas_call(pack_kernel, out_shape=(pltpu.VMEM((rows, cols, wide), jnp...  0.96 us
  transfers between devices with their start and end apart: 7, of which 2 were waited for; matrix products, arithmetic and copies ran while one was open for 2% of the time, Pallas kernels for 2%

profile of v8, /device:TPU:0, one launch (start us, length us, event | category | flops | bytes accessed | tf_op | source)
XLA Modules:
  0.0 37.0 jit_solution(575585013071723920)
XLA Ops:
  0.6 1.0 %pack.1 = (f32[4,16,384]{2,1,0:T(8,128)S(1)}, f32[3,16,384]{2,1,0:T(8,128)S(1)}) custom-call(f32[4,16,256]{2,1,0:T(8,128)} %guess_ref.1, f32[3,4,512]{2,1,0:T(4,128)} %velocity_ref.1, f32[4,512]{1,0:T(4,128)} %leaf_ref.1, s32[4,512]{1,0:T(4,128)} %canopy_ref.1, s32[4,512]{1,0:T(4,128)} %solid_ref.1), custom_call_target="tpu_custom_call" | custom-call | tf_op jit(solution)/shard_map/pack/pallas_call | solution.py:609
  1.6 0.7 %collective-permute-start.3 = (f32[4,16,384]{2,1,0:T(8,128)S(1)}, f32[4,16,384]{2,1,0:T(8,128)S(1)}, u32[]{:S(2)}, u32[]{:S(2)}) collective-permute-start(f32[4,16,384]{2,1,0:T(8,128)S(1)} %get-tuple-element.13.own_ref), channel_id=1, source_target_pairs={{8,16},{16,8},{9,17},{17,9},{10,18},{18,10},{11,19},{19,11},{12,20... | collective-permute-start | bytes 294920 | tf_op jit(solution)/shard_map/ppermute | solution.py:628
  2.3 5.9 %collective-permute-start.2 = (f32[4,16,384]{2,1,0:T(8,128)S(1)}, f32[4,16,384]{2,1,0:T(8,128)S(1)}, u32[]{:S(2)}, u32[]{:S(2)}) collective-permute-start(f32[4,16,384]{2,1,0:T(8,128)S(1)} %get-tuple-element.13.own_ref), channel_id=1, source_target_pairs={{0,8},{16,24},{8,0},{24,16},{1,9},{17,25},{9,1},{25,17},{2,10},{18... | collective-permute-start | bytes 294920 | tf_op jit(solution)/shard_map/ppermute | solution.py:628
  8.2 0.0 collective-permute-start.4
  8.2 0.7 %collective-permute-start = (f32[4,8,384]{2,1,0:T(8,128)S(1)}, f32[4,8,384]{2,1,0:T(8,128)S(1)}, u32[]{:S(2)}, u32[]{:S(2)}) collective-permute-start(f32[4,8,384]{2,1,0:T(8,128)S(1)} %get-tuple-element.14), channel_id=1, source_target_pairs={{1,2},{3,4},{5,6},{2,1},{4,3},{6,5},{9,10},{11,12},{13,14},{10,9},... | collective-permute-start | bytes 147464 | tf_op jit(solution)/shard_map/ppermute | solution.py:628
  8.9 2.9 %collective-permute-start.1 = (f32[4,8,384]{2,1,0:T(8,128)S(1)}, f32[4,8,384]{2,1,0:T(8,128)S(1)}, u32[]{:S(2)}, u32[]{:S(2)}) collective-permute-start(f32[4,8,384]{2,1,0:T(8,128)S(1)} %get-tuple-element.15), channel_id=1, source_target_pairs={{0,1},{2,3},{4,5},{6,7},{1,0},{3,2},{5,4},{7,6},{8,9},{10,11},{12,... | collective-permute-start | bytes 147464 | tf_op jit(solution)/shard_map/ppermute | solution.py:628
  11.8 0.7 %fusion.4 = (s32[1,8]{1,0:T(1,128)S(1)}, s32[1,8]{1,0:T(1,128)S(1)}) fusion(s32[8]{0:T(128)} %param.11), kind=kLoop, calls=%fused_computation.16 | loop fusion | flops 152 | bytes 96 | tf_op jit(solution)/shard_map/stack | solution.py:681
  12.5 0.1 iota_compare_fusion
  12.5 0.1 add_convert_fusion.ex_ref
  12.6 1.5 %collective-permute-done.4.far_ref = f32[3,16,384]{2,1,0:T(8,128)S(1)} collective-permute-done((f32[3,16,384]{2,1,0:T(8,128)S(1)}, f32[3,16,384]{2,1,0:T(8,128)S(1)}, u32[]{:S(2)}, u32[]{:S(2)}) %collective-permute-start.4) | collective-permute-done | bytes 73760 | tf_op jit(solution)/shard_map/ppermute | solution.py:628
  14.2 0.0 collective-permute-done.3.across_ref
  14.2 0.0 collective-permute-done.2.pair_ref
  14.2 0.7 %collective-permute-start.5 = (f32[6,8,384]{2,1,0:T(8,128)S(1)}, f32[6,8,384]{2,1,0:T(8,128)S(1)}, u32[]{:S(2)}, u32[]{:S(2)}) collective-permute-start(f32[6,8,384]{2,1,0:T(8,128)S(1)} %get-tuple-element.17), channel_id=1, source_target_pairs={{1,2},{3,4},{5,6},{2,1},{4,3},{6,5},{9,10},{11,12},{13,14},{10,9},... | collective-permute-start | bytes 221192 | tf_op jit(solution)/shard_map/ppermute | solution.py:628
  14.9 2.9 %collective-permute-start.6 = (f32[6,8,384]{2,1,0:T(8,128)S(1)}, f32[6,8,384]{2,1,0:T(8,128)S(1)}, u32[]{:S(2)}, u32[]{:S(2)}) collective-permute-start(f32[6,8,384]{2,1,0:T(8,128)S(1)} %get-tuple-element.18), channel_id=1, source_target_pairs={{0,1},{2,3},{4,5},{6,7},{1,0},{3,2},{5,4},{7,6},{8,9},{10,11},{12,... | collective-permute-start | bytes 221192 | tf_op jit(solution)/shard_map/ppermute | solution.py:628
  17.8 0.6 %central.1 = (f32[2,18,16,128]{3,2,1,0:T(8,128)S(1)}, f32[7,2,16,16,128]{4,3,2,1,0:T(8,128)S(1)}) custom-call(f32[4,16,384]{2,1,0:T(8,128)S(1)} %get-tuple-element.13.own_ref, f32[4,16,384]{2,1,0:T(8,128)S(1)} %collective-permute-done.2.pair_ref, f32[4,16,384]{2,1,0:T(8,128)S(1)} %collective-permute-done.3.across_ref, ...), custom_call_target="tpu_custom_call" | custom-call | tf_op jit(solution)/shard_map/central/pallas_call | solution.py:664
  18.4 0.0 collective-permute-done.outer_own_ref
  18.4 0.0 collective-permute-done.1.inner_own_ref
  18.4 0.0 collective-permute-done.5.outer_ref
  18.4 0.3 collective-permute-done.6.inner_ref
  18.7 3.7 %krylov.1 = (f32[128,128]{1,0:T(8,128)S(1)}, f32[8,2,18,32,128]{4,3,2,1,0:T(8,128)S(1)}, f32[7,2,16,16,128]{4,3,2,1,0:T(8,128)S(1)}) custom-call(s32[2,8]{1,0:T(2,128)S(1)} %pad_add_fusion.rec_ref, f32[4,8,384]{2,1,0:T(8,128)S(1)} %collective-permute-done.outer_own_ref, f32[4,8,384]{2,1,0:T(8,128)S(1)} %collective-permute-done.1.inner_own_ref, ...), custom_call_target="tpu_custom_call" | custom-call | tf_op jit(solution)/shard_map/krylov/pallas_call | solution.py:683
  22.5 12.7 %all_to_all.11 = f32[32,4,128]{2,1,0:T(4,128)S(1)} all-to-all(f32[32,4,128]{2,1,0:T(4,128)S(1)} %bitcast.7), channel_id=1, replica_groups=mesh['gx'=4,'gy'=8] {'gx','gy'}, dimensions={0} | all-to-all | bytes 131072 | tf_op jit(solution)/shard_map/all_to_all | solution.py:701
  35.2 1.9 %finish.1 = (f32[4,16,256]{2,1,0:T(8,128)}, f32[4,16,256]{2,1,0:T(8,128)}) custom-call(f32[128,128]{1,0:T(8,128)S(1)} %bitcast.6, f32[8,2,18,32,128]{4,3,2,1,0:T(8,128)S(1)} %get-tuple-element.22.f_ref, f32[2,18,16,128]{3,2,1,0:T(8,128)S(1)} %get-tuple-element.19.guess_ref, f32[7,2,16,16,128]{4,3,2,1,0:T(8,128)S(1)} %get-tuple-element.20.mine_ref, ...), custom_call_target="tpu_custom_call" | custom-call | tf_op jit(solution)/shard_map/finish/pallas_call | solution.py:703
  (5 shorter events, 0.1 us)
Async XLA Ops:
  1.6 12.6 %collective-permute-start.3 = (f32[4,16,384]{2,1,0:T(8,128)S(1)}, f32[4,16,384]{2,1,0:T(8,128)S(1)}, u32[]{:S(2)}, u32[]{:S(2)}) collective-permute-start(f32[4,16,384]{2,1,0:T(8,128)S(1)} %get-tuple-element.13.own_ref), channel_id=1, source_target_pairs={{8,16},{16,8},{9,17},{17,9},{10,18},{18,10},{11,19},{19,11},{12,20... | collective-permute-start | bytes 294920 | tf_op jit(solution)/shard_map/ppermute | solution.py:628
  2.3 11.9 %collective-permute-start.2 = (f32[4,16,384]{2,1,0:T(8,128)S(1)}, f32[4,16,384]{2,1,0:T(8,128)S(1)}, u32[]{:S(2)}, u32[]{:S(2)}) collective-permute-start(f32[4,16,384]{2,1,0:T(8,128)S(1)} %get-tuple-element.13.own_ref), channel_id=1, source_target_pairs={{0,8},{16,24},{8,0},{24,16},{1,9},{17,25},{9,1},{25,17},{2,10},{18... | collective-permute-start | bytes 294920 | tf_op jit(solution)/shard_map/ppermute | solution.py:628
  8.2 6.0 %collective-permute-start.4 = (f32[3,16,384]{2,1,0:T(8,128)S(1)}, f32[3,16,384]{2,1,0:T(8,128)S(1)}, u32[]{:S(2)}, u32[]{:S(2)}) collective-permute-start(f32[3,16,384]{2,1,0:T(8,128)S(1)} %get-tuple-element.16), channel_id=1, source_target_pairs={{0,16},{8,24},{16,0},{24,8},{1,17},{9,25},{17,1},{25,9},{2,18},{10... | collective-permute-start | bytes 221192 | tf_op jit(solution)/shard_map/ppermute | solution.py:628
  8.2 10.2 %collective-permute-start = (f32[4,8,384]{2,1,0:T(8,128)S(1)}, f32[4,8,384]{2,1,0:T(8,128)S(1)}, u32[]{:S(2)}, u32[]{:S(2)}) collective-permute-start(f32[4,8,384]{2,1,0:T(8,128)S(1)} %get-tuple-element.14), channel_id=1, source_target_pairs={{1,2},{3,4},{5,6},{2,1},{4,3},{6,5},{9,10},{11,12},{13,14},{10,9},... | collective-permute-start | bytes 147464 | tf_op jit(solution)/shard_map/ppermute | solution.py:628
  8.9 9.6 %collective-permute-start.1 = (f32[4,8,384]{2,1,0:T(8,128)S(1)}, f32[4,8,384]{2,1,0:T(8,128)S(1)}, u32[]{:S(2)}, u32[]{:S(2)}) collective-permute-start(f32[4,8,384]{2,1,0:T(8,128)S(1)} %get-tuple-element.15), channel_id=1, source_target_pairs={{0,1},{2,3},{4,5},{6,7},{1,0},{3,2},{5,4},{7,6},{8,9},{10,11},{12,... | collective-permute-start | bytes 147464 | tf_op jit(solution)/shard_map/ppermute | solution.py:628
  14.2 4.2 %collective-permute-start.5 = (f32[6,8,384]{2,1,0:T(8,128)S(1)}, f32[6,8,384]{2,1,0:T(8,128)S(1)}, u32[]{:S(2)}, u32[]{:S(2)}) collective-permute-start(f32[6,8,384]{2,1,0:T(8,128)S(1)} %get-tuple-element.17), channel_id=1, source_target_pairs={{1,2},{3,4},{5,6},{2,1},{4,3},{6,5},{9,10},{11,12},{13,14},{10,9},... | collective-permute-start | bytes 221192 | tf_op jit(solution)/shard_map/ppermute | solution.py:628
  14.9 3.8 %collective-permute-start.6 = (f32[6,8,384]{2,1,0:T(8,128)S(1)}, f32[6,8,384]{2,1,0:T(8,128)S(1)}, u32[]{:S(2)}, u32[]{:S(2)}) collective-permute-start(f32[6,8,384]{2,1,0:T(8,128)S(1)} %get-tuple-element.18), channel_id=1, source_target_pairs={{0,1},{2,3},{4,5},{6,7},{1,0},{3,2},{5,4},{7,6},{8,9},{10,11},{12,... | collective-permute-start | bytes 221192 | tf_op jit(solution)/shard_map/ppermute | solution.py:628

commit v9 on v8

--- a/solution.py
+++ b/solution.py
@@ -368,7 +368,7 @@
     ]
     zero = jnp.zeros((8, LANES), jnp.float32)
     sums = {}
-    for group in ([0, 1, 2, 3], [4, 5], [6]):
+    for group in ([0, 1, 2, 3, 4], [5, 6]):
         pairs = [(i, j) for j in group for i in range(j + 1)]
 
         done = [(zero, zero)] * len(pairs)
@@ -550,9 +550,9 @@
             turn_list = list_minus(list1, alpha, list2)
             gained = gained + [zero] * (len(half_list) - len(gained))
             for k, one in enumerate(half_list):
-                gained[k] = gained[k] + (omega / SCALE) * one[0]
+                gained[k] = gained[k] + (omega * (1.0 / SCALE)) * one[0]
             for k, one in enumerate(as_list):
-                gained[k] = gained[k] + (alpha / SCALE) * one[0]
+                gained[k] = gained[k] + (alpha * (1.0 / SCALE)) * one[0]
             as_list = list_minus(half_list, omega, turn_list)
             as_sub = minus(minus(as_sub, alpha, sub1), omega, minus(sub1, alpha, sub2))
 
@@ -592,8 +592,8 @@
             for k in range(1, len(gained)):
                 x = x + gained[k] * f_ref[k + 1, h, i, at]
             mine = guess_ref[h, i, 8 * t - HALO : 8 * t - HALO + 8]
-            x = (mine + x) + (alpha / SCALE) * residual[i][h][t]
-            x_ref[out] = x + (omega / SCALE) * half[i][h][t]
+            x = (mine + x) + (alpha * (1.0 / SCALE)) * residual[i][h][t]
+            x_ref[out] = x + (omega * (1.0 / SCALE)) * half[i][h][t]
             r_ref[out] = half[i][h][t] - omega * turned
 
 

time: 37.3 us -> 37.3 us (level)
  no operation moved by 1% of the time
where the time goes in v9:
time: 37.3 us; the launch traced here: 37.1 us
  starting transfers between devices  13.7 us (37%)
  blocking collectives  12.7 us (34%)
  Pallas kernels  7.21 us (19%)
  waiting for transfers between devices  1.85 us (5%)
  other arithmetic  0.83 us (2%)
  between operations  0.73 us (2%)
    ppermute x7, starting transfers between devices, swap(): return lax.ppermute(x, axis, pairs + [(j, i) for i, j in pairs])  13.7 us
    all_to_all x1, blocking collectives, body(): everyone = lax.all_to_all(gram, ('gx', 'gy'), 0, 0, tiled=True)  12.7 us
    pallas_call x1, Pallas kernels, body(): pl.pallas_call(functools.partial(krylov_kernel, rows, cols), out_shape=(j...  3.74 us
    pallas_call x1, Pallas kernels, body(): pl.pallas_call(finish_kernel, out_shape=(out, out), in_specs=[vmem] * 5,...  1.89 us
    ppermute x7, waiting for transfers between devices, swap(): return lax.ppermute(x, axis, pairs + [(j, i) for i, j in pairs])  1.85 us
    pallas_call x1, Pallas kernels, body(): pl.pallas_call(pack_kernel, out_shape=(pltpu.VMEM((rows, cols, wide), jnp...  0.96 us
  transfers between devices with their start and end apart: 7, of which 2 were waited for; matrix products, arithmetic and copies ran while one was open for 2% of the time, Pallas kernels for 2%

profile of v9, /device:TPU:0, one launch (start us, length us, event | category | flops | bytes accessed | tf_op | source)
XLA Modules:
  0.0 37.1 jit_solution(11596358593800872662)
XLA Ops:
  0.6 1.0 %pack.1 = (f32[4,16,384]{2,1,0:T(8,128)S(1)}, f32[3,16,384]{2,1,0:T(8,128)S(1)}) custom-call(f32[4,16,256]{2,1,0:T(8,128)} %guess_ref.1, f32[3,4,512]{2,1,0:T(4,128)} %velocity_ref.1, f32[4,512]{1,0:T(4,128)} %leaf_ref.1, s32[4,512]{1,0:T(4,128)} %canopy_ref.1, s32[4,512]{1,0:T(4,128)} %solid_ref.1), custom_call_target="tpu_custom_call" | custom-call | tf_op jit(solution)/shard_map/pack/pallas_call | solution.py:609
  1.6 0.7 %collective-permute-start.3 = (f32[4,16,384]{2,1,0:T(8,128)S(1)}, f32[4,16,384]{2,1,0:T(8,128)S(1)}, u32[]{:S(2)}, u32[]{:S(2)}) collective-permute-start(f32[4,16,384]{2,1,0:T(8,128)S(1)} %get-tuple-element.13.own_ref), channel_id=1, source_target_pairs={{8,16},{16,8},{9,17},{17,9},{10,18},{18,10},{11,19},{19,11},{12,20... | collective-permute-start | bytes 294920 | tf_op jit(solution)/shard_map/ppermute | solution.py:628
  2.3 5.9 %collective-permute-start.2 = (f32[4,16,384]{2,1,0:T(8,128)S(1)}, f32[4,16,384]{2,1,0:T(8,128)S(1)}, u32[]{:S(2)}, u32[]{:S(2)}) collective-permute-start(f32[4,16,384]{2,1,0:T(8,128)S(1)} %get-tuple-element.13.own_ref), channel_id=1, source_target_pairs={{0,8},{16,24},{8,0},{24,16},{1,9},{17,25},{9,1},{25,17},{2,10},{18... | collective-permute-start | bytes 294920 | tf_op jit(solution)/shard_map/ppermute | solution.py:628
  8.2 0.0 collective-permute-start.4
  8.2 0.7 %collective-permute-start = (f32[4,8,384]{2,1,0:T(8,128)S(1)}, f32[4,8,384]{2,1,0:T(8,128)S(1)}, u32[]{:S(2)}, u32[]{:S(2)}) collective-permute-start(f32[4,8,384]{2,1,0:T(8,128)S(1)} %get-tuple-element.14), channel_id=1, source_target_pairs={{1,2},{3,4},{5,6},{2,1},{4,3},{6,5},{9,10},{11,12},{13,14},{10,9},... | collective-permute-start | bytes 147464 | tf_op jit(solution)/shard_map/ppermute | solution.py:628
  8.9 2.9 %collective-permute-start.1 = (f32[4,8,384]{2,1,0:T(8,128)S(1)}, f32[4,8,384]{2,1,0:T(8,128)S(1)}, u32[]{:S(2)}, u32[]{:S(2)}) collective-permute-start(f32[4,8,384]{2,1,0:T(8,128)S(1)} %get-tuple-element.15), channel_id=1, source_target_pairs={{0,1},{2,3},{4,5},{6,7},{1,0},{3,2},{5,4},{7,6},{8,9},{10,11},{12,... | collective-permute-start | bytes 147464 | tf_op jit(solution)/shard_map/ppermute | solution.py:628
  11.8 0.7 %fusion.4 = (s32[1,8]{1,0:T(1,128)S(1)}, s32[1,8]{1,0:T(1,128)S(1)}) fusion(s32[8]{0:T(128)} %param.11), kind=kLoop, calls=%fused_computation.16 | loop fusion | flops 152 | bytes 96 | tf_op jit(solution)/shard_map/stack | solution.py:681
  12.5 0.1 iota_compare_fusion
  12.5 0.1 add_convert_fusion.ex_ref
  12.6 1.5 %collective-permute-done.4.far_ref = f32[3,16,384]{2,1,0:T(8,128)S(1)} collective-permute-done((f32[3,16,384]{2,1,0:T(8,128)S(1)}, f32[3,16,384]{2,1,0:T(8,128)S(1)}, u32[]{:S(2)}, u32[]{:S(2)}) %collective-permute-start.4) | collective-permute-done | bytes 73760 | tf_op jit(solution)/shard_map/ppermute | solution.py:628
  14.2 0.0 collective-permute-done.3.across_ref
  14.2 0.0 collective-permute-done.2.pair_ref
  14.2 0.7 %collective-permute-start.5 = (f32[6,8,384]{2,1,0:T(8,128)S(1)}, f32[6,8,384]{2,1,0:T(8,128)S(1)}, u32[]{:S(2)}, u32[]{:S(2)}) collective-permute-start(f32[6,8,384]{2,1,0:T(8,128)S(1)} %get-tuple-element.17), channel_id=1, source_target_pairs={{1,2},{3,4},{5,6},{2,1},{4,3},{6,5},{9,10},{11,12},{13,14},{10,9},... | collective-permute-start | bytes 221192 | tf_op jit(solution)/shard_map/ppermute | solution.py:628
  14.9 2.9 %collective-permute-start.6 = (f32[6,8,384]{2,1,0:T(8,128)S(1)}, f32[6,8,384]{2,1,0:T(8,128)S(1)}, u32[]{:S(2)}, u32[]{:S(2)}) collective-permute-start(f32[6,8,384]{2,1,0:T(8,128)S(1)} %get-tuple-element.18), channel_id=1, source_target_pairs={{0,1},{2,3},{4,5},{6,7},{1,0},{3,2},{5,4},{7,6},{8,9},{10,11},{12,... | collective-permute-start | bytes 221192 | tf_op jit(solution)/shard_map/ppermute | solution.py:628
  17.8 0.6 %central.1 = (f32[2,18,16,128]{3,2,1,0:T(8,128)S(1)}, f32[7,2,16,16,128]{4,3,2,1,0:T(8,128)S(1)}) custom-call(f32[4,16,384]{2,1,0:T(8,128)S(1)} %get-tuple-element.13.own_ref, f32[4,16,384]{2,1,0:T(8,128)S(1)} %collective-permute-done.2.pair_ref, f32[4,16,384]{2,1,0:T(8,128)S(1)} %collective-permute-done.3.across_ref, ...), custom_call_target="tpu_custom_call" | custom-call | tf_op jit(solution)/shard_map/central/pallas_call | solution.py:664
  18.4 0.0 collective-permute-done.outer_own_ref
  18.4 0.0 collective-permute-done.1.inner_own_ref
  18.4 0.0 collective-permute-done.5.outer_ref
  18.4 0.3 collective-permute-done.6.inner_ref
  18.7 3.7 %krylov.1 = (f32[128,128]{1,0:T(8,128)S(1)}, f32[8,2,18,32,128]{4,3,2,1,0:T(8,128)S(1)}, f32[7,2,16,16,128]{4,3,2,1,0:T(8,128)S(1)}) custom-call(s32[2,8]{1,0:T(2,128)S(1)} %pad_add_fusion.rec_ref, f32[4,8,384]{2,1,0:T(8,128)S(1)} %collective-permute-done.outer_own_ref, f32[4,8,384]{2,1,0:T(8,128)S(1)} %collective-permute-done.1.inner_own_ref, ...), custom_call_target="tpu_custom_call" | custom-call | tf_op jit(solution)/shard_map/krylov/pallas_call | solution.py:683
  22.5 12.7 %all_to_all.11 = f32[32,4,128]{2,1,0:T(4,128)S(1)} all-to-all(f32[32,4,128]{2,1,0:T(4,128)S(1)} %bitcast.7), channel_id=1, replica_groups=mesh['gx'=4,'gy'=8] {'gx','gy'}, dimensions={0} | all-to-all | bytes 131072 | tf_op jit(solution)/shard_map/all_to_all | solution.py:701
  35.2 1.9 %finish.1 = (f32[4,16,256]{2,1,0:T(8,128)}, f32[4,16,256]{2,1,0:T(8,128)}) custom-call(f32[128,128]{1,0:T(8,128)S(1)} %bitcast.6, f32[8,2,18,32,128]{4,3,2,1,0:T(8,128)S(1)} %get-tuple-element.22.f_ref, f32[2,18,16,128]{3,2,1,0:T(8,128)S(1)} %get-tuple-element.19.guess_ref, f32[7,2,16,16,128]{4,3,2,1,0:T(8,128)S(1)} %get-tuple-element.20.mine_ref, ...), custom_call_target="tpu_custom_call" | custom-call | tf_op jit(solution)/shard_map/finish/pallas_call | solution.py:703
  (5 shorter events, 0.1 us)
Async XLA Ops:
  1.6 12.6 %collective-permute-start.3 = (f32[4,16,384]{2,1,0:T(8,128)S(1)}, f32[4,16,384]{2,1,0:T(8,128)S(1)}, u32[]{:S(2)}, u32[]{:S(2)}) collective-permute-start(f32[4,16,384]{2,1,0:T(8,128)S(1)} %get-tuple-element.13.own_ref), channel_id=1, source_target_pairs={{8,16},{16,8},{9,17},{17,9},{10,18},{18,10},{11,19},{19,11},{12,20... | collective-permute-start | bytes 294920 | tf_op jit(solution)/shard_map/ppermute | solution.py:628
  2.3 11.9 %collective-permute-start.2 = (f32[4,16,384]{2,1,0:T(8,128)S(1)}, f32[4,16,384]{2,1,0:T(8,128)S(1)}, u32[]{:S(2)}, u32[]{:S(2)}) collective-permute-start(f32[4,16,384]{2,1,0:T(8,128)S(1)} %get-tuple-element.13.own_ref), channel_id=1, source_target_pairs={{0,8},{16,24},{8,0},{24,16},{1,9},{17,25},{9,1},{25,17},{2,10},{18... | collective-permute-start | bytes 294920 | tf_op jit(solution)/shard_map/ppermute | solution.py:628
  8.2 6.0 %collective-permute-start.4 = (f32[3,16,384]{2,1,0:T(8,128)S(1)}, f32[3,16,384]{2,1,0:T(8,128)S(1)}, u32[]{:S(2)}, u32[]{:S(2)}) collective-permute-start(f32[3,16,384]{2,1,0:T(8,128)S(1)} %get-tuple-element.16), channel_id=1, source_target_pairs={{0,16},{8,24},{16,0},{24,8},{1,17},{9,25},{17,1},{25,9},{2,18},{10... | collective-permute-start | bytes 221192 | tf_op jit(solution)/shard_map/ppermute | solution.py:628
  8.2 10.2 %collective-permute-start = (f32[4,8,384]{2,1,0:T(8,128)S(1)}, f32[4,8,384]{2,1,0:T(8,128)S(1)}, u32[]{:S(2)}, u32[]{:S(2)}) collective-permute-start(f32[4,8,384]{2,1,0:T(8,128)S(1)} %get-tuple-element.14), channel_id=1, source_target_pairs={{1,2},{3,4},{5,6},{2,1},{4,3},{6,5},{9,10},{11,12},{13,14},{10,9},... | collective-permute-start | bytes 147464 | tf_op jit(solution)/shard_map/ppermute | solution.py:628
  8.9 9.6 %collective-permute-start.1 = (f32[4,8,384]{2,1,0:T(8,128)S(1)}, f32[4,8,384]{2,1,0:T(8,128)S(1)}, u32[]{:S(2)}, u32[]{:S(2)}) collective-permute-start(f32[4,8,384]{2,1,0:T(8,128)S(1)} %get-tuple-element.15), channel_id=1, source_target_pairs={{0,1},{2,3},{4,5},{6,7},{1,0},{3,2},{5,4},{7,6},{8,9},{10,11},{12,... | collective-permute-start | bytes 147464 | tf_op jit(solution)/shard_map/ppermute | solution.py:628
  14.2 4.2 %collective-permute-start.5 = (f32[6,8,384]{2,1,0:T(8,128)S(1)}, f32[6,8,384]{2,1,0:T(8,128)S(1)}, u32[]{:S(2)}, u32[]{:S(2)}) collective-permute-start(f32[6,8,384]{2,1,0:T(8,128)S(1)} %get-tuple-element.17), channel_id=1, source_target_pairs={{1,2},{3,4},{5,6},{2,1},{4,3},{6,5},{9,10},{11,12},{13,14},{10,9},... | collective-permute-start | bytes 221192 | tf_op jit(solution)/shard_map/ppermute | solution.py:628
  14.9 3.8 %collective-permute-start.6 = (f32[6,8,384]{2,1,0:T(8,128)S(1)}, f32[6,8,384]{2,1,0:T(8,128)S(1)}, u32[]{:S(2)}, u32[]{:S(2)}) collective-permute-start(f32[6,8,384]{2,1,0:T(8,128)S(1)} %get-tuple-element.18), channel_id=1, source_target_pairs={{0,1},{2,3},{4,5},{6,7},{1,0},{3,2},{5,4},{7,6},{8,9},{10,11},{12,... | collective-permute-start | bytes 221192 | tf_op jit(solution)/shard_map/ppermute | solution.py:628
